TPU v7x, 128 devices: a whole 4x4x4 slice. The times are simulated.
128 devices in a mesh: blk: 32 (over x, z_lo, y), uly: 4 (over z_hi, core).
Axes of the slice: x: 4, y: 4, z: 4 (z_hi: 2, z_lo: 2; z = z_hi * 2 + z_lo), core: 2. Of those that a mesh axis runs over, the one named last changes fastest.
Arguments:
- queries: bfloat16 [10240, 2560], P(('blk', 'uly')), may hold values from -17 to 17
- keys: bfloat16 [10240, 2560], P(('blk', 'uly')), may hold values from -8 to 8
- values: bfloat16 [10240, 2560], P(('blk', 'uly')), may hold values from -2.5 to 2.5
Outputs:
- attended: bfloat16 [10240, 2560], P(('blk', 'uly'))
All inputs are finite; a program needn't handle non-finite values.
Results may differ from a plain program's by a relative error of at most 0.00665.
Values may be sent and summed in bfloat16 or wider, within the bound.
No kernel may reach another device: no remote copies, remote signals or barrier semaphores. Data moves between devices by JAX's collectives and lax.ppermute only.
A program may use at most 128 MiB of HBM per device.

v0:
```python
import functools

import jax
import jax.numpy as jnp
from jax import lax
from jax.experimental import pallas as pl
from jax.experimental.pallas import tpu as pltpu
from jax.sharding import Mesh, PartitionSpec as P

HEADS = 20
HEAD_DIM = 128
PAIR = 2 * HEAD_DIM
SCALE = HEAD_DIM**-0.5 * 1.4426950408889634
AXES = ("x", "zl", "y", "zh", "c")
SIZES = (4, 2, 4, 2, 2)
COLUMNS = 16
TOKENS = 80
QUARTER = TOKENS // 4
NT = (((1,), (1,)), ((), ()))
KV_ROWS, Q_ROWS, XKV_ROWS, XQ_ROWS = TOKENS, TOKENS // 2, QUARTER, QUARTER // 2
VMEM = pl.BlockSpec(memory_space=pltpu.VMEM)


def along_z(a, step):
    pairs = []
    for zl in range(2):
        for zh in range(2):
            z = (2 * zh + zl + step) % 4
            pairs.append((2 * zl + zh, 2 * (z % 2) + z // 2))
    return lax.ppermute(a, ("zl", "zh"), pairs)


def along_y(a, step):
    return lax.ppermute(a, "y", [(y, (y + step) % 4) for y in range(4)])


def other_core(a):
    return lax.ppermute(a, "c", [(0, 1), (1, 0)])


def scaled_halves(q):
    full = q.astype(jnp.float32) * SCALE
    high = full.astype(jnp.bfloat16)
    low = (full - high.astype(jnp.float32)).astype(jnp.bfloat16)
    return jnp.concatenate([high, low], axis=1)


def attend_kernel(k_block, n_kv, first, last, *refs):
    refs = list(refs)
    q_ref, kv_refs, refs = refs[0], refs[1 : 1 + n_kv], refs[1 + n_kv :]
    if not first:
        acc_in, top_in = refs[:2]
        refs = refs[2:]
    rows = q_ref.shape[0]
    ones = jnp.ones((k_block, HEAD_DIM), jnp.bfloat16)
    for half in range(2):
        lanes = slice(half * HEAD_DIM, (half + 1) * HEAD_DIM)
        here = slice(half * rows, (half + 1) * rows)
        q = scaled_halves(q_ref[:, lanes])
        if first:
            top = jnp.full((rows, 1), -1e30, jnp.float32)
            acc = jnp.zeros((rows, PAIR), jnp.float32)
        else:
            top = jnp.max(top_in[here, :], axis=1, keepdims=True)
            acc = acc_in[here, :]
        for kv_ref in kv_refs:
            for j in range(kv_ref.shape[0] // k_block):
                there = slice(j * k_block, (j + 1) * k_block)
                k = kv_ref[there, :HEAD_DIM]
                v = kv_ref[there, HEAD_DIM:]
                scores = lax.dot_general(
                    q, jnp.concatenate([k, k], axis=1), NT, preferred_element_type=jnp.float32
                )
                fresh = jnp.maximum(top, jnp.max(scores, axis=1, keepdims=True))
                weights = jnp.exp2(scores - fresh).astype(jnp.bfloat16)
                acc = acc * jnp.exp2(top - fresh) + jnp.dot(
                    weights, jnp.concatenate([v, ones], axis=1), preferred_element_type=jnp.float32
                )
                top = fresh
        if last == "out":
            refs[0][:, lanes] = (acc[:, :HEAD_DIM] / acc[:, HEAD_DIM:]).astype(jnp.bfloat16)
        elif last == "part":
            total = acc[:, HEAD_DIM:]
            refs[0][:, lanes] = (acc[:, :HEAD_DIM] / total).astype(jnp.bfloat16)
            level = top + jnp.log2(total)
            high = level.astype(jnp.bfloat16)
            rest = level - high.astype(jnp.float32)
            middle = rest.astype(jnp.bfloat16)
            low = (rest - middle.astype(jnp.float32)).astype(jnp.bfloat16)
            lane = lax.broadcasted_iota(jnp.int32, level.shape, 1)
            zero = jnp.zeros_like(level)
            coded = jnp.where(lane == 0, high.astype(jnp.float32), zero)
            coded = jnp.where(lane == 1, middle.astype(jnp.float32), coded)
            coded = jnp.where(lane == 2, low.astype(jnp.float32), coded)
            refs[0][:, PAIR + half * HEAD_DIM : PAIR + (half + 1) * HEAD_DIM] = coded.astype(jnp.bfloat16)
        else:
            refs[0][here, :] = acc
            refs[1][here, :] = jnp.broadcast_to(top, (rows, HEAD_DIM))


def attend(q, kvs, state, last, k_block=256):
    rows = q.shape[0]
    keys = sum(kv.shape[0] for kv in kvs)
    if last is None:
        out_shape = (
            jax.ShapeDtypeStruct((2 * rows, PAIR), jnp.float32),
            jax.ShapeDtypeStruct((2 * rows, HEAD_DIM), jnp.float32),
        )
    else:
        out_shape = (jax.ShapeDtypeStruct((rows, PAIR if last == "out" else 2 * PAIR), jnp.bfloat16),)
    args = (q, *kvs, *(state or ()))
    result = pl.pallas_call(
        functools.partial(attend_kernel, k_block, len(kvs), state is None, last),
        out_shape=out_shape,
        in_specs=[VMEM] * len(args),
        out_specs=(VMEM,) * len(out_shape),
        compiler_params=pltpu.CompilerParams(vmem_limit_bytes=40 * 2**20),
        cost_estimate=pl.CostEstimate(
            flops=16 * rows * keys * HEAD_DIM, bytes_accessed=4 * keys * HEAD_DIM, transcendentals=2 * rows * keys
        ),
    )(*args)
    return result if last is None else result[0]


def combine_kernel(*refs):
    parts, out = refs[:-1], refs[-1]
    for half in range(2):
        lanes = slice(half * HEAD_DIM, (half + 1) * HEAD_DIM)
        coded = slice(PAIR + half * HEAD_DIM, PAIR + (half + 1) * HEAD_DIM)
        levels = [jnp.sum(p[:, coded].astype(jnp.float32), axis=1, keepdims=True) for p in parts]
        top = functools.reduce(jnp.maximum, levels)
        shares = [jnp.exp2(level - top) for level in levels]
        total = functools.reduce(jnp.add, shares)
        summed = functools.reduce(
            jnp.add, [share * p[:, lanes].astype(jnp.float32) for share, p in zip(shares, parts, strict=True)]
        )
        out[:, lanes] = (summed / total).astype(jnp.bfloat16)


def combine(parts):
    rows = parts[0].shape[0]
    return pl.pallas_call(
        combine_kernel,
        out_shape=jax.ShapeDtypeStruct((rows, PAIR), jnp.bfloat16),
        in_specs=[VMEM] * len(parts),
        out_specs=VMEM,
        cost_estimate=pl.CostEstimate(flops=16 * rows * PAIR, bytes_accessed=16 * rows * PAIR, transcendentals=0),
    )(*parts)


def local(queries, keys, values):
    main = COLUMNS * HEAD_DIM
    extra_heads = HEADS - COLUMNS

    def by_column(a):
        return a[:, :main].reshape(TOKENS, COLUMNS, HEAD_DIM).transpose(1, 0, 2)

    def by_quarter(a):
        a = a[:, main:].reshape(4, QUARTER, extra_heads, HEAD_DIM).transpose(2, 0, 1, 3)
        return a.reshape(COLUMNS, QUARTER, HEAD_DIM)

    def paired(a):
        half = a.shape[1] // 2
        return jnp.concatenate([a[:, :half], a[:, half:]], axis=2)

    sent = jnp.concatenate(
        [
            jnp.concatenate([by_column(keys), by_column(values)], axis=2),
            paired(by_column(queries)),
            jnp.concatenate([by_quarter(keys), by_quarter(values)], axis=2),
            paired(by_quarter(queries)),
        ],
        axis=1,
    )
    got = lax.all_to_all(sent, ("x", "y"), 0, 0, tiled=True)

    def rows(start, count):
        return got[:, start : start + count].reshape(COLUMNS * count, PAIR)

    kv = rows(0, KV_ROWS)
    q = rows(KV_ROWS, Q_ROWS)
    xkv = rows(KV_ROWS + Q_ROWS, XKV_ROWS)
    xq = rows(KV_ROWS + Q_ROWS + XKV_ROWS, XQ_ROWS)

    xqs = [xq] + [along_z(xq, step) for step in (1, 3, 2)]
    xkvs = jnp.concatenate([xkv] + [along_y(xkv, step) for step in (1, 3, 2)], axis=0)
    kv_other = other_core(kv)
    kv_next, kv_before, kv_across = (along_z(kv, step) for step in (1, 3, 2))
    xkvs_other = other_core(xkvs)

    state = attend(q, [kv, kv_other], None, None)
    parts = attend(jnp.concatenate(xqs, axis=0), [xkvs, xkvs_other], None, "part")
    n = xq.shape[0]
    back = [parts[:n]] + [
        along_z(parts[i * n : (i + 1) * n], -step) for i, step in ((1, 1), (2, 3), (3, 2))
    ]
    xout = combine(back)
    state = attend(q, [kv_next, kv_before], state, None)
    state = attend(q, [other_core(kv_next), other_core(kv_before)], state, None)
    out = attend(q, [kv_across, other_core(kv_across)], state, "out")

    sent = jnp.concatenate(
        [out.reshape(COLUMNS, Q_ROWS, PAIR), xout.reshape(COLUMNS, XQ_ROWS, PAIR)], axis=1
    )
    got = lax.all_to_all(sent, ("x", "y"), 0, 0, tiled=True)
    out = got[:, :Q_ROWS].reshape(COLUMNS, Q_ROWS, 2, HEAD_DIM).transpose(2, 1, 0, 3).reshape(TOKENS, main)
    xout = got[:, Q_ROWS:].reshape(extra_heads, 4, XQ_ROWS, 2, HEAD_DIM).transpose(1, 3, 2, 0, 4)
    return jnp.concatenate([out, xout.reshape(TOKENS, extra_heads * HEAD_DIM)], axis=1)


def solution(mesh):
    fine = Mesh(mesh.devices.reshape(SIZES), AXES)
    return jax.shard_map(
        local, mesh=fine, in_specs=(P(AXES, None),) * 3, out_specs=P(AXES, None), check_vma=False
    )
```

profile of v0, /device:TPU:0, one launch (start us, length us, event | category | flops | bytes accessed | tf_op | source)
XLA Modules:
  0.0 129.7 jit_solution(10300549922141923239)
XLA Ops:
  0.0 1.0 bitcast_bitcast_fusion
  1.0 0.0 slice-start.2
  1.0 0.0 slice-start
  1.1 0.0 slice-start.1
  1.1 1.2 bitcast_bitcast_fusion.1
  2.6 0.2 maximum_maximum_fusion
  2.8 26.0 %all_to_all.10 = bf16[16,150,256]{2,1,0:T(8,128)(2,1)S(1)} all-to-all(bf16[16,150,256]{2,1,0:T(8,128)(2,1)S(1)} %maximum_maximum_fusion), channel_id=1, replica_groups=mesh['x'=4,'zl'=2,'y'=4,'zh'=2,'c'=2] {'x','y'}, dimensions={0} | all-to-all | bytes 2457600 | tf_op jit(solution)/shard_map/all_to_all | solution.py:175
  28.8 0.5 collective-permute-start.10
  29.4 2.0 %collective-permute-start.2 = (bf16[1280,256]{1,0:T(8,128)(2,1)S(1)}, bf16[1280,256]{1,0:T(8,128)(2,1)S(1)}, u32[]{:S(2)}, u32[]{:S(2)}) collective-permute-start(bf16[1280,256]{1,0:T(8,128)(2,1)S(1)} %bitcast.43), channel_id=1, source_target_pairs={{0,16},{2,18},{16,2},{18,0},{1,17},{3,19},{17,3},{19,1},{4,20},{6,... | collective-permute-start | bytes 1966088 | tf_op jit(solution)/shard_map/ppermute | solution.py:30
  31.4 2.2 %collective-permute-start.4 = (bf16[1280,256]{1,0:T(8,128)(2,1)S(1)}, bf16[1280,256]{1,0:T(8,128)(2,1)}, u32[]{:S(2)}, u32[]{:S(2)}) collective-permute-start(bf16[1280,256]{1,0:T(8,128)(2,1)S(1)} %bitcast.44), channel_id=1, source_target_pairs={{0,18},{2,16},{16,0},{18,2},{1,19},{3,17},{17,1},{19,3},{4,22},{6,... | collective-permute-start | bytes 1966088 | tf_op jit(solution)/shard_map/ppermute | solution.py:30
  33.6 1.8 %collective-permute-start = (bf16[1280,256]{1,0:T(8,128)(2,1)S(1)}, bf16[1280,256]{1,0:T(8,128)(2,1)S(1)}, u32[]{:S(2)}, u32[]{:S(2)}) collective-permute-start(bf16[1280,256]{1,0:T(8,128)(2,1)S(1)} %bitcast.45), channel_id=1, source_target_pairs={{0,2},{2,0},{16,18},{18,16},{1,3},{3,1},{17,19},{19,17},{4,6},{6,4... | collective-permute-start | bytes 1966088 | tf_op jit(solution)/shard_map/ppermute | solution.py:30
  35.4 2.8 %collective-permute-start.11 = (bf16[320,256]{1,0:T(8,128)(2,1)S(1)}, bf16[320,256]{1,0:T(8,128)(2,1)S(1)}, u32[]{:S(2)}, u32[]{:S(2)}) collective-permute-start(bf16[320,256]{1,0:T(8,128)(2,1)S(1)} %reshape.70), channel_id=1, source_target_pairs={{0,12},{4,0},{8,4},{12,8},{1,13},{5,1},{9,5},{13,9},{2,14},{6,2},{... | collective-permute-start | bytes 491528 | tf_op jit(solution)/shard_map/ppermute | solution.py:34
  38.2 0.5 collective-permute-start.12
  38.6 4.1 %collective-permute-done.11 = bf16[320,256]{1,0:T(8,128)(2,1)S(1)} collective-permute-done((bf16[320,256]{1,0:T(8,128)(2,1)S(1)}, bf16[320,256]{1,0:T(8,128)(2,1)S(1)}, u32[]{:S(2)}, u32[]{:S(2)}) %collective-permute-start.11) | collective-permute-done | bytes 163872 | tf_op jit(solution)/shard_map/ppermute | solution.py:34
  42.8 2.3 %collective-permute-done.12 = bf16[320,256]{1,0:T(8,128)(2,1)S(1)} collective-permute-done((bf16[320,256]{1,0:T(8,128)(2,1)S(1)}, bf16[320,256]{1,0:T(8,128)(2,1)S(1)}, u32[]{:S(2)}, u32[]{:S(2)}) %collective-permute-start.12) | collective-permute-done | bytes 163872 | tf_op jit(solution)/shard_map/ppermute | solution.py:34
  45.1 0.1 collective-permute-start.13
  45.2 0.9 slice.86
  46.2 1.1 collective-permute-start.7
  47.2 16.0 %collective-permute-done.7 = bf16[160,256]{1,0:T(8,128)(2,1)S(1)} collective-permute-done((bf16[160,256]{1,0:T(8,128)(2,1)S(1)}, bf16[160,256]{1,0:T(8,128)(2,1)S(1)}, u32[]{:S(2)}, u32[]{:S(2)}) %collective-permute-start.7) | collective-permute-done | bytes 81952 | tf_op jit(solution)/shard_map/ppermute | solution.py:30
  63.3 0.6 collective-permute-start.8
  63.9 3.8 %collective-permute-done.8 = bf16[160,256]{1,0:T(8,128)(2,1)S(1)} collective-permute-done((bf16[160,256]{1,0:T(8,128)(2,1)S(1)}, bf16[160,256]{1,0:T(8,128)(2,1)S(1)}, u32[]{:S(2)}, u32[]{:S(2)}) %collective-permute-start.8) | collective-permute-done | bytes 81952 | tf_op jit(solution)/shard_map/ppermute | solution.py:30
  67.7 0.4 collective-permute-start.9
  68.1 1.0 slice.84
  69.1 4.5 %collective-permute-done.9 = bf16[160,256]{1,0:T(8,128)(2,1)S(1)} collective-permute-done((bf16[160,256]{1,0:T(8,128)(2,1)S(1)}, bf16[160,256]{1,0:T(8,128)(2,1)S(1)}, u32[]{:S(2)}, u32[]{:S(2)}) %collective-permute-start.9) | collective-permute-done | bytes 81952 | tf_op jit(solution)/shard_map/ppermute | solution.py:30
  73.7 0.6 collective-permute-start.3
  74.3 0.1 collective-permute-start.5
  74.4 0.4 collective-permute-start.1
  74.8 5.5 %shard_map.41 = bf16[640,512]{1,0:T(8,128)(2,1)S(1)} custom-call(bf16[640,256]{1,0:T(8,128)(2,1)S(1)} %pad_maximum_fusion.2.refs_0_, bf16[1280,256]{1,0:T(8,128)(2,1)S(1)} %constant_dynamic-update-slice_fusion.refs_1_, bf16[1280,256]{1,0:T(8,128)(2,1)} %collective-permute-done.13.refs_2_), custom_call_target="tpu_custom_call" | custom-call | flops 3355443200 | bytes 1310720 | tf_op jit(solution)/shard_map/pallas_call | solution.py:112
  80.3 0.7 fusion
  81.0 1.9 %collective-permute-start.14 = (bf16[160,512]{1,0:T(8,128)(2,1)S(1)}, bf16[160,512]{1,0:T(8,128)(2,1)S(1)}, u32[]{:S(2)}, u32[]{:S(2)}) collective-permute-start(bf16[160,512]{1,0:T(8,128)(2,1)S(1)} %get-tuple-element.19), channel_id=1, source_target_pairs={{0,18},{2,16},{16,0},{18,2},{1,19},{3,17},{17,1},{19,3},{4,22},{6,... | collective-permute-start | bytes 491528 | tf_op jit(solution)/shard_map/ppermute | solution.py:30
  82.9 4.1 %shard_map.37 = (f32[1280,256]{1,0:T(8,128)S(1)}, f32[1280,128]{1,0:T(8,128)S(1)}) custom-call(bf16[640,256]{1,0:T(8,128)(2,1)S(1)} %bitcast.49, bf16[1280,256]{1,0:T(8,128)(2,1)S(1)} %bitcast.47, bf16[1280,256]{1,0:T(8,128)(2,1)S(1)} %collective-permute-done.6.refs_2_), custom_call_target="tpu_custom_call" | custom-call | flops 3355443200 | bytes 1310720 | tf_op jit(solution)/shard_map/pallas_call | solution.py:112
  87.0 0.2 collective-permute-start.15
  87.3 1.5 %collective-permute-start.16 = (bf16[160,512]{1,0:T(8,128)(2,1)S(1)}, bf16[160,512]{1,0:T(8,128)(2,1)S(1)}, u32[]{:S(2)}, u32[]{:S(2)}) collective-permute-start(bf16[160,512]{1,0:T(8,128)(2,1)S(1)} %get-tuple-element.17), channel_id=1, source_target_pairs={{0,2},{2,0},{16,18},{18,16},{1,3},{3,1},{17,19},{19,17},{4,6},{6,4... | collective-permute-start | bytes 491528 | tf_op jit(solution)/shard_map/ppermute | solution.py:30
  88.8 5.2 %shard_map.38 = (f32[1280,256]{1,0:T(8,128)S(1)}, f32[1280,128]{1,0:T(8,128)S(1)}) custom-call(bf16[640,256]{1,0:T(8,128)(2,1)S(1)} %bitcast.50, bf16[1280,256]{1,0:T(8,128)(2,1)S(1)} %collective-permute-done.2.refs_1_, bf16[1280,256]{1,0:T(8,128)(2,1)} %collective-permute-done.4.refs_2_, f32[1280,256]{1,0:T(8,128)S(1)} %get-tuple-element.11.refs_3_, ...), custom_call_target="tpu_custom_call" | custom-call | flops 3355443200 | bytes 1310720 | tf_op jit(solution)/shard_map/pallas_call | solution.py:112
  94.1 1.1 copy-done
  95.1 2.6 %collective-permute-done.15.refs_2_ = bf16[160,512]{1,0:T(8,128)(2,1)S(1)} collective-permute-done((bf16[160,512]{1,0:T(8,128)(2,1)S(1)}, bf16[160,512]{1,0:T(8,128)(2,1)S(1)}, u32[]{:S(2)}, u32[]{:S(2)}) %collective-permute-start.15) | collective-permute-done | bytes 163872 | tf_op jit(solution)/shard_map/ppermute | solution.py:30
  97.7 0.7 copy-done.4
  98.4 0.1 copy-done.5
  98.5 2.1 %shard_map.42 = bf16[160,256]{1,0:T(8,128)(2,1)} custom-call(bf16[160,512]{1,0:T(8,128)(2,1)} %get-tuple-element.20.refs_0_, bf16[160,512]{1,0:T(8,128)(2,1)} %copy-done.3, bf16[160,512]{1,0:T(8,128)(2,1)} %copy-done.4, bf16[160,512]{1,0:T(8,128)(2,1)} %copy-done.5), custom_call_target="tpu_custom_call" | custom-call | flops 655360 | bytes 655360 | tf_op jit(solution)/shard_map/pallas_call | solution.py:142
  100.6 0.9 reshape.71
  101.5 1.3 %copy-done.1 = f32[1280,256]{1,0:T(8,128)S(1)} copy-done((f32[1280,256]{1,0:T(8,128)S(1)}, f32[1280,256]{1,0:T(8,128)}, u32[]{:S(2)}) %copy-start.1) | copy-done | bytes 1310744
  102.8 5.4 %shard_map.39 = (f32[1280,256]{1,0:T(8,128)S(1)}, f32[1280,128]{1,0:T(8,128)S(1)}) custom-call(bf16[640,256]{1,0:T(8,128)(2,1)S(1)} %bitcast.51, bf16[1280,256]{1,0:T(8,128)(2,1)} %collective-permute-done.3.refs_1_, bf16[1280,256]{1,0:T(8,128)(2,1)} %collective-permute-done.5.refs_2_, f32[1280,256]{1,0:T(8,128)S(1)} %copy-done.1, ...), custom_call_target="tpu_custom_call" | custom-call | flops 3355443200 | bytes 1310720 | tf_op jit(solution)/shard_map/pallas_call | solution.py:112
  108.3 5.2 %shard_map.40 = bf16[640,256]{1,0:T(8,128)(2,1)S(1)} custom-call(bf16[640,256]{1,0:T(8,128)(2,1)S(1)} %bitcast.52, bf16[1280,256]{1,0:T(8,128)(2,1)S(1)} %collective-permute-done.refs_1_, bf16[1280,256]{1,0:T(8,128)(2,1)} %collective-permute-done.1.refs_2_, f32[1280,256]{1,0:T(8,128)S(1)} %get-tuple-element.15.refs_3_, f32[1280,128]{1,0:T(8,128)S(1)} %get-tuple-element.16.refs_4_), custom_call_target="tpu_custom_call" | custom-call | flops 3355443200 | bytes 1310720 | tf_op jit(solution)/shard_map/pallas_call | solution.py:112
  113.6 14.9 %all_to_all.11 = bf16[16,50,256]{2,1,0:T(8,128)(2,1)S(1)} all-to-all(bf16[16,50,256]{2,1,0:T(8,128)(2,1)S(1)} %pad_maximum_fusion), channel_id=1, replica_groups=mesh['x'=4,'zl'=2,'y'=4,'zh'=2,'c'=2] {'x','y'}, dimensions={0} | all-to-all | bytes 819200 | tf_op jit(solution)/shard_map/all_to_all | solution.py:205
  128.5 0.1 reshape.72
  128.6 0.1 copy.37
  128.7 0.1 copy.52
  128.9 0.8 pad_maximum_fusion.1
  (46 shorter events, 0.6 us)
Async XLA Ops:
  1.0 1.3 %slice-start.2 = ((bf16[80,2560]{1,0:T(8,128)(2,1)}), bf16[80,512]{1,0:T(8,128)(2,1)S(1)}, s32[]{:S(2)}) async-start(bf16[80,2560]{1,0:T(8,128)(2,1)} %param.3), calls=%async_computation.4 | async-start | bytes 163840 | tf_op jit(solution)/shard_map/slice | solution.py:159
  1.0 1.4 %slice-start = ((bf16[80,2560]{1,0:T(8,128)(2,1)}), bf16[80,512]{1,0:T(8,128)(2,1)S(1)}, s32[]{:S(2)}) async-start(bf16[80,2560]{1,0:T(8,128)(2,1)} %param.4), calls=%async_computation.2 | async-start | bytes 163840 | tf_op jit(solution)/shard_map/slice | solution.py:159
  1.1 1.5 %slice-start.1 = ((bf16[80,2560]{1,0:T(8,128)(2,1)}), bf16[80,512]{1,0:T(8,128)(2,1)S(1)}, s32[]{:S(2)}) async-start(bf16[80,2560]{1,0:T(8,128)(2,1)} %param.5), calls=%async_computation.3 | async-start | bytes 163840 | tf_op jit(solution)/shard_map/slice | solution.py:159
  28.7 6.6 %copy-start.2 = (bf16[16,150,256]{2,1,0:T(8,128)(2,1)}, bf16[16,150,256]{2,1,0:T(8,128)(2,1)S(1)}, u32[]{:S(2)}) copy-start(bf16[16,150,256]{2,1,0:T(8,128)(2,1)S(1)} %all_to_all.10) | copy-start | bytes 3686404
  28.8 9.3 %collective-permute-start.10 = (bf16[320,256]{1,0:T(8,128)(2,1)S(1)}, bf16[320,256]{1,0:T(8,128)(2,1)S(1)}, u32[]{:S(2)}, u32[]{:S(2)}) collective-permute-start(bf16[320,256]{1,0:T(8,128)(2,1)S(1)} %reshape.70), channel_id=1, source_target_pairs={{0,4},{4,8},{8,12},{12,0},{1,5},{5,9},{9,13},{13,1},{2,6},{6,10},{... | collective-permute-start | bytes 491528 | tf_op jit(solution)/shard_map/ppermute | solution.py:34
  29.4 44.3 %collective-permute-start.2 = (bf16[1280,256]{1,0:T(8,128)(2,1)S(1)}, bf16[1280,256]{1,0:T(8,128)(2,1)S(1)}, u32[]{:S(2)}, u32[]{:S(2)}) collective-permute-start(bf16[1280,256]{1,0:T(8,128)(2,1)S(1)} %bitcast.43), channel_id=1, source_target_pairs={{0,16},{2,18},{16,2},{18,0},{1,17},{3,19},{17,3},{19,1},{4,20},{6,... | collective-permute-start | bytes 1966088 | tf_op jit(solution)/shard_map/ppermute | solution.py:30
  31.4 42.9 %collective-permute-start.4 = (bf16[1280,256]{1,0:T(8,128)(2,1)S(1)}, bf16[1280,256]{1,0:T(8,128)(2,1)}, u32[]{:S(2)}, u32[]{:S(2)}) collective-permute-start(bf16[1280,256]{1,0:T(8,128)(2,1)S(1)} %bitcast.44), channel_id=1, source_target_pairs={{0,18},{2,16},{16,0},{18,2},{1,19},{3,17},{17,1},{19,3},{4,22},{6,... | collective-permute-start | bytes 1966088 | tf_op jit(solution)/shard_map/ppermute | solution.py:30
  33.6 40.8 %collective-permute-start = (bf16[1280,256]{1,0:T(8,128)(2,1)S(1)}, bf16[1280,256]{1,0:T(8,128)(2,1)S(1)}, u32[]{:S(2)}, u32[]{:S(2)}) collective-permute-start(bf16[1280,256]{1,0:T(8,128)(2,1)S(1)} %bitcast.45), channel_id=1, source_target_pairs={{0,2},{2,0},{16,18},{18,16},{1,3},{3,1},{17,19},{19,17},{4,6},{6,4... | collective-permute-start | bytes 1966088 | tf_op jit(solution)/shard_map/ppermute | solution.py:30
  35.4 7.4 %collective-permute-start.11 = (bf16[320,256]{1,0:T(8,128)(2,1)S(1)}, bf16[320,256]{1,0:T(8,128)(2,1)S(1)}, u32[]{:S(2)}, u32[]{:S(2)}) collective-permute-start(bf16[320,256]{1,0:T(8,128)(2,1)S(1)} %reshape.70), channel_id=1, source_target_pairs={{0,12},{4,0},{8,4},{12,8},{1,13},{5,1},{9,5},{13,9},{2,14},{6,2},{... | collective-permute-start | bytes 491528 | tf_op jit(solution)/shard_map/ppermute | solution.py:34
  38.2 6.9 %collective-permute-start.12 = (bf16[320,256]{1,0:T(8,128)(2,1)S(1)}, bf16[320,256]{1,0:T(8,128)(2,1)S(1)}, u32[]{:S(2)}, u32[]{:S(2)}) collective-permute-start(bf16[320,256]{1,0:T(8,128)(2,1)S(1)} %reshape.70), channel_id=1, source_target_pairs={{0,8},{4,12},{8,0},{12,4},{1,9},{5,13},{9,1},{13,5},{2,10},{6,14},... | collective-permute-start | bytes 491528 | tf_op jit(solution)/shard_map/ppermute | solution.py:34
  45.1 29.7 %collective-permute-start.13 = (bf16[1280,256]{1,0:T(8,128)(2,1)S(1)}, bf16[1280,256]{1,0:T(8,128)(2,1)}, u32[]{:S(2)}, u32[]{:S(2)}) collective-permute-start(bf16[1280,256]{1,0:T(8,128)(2,1)S(1)} %constant_dynamic-update-slice_fusion.refs_1_), channel_id=1, source_target_pairs={{0,1},{1,0},{2,3},{3,2},{4,5},{5,4},{6,7},{7,6},{8,9},{9,8},{10,11... | collective-permute-start | bytes 1966088 | tf_op jit(solution)/shard_map/ppermute | solution.py:38
  46.2 17.1 %collective-permute-start.7 = (bf16[160,256]{1,0:T(8,128)(2,1)S(1)}, bf16[160,256]{1,0:T(8,128)(2,1)S(1)}, u32[]{:S(2)}, u32[]{:S(2)}) collective-permute-start(bf16[160,256]{1,0:T(8,128)(2,1)S(1)} %reshape.69), channel_id=1, source_target_pairs={{0,16},{2,18},{16,2},{18,0},{1,17},{3,19},{17,3},{19,1},{4,20},{6,... | collective-permute-start | bytes 245768 | tf_op jit(solution)/shard_map/ppermute | solution.py:30
  63.3 4.4 %collective-permute-start.8 = (bf16[160,256]{1,0:T(8,128)(2,1)S(1)}, bf16[160,256]{1,0:T(8,128)(2,1)S(1)}, u32[]{:S(2)}, u32[]{:S(2)}) collective-permute-start(bf16[160,256]{1,0:T(8,128)(2,1)S(1)} %reshape.69), channel_id=1, source_target_pairs={{0,18},{2,16},{16,0},{18,2},{1,19},{3,17},{17,1},{19,3},{4,22},{6,... | collective-permute-start | bytes 245768 | tf_op jit(solution)/shard_map/ppermute | solution.py:30
  67.7 5.9 %collective-permute-start.9 = (bf16[160,256]{1,0:T(8,128)(2,1)S(1)}, bf16[160,256]{1,0:T(8,128)(2,1)S(1)}, u32[]{:S(2)}, u32[]{:S(2)}) collective-permute-start(bf16[160,256]{1,0:T(8,128)(2,1)S(1)} %reshape.69), channel_id=1, source_target_pairs={{0,2},{2,0},{16,18},{18,16},{1,3},{3,1},{17,19},{19,17},{4,6},{6,4... | collective-permute-start | bytes 245768 | tf_op jit(solution)/shard_map/ppermute | solution.py:30
  73.6 9.2 %collective-permute-start.6 = (bf16[1280,256]{1,0:T(8,128)(2,1)S(1)}, bf16[1280,256]{1,0:T(8,128)(2,1)S(1)}, u32[]{:S(2)}, u32[]{:S(2)}) collective-permute-start(bf16[1280,256]{1,0:T(8,128)(2,1)S(1)} %bitcast.46), channel_id=1, source_target_pairs={{0,1},{1,0},{2,3},{3,2},{4,5},{5,4},{6,7},{7,6},{8,9},{9,8},{10,11... | collective-permute-start | bytes 1966088 | tf_op jit(solution)/shard_map/ppermute | solution.py:38
  73.7 27.8 %collective-permute-start.3 = (bf16[1280,256]{1,0:T(8,128)(2,1)S(1)}, bf16[1280,256]{1,0:T(8,128)(2,1)}, u32[]{:S(2)}, u32[]{:S(2)}) collective-permute-start(bf16[1280,256]{1,0:T(8,128)(2,1)S(1)} %collective-permute-done.2.refs_1_), channel_id=1, source_target_pairs={{0,1},{1,0},{2,3},{3,2},{4,5},{5,4},{6,7},{7,6},{8,9},{9,8},{10,11... | collective-permute-start | bytes 1966088 | tf_op jit(solution)/shard_map/ppermute | solution.py:38
  74.3 27.2 %collective-permute-start.5 = (bf16[1280,256]{1,0:T(8,128)(2,1)}, bf16[1280,256]{1,0:T(8,128)(2,1)}, u32[]{:S(2)}, u32[]{:S(2)}) collective-permute-start(bf16[1280,256]{1,0:T(8,128)(2,1)} %collective-permute-done.4.refs_2_), channel_id=1, source_target_pairs={{0,1},{1,0},{2,3},{3,2},{4,5},{5,4},{6,7},{7,6},{8,9},{9,8},{10,11... | collective-permute-start | bytes 1966088 | tf_op jit(solution)/shard_map/ppermute | solution.py:38
  74.4 33.9 %collective-permute-start.1 = (bf16[1280,256]{1,0:T(8,128)(2,1)S(1)}, bf16[1280,256]{1,0:T(8,128)(2,1)}, u32[]{:S(2)}, u32[]{:S(2)}) collective-permute-start(bf16[1280,256]{1,0:T(8,128)(2,1)S(1)} %collective-permute-done.refs_1_), channel_id=1, source_target_pairs={{0,1},{1,0},{2,3},{3,2},{4,5},{5,4},{6,7},{7,6},{8,9},{9,8},{10,11... | collective-permute-start | bytes 1966088 | tf_op jit(solution)/shard_map/ppermute | solution.py:38
  81.0 6.3 %collective-permute-start.14 = (bf16[160,512]{1,0:T(8,128)(2,1)S(1)}, bf16[160,512]{1,0:T(8,128)(2,1)S(1)}, u32[]{:S(2)}, u32[]{:S(2)}) collective-permute-start(bf16[160,512]{1,0:T(8,128)(2,1)S(1)} %get-tuple-element.19), channel_id=1, source_target_pairs={{0,18},{2,16},{16,0},{18,2},{1,19},{3,17},{17,1},{19,3},{4,22},{6,... | collective-permute-start | bytes 491528 | tf_op jit(solution)/shard_map/ppermute | solution.py:30
  87.0 10.7 %collective-permute-start.15 = (bf16[160,512]{1,0:T(8,128)(2,1)S(1)}, bf16[160,512]{1,0:T(8,128)(2,1)S(1)}, u32[]{:S(2)}, u32[]{:S(2)}) collective-permute-start(bf16[160,512]{1,0:T(8,128)(2,1)S(1)} %get-tuple-element.18), channel_id=1, source_target_pairs={{0,16},{2,18},{16,2},{18,0},{1,17},{3,19},{17,3},{19,1},{4,20},{6,... | collective-permute-start | bytes 491528 | tf_op jit(solution)/shard_map/ppermute | solution.py:30
  87.3 6.8 %copy-start.3 = (bf16[160,512]{1,0:T(8,128)(2,1)}, bf16[160,512]{1,0:T(8,128)(2,1)S(1)}, u32[]{:S(2)}) copy-start(bf16[160,512]{1,0:T(8,128)(2,1)S(1)} %collective-permute-done.14.refs_1_) | copy-start | bytes 491524
  87.3 10.5 %collective-permute-start.16 = (bf16[160,512]{1,0:T(8,128)(2,1)S(1)}, bf16[160,512]{1,0:T(8,128)(2,1)S(1)}, u32[]{:S(2)}, u32[]{:S(2)}) collective-permute-start(bf16[160,512]{1,0:T(8,128)(2,1)S(1)} %get-tuple-element.17), channel_id=1, source_target_pairs={{0,2},{2,0},{16,18},{18,16},{1,3},{3,1},{17,19},{19,17},{4,6},{6,4... | collective-permute-start | bytes 491528 | tf_op jit(solution)/shard_map/ppermute | solution.py:30
  94.0 1.1 copy-start
  97.7 0.7 copy-start.4
  97.7 0.7 copy-start.5
  101.5 1.3 %copy-start.1 = (f32[1280,256]{1,0:T(8,128)S(1)}, f32[1280,256]{1,0:T(8,128)}, u32[]{:S(2)}) copy-start(f32[1280,256]{1,0:T(8,128)} %copy-done) | copy-start | bytes 3932164
where the time goes:
time: 130 us
  blocking collectives  40.9 us (31%)
  waiting for transfers between devices  33.4 us (26%)
  Pallas kernels  27.7 us (21%)
  starting transfers between devices  16.7 us (13%)
  local copies, waits for them, and re-layouts  9.71 us (7%)
    all_to_all x2, blocking collectives, local(): got = lax.all_to_all(sent, ('x', 'y'), 0, 0, tiled=True)  40.9 us
    ppermute x9, waiting for transfers between devices, along_z(): return lax.ppermute(a, ('zl', 'zh'), pairs)  26.9 us
    pallas_call x5, Pallas kernels, attend(): pl.pallas_call(functools.partial(attend_kernel, k_block, len(kvs), state...  25.6 us
    ppermute x9, starting transfers between devices, along_z(): return lax.ppermute(a, ('zl', 'zh'), pairs)  11.8 us
    ppermute x3, waiting for transfers between devices, along_y(): return lax.ppermute(a, 'y', [(y, (y + step) % 4) for y in range(4)])  6.42 us
    ppermute x3, starting transfers between devices, along_y(): return lax.ppermute(a, 'y', [(y, (y + step) % 4) for y in range(4)])  3.76 us
    unnamed x17, local copies, waits for them, and re-layouts  3.24 us
  transfers between devices with their start and end apart: 17, of which 6 were waited for; matrix products, arithmetic and copies ran while one was open for 3% of the time, Pallas kernels for 17%

commit v1 on v0

v1 whole, which is shorter than its diff:
```python
import functools

import jax
import jax.numpy as jnp
from jax import lax
from jax.experimental import pallas as pl
from jax.experimental.pallas import tpu as pltpu
from jax.sharding import Mesh, PartitionSpec as P

HEADS = 20
HEAD_DIM = 128
PAIR = 2 * HEAD_DIM
SCALE = HEAD_DIM**-0.5 * 1.4426950408889634
AXES = ("x", "zl", "y", "zh", "c")
SIZES = (4, 2, 4, 2, 2)
COLUMNS = 16
TOKENS = 80
EXTRA = HEADS - COLUMNS
K_BLOCK = 256
STEPS = (1, 3, 2)
NT = (((1,), (1,)), ((), ()))
KV_ROWS, Q_ROWS = TOKENS, TOKENS // 2
VMEM = pl.BlockSpec(memory_space=pltpu.VMEM)
HBM = pl.BlockSpec(memory_space=pltpu.HBM)


def along_z(a, step):
    pairs = []
    for zl in range(2):
        for zh in range(2):
            z = (2 * zh + zl + step) % 4
            pairs.append((2 * zl + zh, 2 * (z % 2) + z // 2))
    return lax.ppermute(a, ("zl", "zh"), pairs)


def along(axis, a, step):
    return lax.ppermute(a, axis, [(i, (i + step) % 4) for i in range(4)])


def other_core(a):
    return lax.ppermute(a, "c", [(0, 1), (1, 0)])


def scaled_halves(q):
    full = q.astype(jnp.float32) * SCALE
    high = full.astype(jnp.bfloat16)
    low = (full - high.astype(jnp.float32)).astype(jnp.bfloat16)
    return jnp.concatenate([high, low], axis=1)


def attend_kernel(n_kv, n_after, first, last, *refs):
    refs = list(refs)
    q_ref, kv_refs, refs = refs[0], refs[1 : 1 + n_kv], refs[1 + n_kv :]
    if not first:
        acc_in, top_in = refs[:2]
        refs = refs[2:]
    refs = refs[n_after:]
    rows = q_ref.shape[0]
    ones = jnp.ones((K_BLOCK, HEAD_DIM), jnp.bfloat16)
    for half in range(2):
        lanes = slice(half * HEAD_DIM, (half + 1) * HEAD_DIM)
        here = slice(half * rows, (half + 1) * rows)
        q = scaled_halves(q_ref[:, lanes])
        if first:
            top = jnp.full((rows, 1), -1e30, jnp.float32)
            acc = jnp.zeros((rows, PAIR), jnp.float32)
        else:
            top = jnp.max(top_in[here, :], axis=1, keepdims=True)
            acc = acc_in[here, :]
        for kv_ref in kv_refs:
            for j in range(kv_ref.shape[0] // K_BLOCK):
                there = slice(j * K_BLOCK, (j + 1) * K_BLOCK)
                k = kv_ref[there, :HEAD_DIM]
                v = kv_ref[there, HEAD_DIM:]
                scores = lax.dot_general(
                    q, jnp.concatenate([k, k], axis=1), NT, preferred_element_type=jnp.float32
                )
                fresh = jnp.maximum(top, jnp.max(scores, axis=1, keepdims=True))
                weights = jnp.exp2(scores - fresh).astype(jnp.bfloat16)
                acc = acc * jnp.exp2(top - fresh) + jnp.dot(
                    weights, jnp.concatenate([v, ones], axis=1), preferred_element_type=jnp.float32
                )
                top = fresh
        if last == "out":
            refs[0][:, lanes] = (acc[:, :HEAD_DIM] / acc[:, HEAD_DIM:]).astype(jnp.bfloat16)
        elif last == "part":
            total = acc[:, HEAD_DIM:]
            part = (acc[:, :HEAD_DIM] / total).astype(jnp.bfloat16)
            level = top + jnp.log2(total)
            high = level.astype(jnp.bfloat16)
            rest = level - high.astype(jnp.float32)
            middle = rest.astype(jnp.bfloat16)
            low = (rest - middle.astype(jnp.float32)).astype(jnp.bfloat16)
            lane = lax.broadcasted_iota(jnp.int32, level.shape, 1)
            zero = jnp.zeros_like(level)
            coded = jnp.where(lane == 0, high.astype(jnp.float32), zero)
            coded = jnp.where(lane == 1, middle.astype(jnp.float32), coded)
            coded = jnp.where(lane == 2, low.astype(jnp.float32), coded)
            coded = coded.astype(jnp.bfloat16)
            for i, ref in enumerate(refs):
                some = slice(i * ref.shape[0], (i + 1) * ref.shape[0])
                ref[:, lanes] = part[some, :]
                ref[:, PAIR + half * HEAD_DIM : PAIR + (half + 1) * HEAD_DIM] = coded[some, :]
        else:
            refs[0][here, :] = acc
            refs[1][here, :] = jnp.broadcast_to(top, (rows, HEAD_DIM))


def attend(q, kvs, state, last, after=()):
    rows = q.shape[0]
    keys = sum(kv.shape[0] for kv in kvs)
    if last is None:
        out_shape = (
            jax.ShapeDtypeStruct((2 * rows, PAIR), jnp.float32),
            jax.ShapeDtypeStruct((2 * rows, HEAD_DIM), jnp.float32),
        )
    elif last == "part":
        out_shape = (jax.ShapeDtypeStruct((rows // 4, 2 * PAIR), jnp.bfloat16),) * 4
    else:
        out_shape = (jax.ShapeDtypeStruct((rows, PAIR), jnp.bfloat16),)
    args = (q, *kvs, *(state or ()))
    result = pl.pallas_call(
        functools.partial(attend_kernel, len(kvs), len(after), state is None, last),
        out_shape=out_shape,
        in_specs=[VMEM] * len(args) + [HBM] * len(after),
        out_specs=(VMEM,) * len(out_shape),
        compiler_params=pltpu.CompilerParams(vmem_limit_bytes=20 * 2**20),
        cost_estimate=pl.CostEstimate(
            flops=rows * keys * HEAD_DIM, bytes_accessed=4 * keys * HEAD_DIM, transcendentals=0
        ),
    )(*args, *after)
    return result[0] if last == "out" else result


def combine_kernel(*refs):
    parts, outs = refs[:4], refs[4:]
    for half in range(2):
        lanes = slice(half * HEAD_DIM, (half + 1) * HEAD_DIM)
        coded = slice(PAIR + half * HEAD_DIM, PAIR + (half + 1) * HEAD_DIM)
        levels = [jnp.sum(p[:, coded].astype(jnp.float32), axis=1, keepdims=True) for p in parts]
        top = functools.reduce(jnp.maximum, levels)
        shares = [jnp.exp2(level - top) for level in levels]
        total = functools.reduce(jnp.add, shares)
        summed = functools.reduce(
            jnp.add, [share * p[:, lanes].astype(jnp.float32) for share, p in zip(shares, parts, strict=True)]
        )
        whole = (summed / total).astype(jnp.bfloat16)
        for i, out in enumerate(outs):
            out[:, lanes] = whole[i * Q_ROWS : (i + 1) * Q_ROWS, :]


def combine(parts):
    rows = parts[0].shape[0]
    return pl.pallas_call(
        combine_kernel,
        out_shape=[jax.ShapeDtypeStruct((Q_ROWS, PAIR), jnp.bfloat16)] * 4,
        in_specs=[VMEM] * 4,
        out_specs=[VMEM] * 4,
        compiler_params=pltpu.CompilerParams(vmem_limit_bytes=8 * 2**20),
        cost_estimate=pl.CostEstimate(flops=16 * rows * PAIR, bytes_accessed=16 * rows * PAIR, transcendentals=0),
    )(*parts)


def fetch(sources, first, scratch, sems):
    copies = [
        pltpu.make_async_copy(source.at[:, pl.ds(first, held.shape[1])], held, sems.at[i])
        for i, (source, held) in enumerate(zip(sources, scratch, strict=True))
    ]
    for copy in copies:
        copy.start()
    for copy in copies:
        copy.wait()


def pack(out, q_ref, k_ref, v_ref, lanes):
    out[:KV_ROWS, :HEAD_DIM] = k_ref[:, lanes]
    out[:KV_ROWS, HEAD_DIM:] = v_ref[:, lanes]
    out[KV_ROWS:, :HEAD_DIM] = q_ref[:Q_ROWS, lanes]
    out[KV_ROWS:, HEAD_DIM:] = q_ref[Q_ROWS:, lanes]


def pack_extra_kernel(*refs):
    sources, outs, scratch, sems = refs[:3], refs[3:7], refs[7:10], refs[10]
    fetch(sources, COLUMNS * HEAD_DIM, scratch, sems)
    x = lax.axis_index("x")
    for step, out in zip((0, *STEPS), outs, strict=True):
        head = lax.rem(x + step, 4)
        pack(out, *scratch, pl.ds(pl.multiple_of(head * HEAD_DIM, HEAD_DIM), HEAD_DIM))


def pack_main_kernel(*refs):
    sources, out, scratch, sems = refs[:3], refs[3], refs[4:7], refs[7]
    fetch(sources, 0, scratch, sems)
    for head in range(COLUMNS):
        pack(out.at[head], *scratch, pl.ds(head * HEAD_DIM, HEAD_DIM))


def packed(kernel, arrays, shapes, columns, grant):
    return pl.pallas_call(
        kernel,
        out_shape=[jax.ShapeDtypeStruct(shape, jnp.bfloat16) for shape in shapes],
        in_specs=[HBM] * 3,
        out_specs=[VMEM] * len(shapes),
        scratch_shapes=[pltpu.VMEM((TOKENS, columns), jnp.bfloat16)] * 3 + [pltpu.SemaphoreType.DMA((3,))],
        compiler_params=pltpu.CompilerParams(vmem_limit_bytes=grant * 2**20),
        cost_estimate=pl.CostEstimate(flops=0, bytes_accessed=2**20, transcendentals=0),
    )(*arrays)


def gather_kernel(*refs):
    pieces, xkv, xq = refs[:4], refs[4], refs[5]
    for i, piece in enumerate(pieces):
        xkv[i * KV_ROWS : (i + 1) * KV_ROWS, :] = piece[:KV_ROWS, :]
        xq[i * Q_ROWS : (i + 1) * Q_ROWS, :] = piece[KV_ROWS:, :]


def gather(pieces):
    return pl.pallas_call(
        gather_kernel,
        out_shape=[jax.ShapeDtypeStruct((4 * rows, PAIR), jnp.bfloat16) for rows in (KV_ROWS, Q_ROWS)],
        in_specs=[VMEM] * 4,
        out_specs=[VMEM] * 2,
        compiler_params=pltpu.CompilerParams(vmem_limit_bytes=8 * 2**20),
        cost_estimate=pl.CostEstimate(flops=2 * 10**10, bytes_accessed=2**20, transcendentals=0),
    )(*pieces)


def sort_kernel(got, *refs):
    xkvs, xqs, (kv, both, q, xq) = refs[:4], refs[4:8], refs[8:]
    n = COLUMNS * KV_ROWS
    for i in range(COLUMNS):
        here = slice(i * KV_ROWS, (i + 1) * KV_ROWS)
        block = got[i, :KV_ROWS, :]
        kv[here, :] = block
        both[here, :] = block
        q[i * Q_ROWS : (i + 1) * Q_ROWS, :] = got[i, KV_ROWS:, :]
    for i in range(4):
        rows = xkvs[i].shape[0]
        both[n + i * rows : n + (i + 1) * rows, :] = xkvs[i][...]
        rows = xqs[i].shape[0]
        xq[i * rows : (i + 1) * rows, :] = xqs[i][...]


def sort(got, xkvs, xqs):
    kv, q = COLUMNS * KV_ROWS, COLUMNS * Q_ROWS
    return pl.pallas_call(
        sort_kernel,
        out_shape=[jax.ShapeDtypeStruct((rows, PAIR), jnp.bfloat16) for rows in (kv, 2 * kv, q, q)],
        in_specs=[VMEM] * 9,
        out_specs=[VMEM] * 4,
        compiler_params=pltpu.CompilerParams(vmem_limit_bytes=16 * 2**20),
        cost_estimate=pl.CostEstimate(flops=0, bytes_accessed=2**20, transcendentals=0),
    )(got, *xkvs, *xqs)


def beside_kernel(a, b, *refs):
    both, first, second = refs[-3:]
    rows = a.shape[0]
    both[:rows, :] = a[...]
    both[rows:, :] = b[...]
    first[...] = a[: first.shape[0], :]
    second[...] = b[first.shape[0] :, :]


def beside(a, b, *after):
    rows = (2 * a.shape[0], 3 * K_BLOCK, a.shape[0] - 3 * K_BLOCK)
    return pl.pallas_call(
        beside_kernel,
        out_shape=[jax.ShapeDtypeStruct((count, PAIR), jnp.bfloat16) for count in rows],
        in_specs=[VMEM, VMEM] + [HBM] * len(after),
        out_specs=[VMEM] * 3,
        compiler_params=pltpu.CompilerParams(vmem_limit_bytes=12 * 2**20),
        cost_estimate=pl.CostEstimate(flops=0, bytes_accessed=2**20, transcendentals=0),
    )(a, b, *after)


def join_kernel(a, b, after, out):
    out[: a.shape[0], :] = a[...]
    out[a.shape[0] :, :] = b[...]


def join(a, b, after):
    return pl.pallas_call(
        join_kernel,
        out_shape=jax.ShapeDtypeStruct((a.shape[0] + b.shape[0], PAIR), jnp.bfloat16),
        in_specs=[VMEM, VMEM, HBM],
        out_specs=VMEM,
        compiler_params=pltpu.CompilerParams(vmem_limit_bytes=8 * 2**20),
        cost_estimate=pl.CostEstimate(flops=0, bytes_accessed=2**20, transcendentals=0),
    )(a, b, after)


def unpack_kernel(main, *refs):
    extra, out = refs[:4], refs[4]

    def put(block, lanes):
        out[:Q_ROWS, lanes] = block[:, :HEAD_DIM]
        out[Q_ROWS:, lanes] = block[:, HEAD_DIM:]

    for head in range(COLUMNS):
        put(main.at[head], pl.ds(head * HEAD_DIM, HEAD_DIM))
    x = lax.axis_index("x")
    for step, block in zip((0, *STEPS), extra, strict=True):
        head = COLUMNS + lax.rem(x + step, 4)
        put(block, pl.ds(pl.multiple_of(head * HEAD_DIM, HEAD_DIM), HEAD_DIM))


def unpack(main, extra):
    return pl.pallas_call(
        unpack_kernel,
        out_shape=jax.ShapeDtypeStruct((TOKENS, HEADS * HEAD_DIM), jnp.bfloat16),
        in_specs=[VMEM] * 5,
        out_specs=VMEM,
        compiler_params=pltpu.CompilerParams(vmem_limit_bytes=8 * 2**20),
        cost_estimate=pl.CostEstimate(flops=0, bytes_accessed=2**20, transcendentals=0),
    )(main, *extra)


def local(queries, keys, values):
    arrays = (queries, keys, values)
    rows = KV_ROWS + Q_ROWS
    extra = packed(pack_extra_kernel, arrays, [(rows, PAIR)] * 4, EXTRA * HEAD_DIM, 60)
    (sent,) = packed(pack_main_kernel, arrays, [(COLUMNS, rows, PAIR)], COLUMNS * HEAD_DIM, 12)

    extra = [extra[0]] + [along("x", a, step) for a, step in zip(extra[1:], STEPS, strict=True)]
    xkv, xq = gather(extra)
    xqs = [xq] + [along("y", xq, step) for step in STEPS]
    xkvs = [xkv] + [along_z(xkv, step) for step in STEPS]

    got = lax.all_to_all(sent, ("x", "y"), 0, 0, tiled=True)
    kv, both, q, xq = sort(got, xkvs, xqs)
    kv_next, kv_before = along_z(kv, 1), along_z(kv, 3)
    other = other_core(both)

    rows = kv.shape[0]
    parts = attend(xq, [both[rows:], other[rows:]], None, "part")
    back = [along("y", part, -step) for part, step in zip(parts[1:], STEPS, strict=True)]
    state = attend(q, [kv, other[:rows]], None, None)
    xout = combine([parts[0], *back])

    near, first, second = beside(kv_next, kv_before, state[0], *back)
    first, second = along_z(first, 1), along_z(second, 3)
    state = attend(q, [near, other_core(near)], state, None)
    across = join(first, second, state[0])
    out = attend(q, [across, other_core(across)], state, "out", xout[:1])
    out = lax.all_to_all(out.reshape(COLUMNS, Q_ROWS, PAIR), ("x", "y"), 0, 0, tiled=True)
    xout = [xout[0]] + [along("x", a, -step) for a, step in zip(xout[1:], STEPS, strict=True)]
    return unpack(out, xout)


def solution(mesh):
    fine = Mesh(mesh.devices.reshape(SIZES), AXES)
    return jax.shard_map(
        local, mesh=fine, in_specs=(P(AXES, None),) * 3, out_specs=P(AXES, None), check_vma=False
    )
```

time: 130 us -> 93.6 us (0.72)
  blocking collectives: 40.9 us -> 0 us
  starting transfers between devices: 16.7 us -> 42.5 us
  local copies, waits for them, and re-layouts: 9.71 us -> 0.15 us
  waiting for transfers between devices: 33.4 us -> 24.7 us
  Pallas kernels: 27.7 us -> 25.7 us
    all_to_all x2 -> x0, blocking collectives: 40.9 us -> none  [local(): got = lax.all_to_all(sent, ('x', 'y'), 0, 0, tiled=True)]
    ppermute x9 -> x7, waiting for transfers between devices: 26.9 us -> 8.98 us  [along_z(): return lax.ppermute(a, ('zl', 'zh'), pairs)]
    ppermute x3 -> x12, starting transfers between devices: 3.76 us -> 18.8 us  [along(): return lax.ppermute(a, axis, [(i, (i + step) % 4) for i in range(4)])]
    all_to_all x0 -> x2, starting transfers between devices: none -> 9.89 us  [the longest x1 5.87 us: local(): got = lax.all_to_all(sent, ('x', 'y'), 0, 0, tiled=True)]
    ppermute x3 -> x12, waiting for transfers between devices: 6.42 us -> 12.7 us  [along(): return lax.ppermute(a, axis, [(i, (i + step) % 4) for i in range(4)])]
    unnamed x17 -> x8, local copies, waits for them, and re-layouts: 3.24 us -> 0.02 us
    slice x15 -> x2, local copies, waits for them, and re-layouts: 2.82 us -> 0.13 us  [local(): parts = attend(xq, [both[rows:], other[rows:]], None, 'part')]
    transpose x7 -> x0, local copies, waits for them, and re-layouts: 2.44 us -> none  [the longest x2 2.27 us: by_column(): return a[:, :main].reshape(TOKENS, COLUMNS, HEAD_DIM).transpose(1, 0, 2)]
  transfers between devices with their start and end apart: 17 -> 24, of which waited for: 6 -> 10; matrix products, arithmetic and copies ran while one was open for 3% -> 0% of each run, Pallas kernels for 17% -> 19%
where the time goes in v1:
time: 93.6 us; the launch traced here: 93.2 us
  starting transfers between devices  42.5 us (45%)
  Pallas kernels  25.7 us (27%)
  waiting for transfers between devices  24.7 us (26%)
    pallas_call x4, Pallas kernels, attend(): pl.pallas_call(functools.partial(attend_kernel, len(kvs), len(after), sta...  21.1 us
    ppermute x12, starting transfers between devices, along(): return lax.ppermute(a, axis, [(i, (i + step) % 4) for i in range(4)])  18.8 us
    ppermute x7, starting transfers between devices, along_z(): return lax.ppermute(a, ('zl', 'zh'), pairs)  13.3 us
    ppermute x12, waiting for transfers between devices, along(): return lax.ppermute(a, axis, [(i, (i + step) % 4) for i in range(4)])  12.7 us
    ppermute x7, waiting for transfers between devices, along_z(): return lax.ppermute(a, ('zl', 'zh'), pairs)  8.98 us
    all_to_all x1, starting transfers between devices, local(): got = lax.all_to_all(sent, ('x', 'y'), 0, 0, tiled=True)  5.87 us
    all_to_all x1, starting transfers between devices, local(): lax.all_to_all(out.reshape(COLUMNS, Q_ROWS, PAIR), ('x', 'y'), 0, 0, tile...  4.02 us
    pallas_call x2, Pallas kernels, packed(): pl.pallas_call(kernel, out_shape=[jax.ShapeDtypeStruct(shape, jnp.bfloat1...  3.06 us
  transfers between devices with their start and end apart: 24, of which 10 were waited for; matrix products, arithmetic and copies ran while one was open for 0% of the time, Pallas kernels for 19%

profile of v1, /device:TPU:0, one launch (start us, length us, event | category | flops | bytes accessed | tf_op | source)
XLA Modules:
  0.0 93.2 jit_solution(9678600531017110611)
XLA Ops:
  0.0 1.8 %shard_map.38 = (bf16[120,256]{1,0:T(8,128)(2,1)}, bf16[120,256]{1,0:T(8,128)(2,1)}, bf16[120,256]{1,0:T(8,128)(2,1)}, bf16[120,256]{1,0:T(8,128)(2,1)}) custom-call(bf16[80,2560]{1,0:T(8,128)(2,1)} %refs_0_.3, bf16[80,2560]{1,0:T(8,128)(2,1)} %refs_1_.3, bf16[80,2560]{1,0:T(8,128)(2,1)} %refs_2_.3), custom_call_target="tpu_custom_call" | custom-call | bytes 1048576 | tf_op jit(solution)/shard_map/pallas_call | solution.py:199
  1.8 1.6 %collective-permute-start = (bf16[120,256]{1,0:T(8,128)(2,1)}, bf16[120,256]{1,0:T(8,128)(2,1)S(1)}, u32[]{:S(2)}, u32[]{:S(2)}) collective-permute-start(bf16[120,256]{1,0:T(8,128)(2,1)} %get-tuple-element.31), channel_id=1, source_target_pairs={{0,32},{32,64},{64,96},{96,0},{1,33},{33,65},{65,97},{97,1},{2,34}... | collective-permute-start | bytes 184328 | tf_op jit(solution)/shard_map/ppermute | solution.py:37
  3.5 1.7 %collective-permute-start.1 = (bf16[120,256]{1,0:T(8,128)(2,1)}, bf16[120,256]{1,0:T(8,128)(2,1)S(1)}, u32[]{:S(2)}, u32[]{:S(2)}) collective-permute-start(bf16[120,256]{1,0:T(8,128)(2,1)} %get-tuple-element.32), channel_id=1, source_target_pairs={{0,96},{32,0},{64,32},{96,64},{1,97},{33,1},{65,33},{97,65},{2,98}... | collective-permute-start | bytes 184328 | tf_op jit(solution)/shard_map/ppermute | solution.py:37
  5.1 1.9 %collective-permute-start.2 = (bf16[120,256]{1,0:T(8,128)(2,1)}, bf16[120,256]{1,0:T(8,128)(2,1)S(1)}, u32[]{:S(2)}, u32[]{:S(2)}) collective-permute-start(bf16[120,256]{1,0:T(8,128)(2,1)} %get-tuple-element.33), channel_id=1, source_target_pairs={{0,64},{32,96},{64,0},{96,32},{1,65},{33,97},{65,1},{97,33},{2,66}... | collective-permute-start | bytes 184328 | tf_op jit(solution)/shard_map/ppermute | solution.py:37
  7.1 1.2 %shard_map.37 = bf16[16,120,256]{2,1,0:T(8,128)(2,1)} custom-call(bf16[80,2560]{1,0:T(8,128)(2,1)S(1)} %copy-done, bf16[80,2560]{1,0:T(8,128)(2,1)S(1)} %copy-done.1, bf16[80,2560]{1,0:T(8,128)(2,1)S(1)} %copy-done.2), custom_call_target="tpu_custom_call" | custom-call | bytes 1048576 | tf_op jit(solution)/shard_map/pallas_call | solution.py:199
  8.3 0.0 copy-start.3
  8.3 5.9 %all-to-all-start = ((bf16[16,120,256]{2,1,0:T(8,128)(2,1)}), bf16[16,120,256]{2,1,0:T(8,128)(2,1)S(1)}, u32[]{:S(2)}, u32[]{:S(2)}) async-start(bf16[16,120,256]{2,1,0:T(8,128)(2,1)} %shard_map.37), calls=%async_computation | async-start | bytes 1966080 | tf_op jit(solution)/shard_map/all_to_all | solution.py:330
  14.2 0.0 collective-permute-done.refs_1_
  14.2 0.0 collective-permute-done.1.refs_2_
  14.3 3.5 %collective-permute-start.8 = (bf16[160,256]{1,0:T(8,128)(2,1)S(1)}, bf16[160,256]{1,0:T(8,128)(2,1)S(1)}, u32[]{:S(2)}, u32[]{:S(2)}) collective-permute-start(bf16[160,256]{1,0:T(8,128)(2,1)S(1)} %get-tuple-element.35.refs_4_), channel_id=1, source_target_pairs={{0,8},{4,12},{8,0},{12,4},{1,9},{5,13},{9,1},{13,5},{2,10},{6,14},... | collective-permute-start | bytes 245768 | tf_op jit(solution)/shard_map/ppermute | solution.py:37
  17.8 3.9 %collective-permute-start.5 = (bf16[320,256]{1,0:T(8,128)(2,1)S(1)}, bf16[320,256]{1,0:T(8,128)(2,1)S(1)}, u32[]{:S(2)}, u32[]{:S(2)}) collective-permute-start(bf16[320,256]{1,0:T(8,128)(2,1)S(1)} %get-tuple-element.34.refs_0_), channel_id=1, source_target_pairs={{0,2},{2,0},{16,18},{18,16},{1,3},{3,1},{17,19},{19,17},{4,6},{6,4... | collective-permute-start | bytes 491528 | tf_op jit(solution)/shard_map/ppermute | solution.py:33
  21.6 0.7 collective-permute-start.4
  22.4 1.3 %collective-permute-start.3 = (bf16[320,256]{1,0:T(8,128)(2,1)S(1)}, bf16[320,256]{1,0:T(8,128)(2,1)S(1)}, u32[]{:S(2)}, u32[]{:S(2)}) collective-permute-start(bf16[320,256]{1,0:T(8,128)(2,1)S(1)} %get-tuple-element.34.refs_0_), channel_id=1, source_target_pairs={{0,16},{2,18},{16,2},{18,0},{1,17},{3,19},{17,3},{19,1},{4,20},{6,... | collective-permute-start | bytes 491528 | tf_op jit(solution)/shard_map/ppermute | solution.py:33
  23.7 1.2 %collective-permute-start.7 = (bf16[160,256]{1,0:T(8,128)(2,1)S(1)}, bf16[160,256]{1,0:T(8,128)(2,1)S(1)}, u32[]{:S(2)}, u32[]{:S(2)}) collective-permute-start(bf16[160,256]{1,0:T(8,128)(2,1)S(1)} %get-tuple-element.35.refs_4_), channel_id=1, source_target_pairs={{0,12},{4,0},{8,4},{12,8},{1,13},{5,1},{9,5},{13,9},{2,14},{6,2},{... | collective-permute-start | bytes 245768 | tf_op jit(solution)/shard_map/ppermute | solution.py:37
  24.8 5.2 %collective-permute-done.8.refs_7_ = bf16[160,256]{1,0:T(8,128)(2,1)S(1)} collective-permute-done((bf16[160,256]{1,0:T(8,128)(2,1)S(1)}, bf16[160,256]{1,0:T(8,128)(2,1)S(1)}, u32[]{:S(2)}, u32[]{:S(2)}) %collective-permute-start.8) | collective-permute-done | bytes 81952 | tf_op jit(solution)/shard_map/ppermute | solution.py:37
  30.1 1.2 %collective-permute-start.6 = (bf16[160,256]{1,0:T(8,128)(2,1)S(1)}, bf16[160,256]{1,0:T(8,128)(2,1)S(1)}, u32[]{:S(2)}, u32[]{:S(2)}) collective-permute-start(bf16[160,256]{1,0:T(8,128)(2,1)S(1)} %get-tuple-element.35.refs_4_), channel_id=1, source_target_pairs={{0,4},{4,8},{8,12},{12,0},{1,5},{5,9},{9,13},{13,1},{2,6},{6,10},{... | collective-permute-start | bytes 245768 | tf_op jit(solution)/shard_map/ppermute | solution.py:37
  31.3 0.0 collective-permute-done.7.refs_6_
  31.3 4.4 %collective-permute-done.6.refs_5_ = bf16[160,256]{1,0:T(8,128)(2,1)S(1)} collective-permute-done((bf16[160,256]{1,0:T(8,128)(2,1)S(1)}, bf16[160,256]{1,0:T(8,128)(2,1)S(1)}, u32[]{:S(2)}, u32[]{:S(2)}) %collective-permute-start.6) | collective-permute-done | bytes 81952 | tf_op jit(solution)/shard_map/ppermute | solution.py:37
  35.7 0.0 all-to-all-done.got
  35.7 0.2 shard_map.40
  35.9 0.1 collective-permute-start.11
  36.1 4.1 %collective-permute-start.10 = (bf16[1280,256]{1,0:T(8,128)(2,1)S(1)}, bf16[1280,256]{1,0:T(8,128)(2,1)S(1)}, u32[]{:S(2)}, u32[]{:S(2)}) collective-permute-start(bf16[1280,256]{1,0:T(8,128)(2,1)S(1)} %get-tuple-element.37.refs_1_), channel_id=1, source_target_pairs={{0,18},{2,16},{16,0},{18,2},{1,19},{3,17},{17,1},{19,3},{4,22},{6,... | collective-permute-start | bytes 1966088 | tf_op jit(solution)/shard_map/ppermute | solution.py:33
  40.2 0.1 fusion
  40.3 4.4 %shard_map.42 = (bf16[160,512]{1,0:T(8,128)(2,1)S(1)}, bf16[160,512]{1,0:T(8,128)(2,1)S(1)}, bf16[160,512]{1,0:T(8,128)(2,1)S(1)}, bf16[160,512]{1,0:T(8,128)(2,1)S(1)}) custom-call(bf16[640,256]{1,0:T(8,128)(2,1)S(1)} %get-tuple-element.40.refs_0_, bf16[1280,256]{1,0:T(8,128)(2,1)S(1)} %slice.10.refs_1_, bf16[1280,256]{1,0:T(8,128)(2,1)S(1)} %get-tuple-element.55.refs_2_), custom_call_target="tpu_custom_call" | custom-call | flops 209715200 | bytes 1310720 | tf_op jit(solution)/shard_map/pallas_call | solution.py:122
  44.7 0.7 collective-permute-start.12
  45.4 1.4 %collective-permute-start.13 = (bf16[160,512]{1,0:T(8,128)(2,1)S(1)}, bf16[160,512]{1,0:T(8,128)(2,1)S(1)}, u32[]{:S(2)}, u32[]{:S(2)}) collective-permute-start(bf16[160,512]{1,0:T(8,128)(2,1)S(1)} %get-tuple-element.42), channel_id=1, source_target_pairs={{0,4},{4,8},{8,12},{12,0},{1,5},{5,9},{9,13},{13,1},{2,6},{6,10},{... | collective-permute-start | bytes 491528 | tf_op jit(solution)/shard_map/ppermute | solution.py:37
  46.8 0.2 collective-permute-start.14
  46.9 4.1 %shard_map.41 = (f32[1280,256]{1,0:T(8,128)S(1)}, f32[1280,128]{1,0:T(8,128)S(1)}) custom-call(bf16[640,256]{1,0:T(8,128)(2,1)S(1)} %get-tuple-element.36.refs_0_, bf16[1280,256]{1,0:T(8,128)(2,1)S(1)} %get-tuple-element.37.refs_1_, bf16[1280,256]{1,0:T(8,128)(2,1)S(1)} %get-tuple-element.56.refs_2_), custom_call_target="tpu_custom_call" | custom-call | flops 209715200 | bytes 1310720 | tf_op jit(solution)/shard_map/pallas_call | solution.py:122
  51.1 3.7 %collective-permute-done.10.b = bf16[1280,256]{1,0:T(8,128)(2,1)S(1)} collective-permute-done((bf16[1280,256]{1,0:T(8,128)(2,1)S(1)}, bf16[1280,256]{1,0:T(8,128)(2,1)S(1)}, u32[]{:S(2)}, u32[]{:S(2)}) %collective-permute-start.10) | collective-permute-done | bytes 655392 | tf_op jit(solution)/shard_map/ppermute | solution.py:33
  54.8 3.4 %collective-permute-done.9.a = bf16[1280,256]{1,0:T(8,128)(2,1)S(1)} collective-permute-done((bf16[1280,256]{1,0:T(8,128)(2,1)S(1)}, bf16[1280,256]{1,0:T(8,128)(2,1)S(1)}, u32[]{:S(2)}, u32[]{:S(2)}) %collective-permute-start.9) | collective-permute-done | bytes 655392 | tf_op jit(solution)/shard_map/ppermute | solution.py:33
  58.2 0.1 shard_map.43
  58.4 0.1 collective-permute-start.17
  58.5 0.1 collective-permute-start.15
  58.6 3.2 %collective-permute-start.16 = (bf16[512,256]{1,0:T(8,128)(2,1)S(1)}, bf16[512,256]{1,0:T(8,128)(2,1)S(1)}, u32[]{:S(2)}, u32[]{:S(2)}) collective-permute-start(bf16[512,256]{1,0:T(8,128)(2,1)S(1)} %get-tuple-element.45), channel_id=1, source_target_pairs={{0,18},{2,16},{16,0},{18,2},{1,19},{3,17},{17,1},{19,3},{4,22},{6,... | collective-permute-start | bytes 786440 | tf_op jit(solution)/shard_map/ppermute | solution.py:33
  61.8 7.6 %shard_map.44 = (f32[1280,256]{1,0:T(8,128)S(1)}, f32[1280,128]{1,0:T(8,128)S(1)}) custom-call(bf16[640,256]{1,0:T(8,128)(2,1)S(1)} %get-tuple-element.36.refs_0_, bf16[2560,256]{1,0:T(8,128)(2,1)S(1)} %get-tuple-element.46.refs_1_, bf16[2560,256]{1,0:T(8,128)(2,1)S(1)} %collective-permute-done.17.refs_2_, ...), custom_call_target="tpu_custom_call" | custom-call | flops 419430400 | bytes 2621440 | tf_op jit(solution)/shard_map/pallas_call | solution.py:122
  69.4 1.8 %collective-permute-done.15.a = bf16[768,256]{1,0:T(8,128)(2,1)S(1)} collective-permute-done((bf16[768,256]{1,0:T(8,128)(2,1)S(1)}, bf16[768,256]{1,0:T(8,128)(2,1)S(1)}, u32[]{:S(2)}, u32[]{:S(2)}) %collective-permute-start.15) | collective-permute-done | bytes 393248 | tf_op jit(solution)/shard_map/ppermute | solution.py:33
  71.3 0.3 collective-permute-start.18
  71.6 0.3 shard_map.46
  71.9 1.8 %collective-permute-done.18.refs_2_ = bf16[1280,256]{1,0:T(8,128)(2,1)S(1)} collective-permute-done((bf16[1280,256]{1,0:T(8,128)(2,1)S(1)}, bf16[1280,256]{1,0:T(8,128)(2,1)S(1)}, u32[]{:S(2)}, u32[]{:S(2)}) %collective-permute-start.18) | collective-permute-done | bytes 655392 | tf_op jit(solution)/shard_map/ppermute | solution.py:41
  73.7 4.9 %shard_map.47 = bf16[640,256]{1,0:T(8,128)(2,1)} custom-call(bf16[640,256]{1,0:T(8,128)(2,1)S(1)} %get-tuple-element.36.refs_0_, bf16[1280,256]{1,0:T(8,128)(2,1)S(1)} %shard_map.45.refs_1_, bf16[1280,256]{1,0:T(8,128)(2,1)S(1)} %collective-permute-done.18.refs_2_, f32[1280,256]{1,0:T(8,128)S(1)} %get-tuple-element.48.after.refs_3_, ...), custom_call_target="tpu_custom_call" | custom-call | flops 209715200 | bytes 1310720 | tf_op jit(solution)/shard_map/pallas_call | solution.py:122
  78.6 4.0 %all-to-all-start.1 = ((bf16[16,40,256]{2,1,0:T(8,128)(2,1)}), bf16[16,40,256]{2,1,0:T(8,128)(2,1)S(1)}, u32[]{:S(2)}, u32[]{:S(2)}) async-start(bf16[16,40,256]{2,1,0:T(8,128)(2,1)} %bitcast), calls=%async_computation.1 | async-start | bytes 655360 | tf_op jit(solution)/shard_map/all_to_all | solution.py:346
  82.6 3.1 %collective-permute-start.19 = (bf16[40,256]{1,0:T(8,128)(2,1)S(1)}, bf16[40,256]{1,0:T(8,128)(2,1)S(1)}, u32[]{:S(2)}, u32[]{:S(2)}) collective-permute-start(bf16[40,256]{1,0:T(8,128)(2,1)S(1)} %get-tuple-element.52), channel_id=1, source_target_pairs={{0,96},{32,0},{64,32},{96,64},{1,97},{33,1},{65,33},{97,65},{2,98}... | collective-permute-start | bytes 61448 | tf_op jit(solution)/shard_map/ppermute | solution.py:37
  85.8 2.3 %collective-permute-start.21 = (bf16[40,256]{1,0:T(8,128)(2,1)S(1)}, bf16[40,256]{1,0:T(8,128)(2,1)S(1)}, u32[]{:S(2)}, u32[]{:S(2)}) collective-permute-start(bf16[40,256]{1,0:T(8,128)(2,1)S(1)} %get-tuple-element.54), channel_id=1, source_target_pairs={{0,64},{32,96},{64,0},{96,32},{1,65},{33,97},{65,1},{97,33},{2,66}... | collective-permute-start | bytes 61448 | tf_op jit(solution)/shard_map/ppermute | solution.py:37
  88.1 1.0 %collective-permute-done.19.refs_1_ = bf16[40,256]{1,0:T(8,128)(2,1)S(1)} collective-permute-done((bf16[40,256]{1,0:T(8,128)(2,1)S(1)}, bf16[40,256]{1,0:T(8,128)(2,1)S(1)}, u32[]{:S(2)}, u32[]{:S(2)}) %collective-permute-start.19) | collective-permute-done | bytes 20512 | tf_op jit(solution)/shard_map/ppermute | solution.py:37
  89.1 1.7 %collective-permute-done.20.refs_2_ = bf16[40,256]{1,0:T(8,128)(2,1)S(1)} collective-permute-done((bf16[40,256]{1,0:T(8,128)(2,1)S(1)}, bf16[40,256]{1,0:T(8,128)(2,1)S(1)}, u32[]{:S(2)}, u32[]{:S(2)}) %collective-permute-start.20) | collective-permute-done | bytes 20512 | tf_op jit(solution)/shard_map/ppermute | solution.py:37
  90.9 0.2 collective-permute-done.21.refs_3_
  91.1 1.3 %all-to-all-done.1.main = bf16[16,40,256]{2,1,0:T(8,128)(2,1)S(1)} async-done(((bf16[16,40,256]{2,1,0:T(8,128)(2,1)}), bf16[16,40,256]{2,1,0:T(8,128)(2,1)S(1)}, u32[]{:S(2)}, u32[]{:S(2)}) %all-to-all-start.1) | async-done | bytes 327712 | tf_op jit(solution)/shard_map/all_to_all | solution.py:346
  92.4 0.8 shard_map.48
  (22 shorter events, 0.2 us)
Async XLA Ops:
  0.0 7.0 %copy-start.2 = (bf16[80,2560]{1,0:T(8,128)(2,1)S(1)}, bf16[80,2560]{1,0:T(8,128)(2,1)}, u32[]{:S(2)}) copy-start(bf16[80,2560]{1,0:T(8,128)(2,1)} %refs_2_.3) | copy-start | bytes 1228804
  0.0 7.0 %copy-start.1 = (bf16[80,2560]{1,0:T(8,128)(2,1)S(1)}, bf16[80,2560]{1,0:T(8,128)(2,1)}, u32[]{:S(2)}) copy-start(bf16[80,2560]{1,0:T(8,128)(2,1)} %refs_1_.3) | copy-start | bytes 1228804
  0.0 7.0 %copy-start = (bf16[80,2560]{1,0:T(8,128)(2,1)S(1)}, bf16[80,2560]{1,0:T(8,128)(2,1)}, u32[]{:S(2)}) copy-start(bf16[80,2560]{1,0:T(8,128)(2,1)} %refs_0_.3) | copy-start | bytes 1228804
  1.8 12.4 %collective-permute-start = (bf16[120,256]{1,0:T(8,128)(2,1)}, bf16[120,256]{1,0:T(8,128)(2,1)S(1)}, u32[]{:S(2)}, u32[]{:S(2)}) collective-permute-start(bf16[120,256]{1,0:T(8,128)(2,1)} %get-tuple-element.31), channel_id=1, source_target_pairs={{0,32},{32,64},{64,96},{96,0},{1,33},{33,65},{65,97},{97,1},{2,34}... | collective-permute-start | bytes 184328 | tf_op jit(solution)/shard_map/ppermute | solution.py:37
  3.5 10.7 %collective-permute-start.1 = (bf16[120,256]{1,0:T(8,128)(2,1)}, bf16[120,256]{1,0:T(8,128)(2,1)S(1)}, u32[]{:S(2)}, u32[]{:S(2)}) collective-permute-start(bf16[120,256]{1,0:T(8,128)(2,1)} %get-tuple-element.32), channel_id=1, source_target_pairs={{0,96},{32,0},{64,32},{96,64},{1,97},{33,1},{65,33},{97,65},{2,98}... | collective-permute-start | bytes 184328 | tf_op jit(solution)/shard_map/ppermute | solution.py:37
  5.1 9.1 %collective-permute-start.2 = (bf16[120,256]{1,0:T(8,128)(2,1)}, bf16[120,256]{1,0:T(8,128)(2,1)S(1)}, u32[]{:S(2)}, u32[]{:S(2)}) collective-permute-start(bf16[120,256]{1,0:T(8,128)(2,1)} %get-tuple-element.33), channel_id=1, source_target_pairs={{0,64},{32,96},{64,0},{96,32},{1,65},{33,97},{65,1},{97,33},{2,66}... | collective-permute-start | bytes 184328 | tf_op jit(solution)/shard_map/ppermute | solution.py:37
  8.3 5.9 %copy-start.3 = (bf16[120,256]{1,0:T(8,128)(2,1)S(1)}, bf16[120,256]{1,0:T(8,128)(2,1)}, u32[]{:S(2)}) copy-start(bf16[120,256]{1,0:T(8,128)(2,1)} %get-tuple-element.30.refs_0_) | copy-start | bytes 184324
  8.3 27.4 %all-to-all-start = ((bf16[16,120,256]{2,1,0:T(8,128)(2,1)}), bf16[16,120,256]{2,1,0:T(8,128)(2,1)S(1)}, u32[]{:S(2)}, u32[]{:S(2)}) async-start(bf16[16,120,256]{2,1,0:T(8,128)(2,1)} %shard_map.37), calls=%async_computation | async-start | bytes 1966080 | tf_op jit(solution)/shard_map/all_to_all | solution.py:330
  14.3 15.8 %collective-permute-start.8 = (bf16[160,256]{1,0:T(8,128)(2,1)S(1)}, bf16[160,256]{1,0:T(8,128)(2,1)S(1)}, u32[]{:S(2)}, u32[]{:S(2)}) collective-permute-start(bf16[160,256]{1,0:T(8,128)(2,1)S(1)} %get-tuple-element.35.refs_4_), channel_id=1, source_target_pairs={{0,8},{4,12},{8,0},{12,4},{1,9},{5,13},{9,1},{13,5},{2,10},{6,14},... | collective-permute-start | bytes 245768 | tf_op jit(solution)/shard_map/ppermute | solution.py:37
  17.8 18.0 %collective-permute-start.5 = (bf16[320,256]{1,0:T(8,128)(2,1)S(1)}, bf16[320,256]{1,0:T(8,128)(2,1)S(1)}, u32[]{:S(2)}, u32[]{:S(2)}) collective-permute-start(bf16[320,256]{1,0:T(8,128)(2,1)S(1)} %get-tuple-element.34.refs_0_), channel_id=1, source_target_pairs={{0,2},{2,0},{16,18},{18,16},{1,3},{3,1},{17,19},{19,17},{4,6},{6,4... | collective-permute-start | bytes 491528 | tf_op jit(solution)/shard_map/ppermute | solution.py:33
  21.6 14.1 %collective-permute-start.4 = (bf16[320,256]{1,0:T(8,128)(2,1)S(1)}, bf16[320,256]{1,0:T(8,128)(2,1)S(1)}, u32[]{:S(2)}, u32[]{:S(2)}) collective-permute-start(bf16[320,256]{1,0:T(8,128)(2,1)S(1)} %get-tuple-element.34.refs_0_), channel_id=1, source_target_pairs={{0,18},{2,16},{16,0},{18,2},{1,19},{3,17},{17,1},{19,3},{4,22},{6,... | collective-permute-start | bytes 491528 | tf_op jit(solution)/shard_map/ppermute | solution.py:33
  22.4 13.4 %collective-permute-start.3 = (bf16[320,256]{1,0:T(8,128)(2,1)S(1)}, bf16[320,256]{1,0:T(8,128)(2,1)S(1)}, u32[]{:S(2)}, u32[]{:S(2)}) collective-permute-start(bf16[320,256]{1,0:T(8,128)(2,1)S(1)} %get-tuple-element.34.refs_0_), channel_id=1, source_target_pairs={{0,16},{2,18},{16,2},{18,0},{1,17},{3,19},{17,3},{19,1},{4,20},{6,... | collective-permute-start | bytes 491528 | tf_op jit(solution)/shard_map/ppermute | solution.py:33
  23.7 7.6 %collective-permute-start.7 = (bf16[160,256]{1,0:T(8,128)(2,1)S(1)}, bf16[160,256]{1,0:T(8,128)(2,1)S(1)}, u32[]{:S(2)}, u32[]{:S(2)}) collective-permute-start(bf16[160,256]{1,0:T(8,128)(2,1)S(1)} %get-tuple-element.35.refs_4_), channel_id=1, source_target_pairs={{0,12},{4,0},{8,4},{12,8},{1,13},{5,1},{9,5},{13,9},{2,14},{6,2},{... | collective-permute-start | bytes 245768 | tf_op jit(solution)/shard_map/ppermute | solution.py:37
  30.1 5.7 %collective-permute-start.6 = (bf16[160,256]{1,0:T(8,128)(2,1)S(1)}, bf16[160,256]{1,0:T(8,128)(2,1)S(1)}, u32[]{:S(2)}, u32[]{:S(2)}) collective-permute-start(bf16[160,256]{1,0:T(8,128)(2,1)S(1)} %get-tuple-element.35.refs_4_), channel_id=1, source_target_pairs={{0,4},{4,8},{8,12},{12,0},{1,5},{5,9},{9,13},{13,1},{2,6},{6,10},{... | collective-permute-start | bytes 245768 | tf_op jit(solution)/shard_map/ppermute | solution.py:37
  35.9 4.3 %collective-permute-start.11 = (bf16[2560,256]{1,0:T(8,128)(2,1)S(1)}, bf16[2560,256]{1,0:T(8,128)(2,1)S(1)}, u32[]{:S(2)}, u32[]{:S(2)}) collective-permute-start(bf16[2560,256]{1,0:T(8,128)(2,1)S(1)} %get-tuple-element.38), channel_id=1, source_target_pairs={{0,1},{1,0},{2,3},{3,2},{4,5},{5,4},{6,7},{7,6},{8,9},{9,8},{10,11... | collective-permute-start | bytes 3932168 | tf_op jit(solution)/shard_map/ppermute | solution.py:41
  36.1 18.8 %collective-permute-start.10 = (bf16[1280,256]{1,0:T(8,128)(2,1)S(1)}, bf16[1280,256]{1,0:T(8,128)(2,1)S(1)}, u32[]{:S(2)}, u32[]{:S(2)}) collective-permute-start(bf16[1280,256]{1,0:T(8,128)(2,1)S(1)} %get-tuple-element.37.refs_1_), channel_id=1, source_target_pairs={{0,18},{2,16},{16,0},{18,2},{1,19},{3,17},{17,1},{19,3},{4,22},{6,... | collective-permute-start | bytes 1966088 | tf_op jit(solution)/shard_map/ppermute | solution.py:33
  40.2 18.1 %collective-permute-start.9 = (bf16[1280,256]{1,0:T(8,128)(2,1)S(1)}, bf16[1280,256]{1,0:T(8,128)(2,1)S(1)}, u32[]{:S(2)}, u32[]{:S(2)}) collective-permute-start(bf16[1280,256]{1,0:T(8,128)(2,1)S(1)} %get-tuple-element.37.refs_1_), channel_id=1, source_target_pairs={{0,16},{2,18},{16,2},{18,0},{1,17},{3,19},{17,3},{19,1},{4,20},{6,... | collective-permute-start | bytes 1966088 | tf_op jit(solution)/shard_map/ppermute | solution.py:33
  44.7 13.5 %collective-permute-start.12 = (bf16[160,512]{1,0:T(8,128)(2,1)S(1)}, bf16[160,512]{1,0:T(8,128)(2,1)S(1)}, u32[]{:S(2)}, u32[]{:S(2)}) collective-permute-start(bf16[160,512]{1,0:T(8,128)(2,1)S(1)} %get-tuple-element.41), channel_id=1, source_target_pairs={{0,12},{4,0},{8,4},{12,8},{1,13},{5,1},{9,5},{13,9},{2,14},{6,2},{... | collective-permute-start | bytes 491528 | tf_op jit(solution)/shard_map/ppermute | solution.py:37
  45.4 12.8 %collective-permute-start.13 = (bf16[160,512]{1,0:T(8,128)(2,1)S(1)}, bf16[160,512]{1,0:T(8,128)(2,1)S(1)}, u32[]{:S(2)}, u32[]{:S(2)}) collective-permute-start(bf16[160,512]{1,0:T(8,128)(2,1)S(1)} %get-tuple-element.42), channel_id=1, source_target_pairs={{0,4},{4,8},{8,12},{12,0},{1,5},{5,9},{9,13},{13,1},{2,6},{6,10},{... | collective-permute-start | bytes 491528 | tf_op jit(solution)/shard_map/ppermute | solution.py:37
  46.8 11.4 %collective-permute-start.14 = (bf16[160,512]{1,0:T(8,128)(2,1)S(1)}, bf16[160,512]{1,0:T(8,128)(2,1)S(1)}, u32[]{:S(2)}, u32[]{:S(2)}) collective-permute-start(bf16[160,512]{1,0:T(8,128)(2,1)S(1)} %get-tuple-element.43), channel_id=1, source_target_pairs={{0,8},{4,12},{8,0},{12,4},{1,9},{5,13},{9,1},{13,5},{2,10},{6,14},... | collective-permute-start | bytes 491528 | tf_op jit(solution)/shard_map/ppermute | solution.py:37
  58.4 3.4 %collective-permute-start.17 = (bf16[2560,256]{1,0:T(8,128)(2,1)S(1)}, bf16[2560,256]{1,0:T(8,128)(2,1)S(1)}, u32[]{:S(2)}, u32[]{:S(2)}) collective-permute-start(bf16[2560,256]{1,0:T(8,128)(2,1)S(1)} %get-tuple-element.46.refs_1_), channel_id=1, source_target_pairs={{0,1},{1,0},{2,3},{3,2},{4,5},{5,4},{6,7},{7,6},{8,9},{9,8},{10,11... | collective-permute-start | bytes 3932168 | tf_op jit(solution)/shard_map/ppermute | solution.py:41
  58.5 12.7 %collective-permute-start.15 = (bf16[768,256]{1,0:T(8,128)(2,1)S(1)}, bf16[768,256]{1,0:T(8,128)(2,1)S(1)}, u32[]{:S(2)}, u32[]{:S(2)}) collective-permute-start(bf16[768,256]{1,0:T(8,128)(2,1)S(1)} %get-tuple-element.44), channel_id=1, source_target_pairs={{0,16},{2,18},{16,2},{18,0},{1,17},{3,19},{17,3},{19,1},{4,20},{6,... | collective-permute-start | bytes 1179656 | tf_op jit(solution)/shard_map/ppermute | solution.py:33
  58.6 10.8 %collective-permute-start.16 = (bf16[512,256]{1,0:T(8,128)(2,1)S(1)}, bf16[512,256]{1,0:T(8,128)(2,1)S(1)}, u32[]{:S(2)}, u32[]{:S(2)}) collective-permute-start(bf16[512,256]{1,0:T(8,128)(2,1)S(1)} %get-tuple-element.45), channel_id=1, source_target_pairs={{0,18},{2,16},{16,0},{18,2},{1,19},{3,17},{17,1},{19,3},{4,22},{6,... | collective-permute-start | bytes 786440 | tf_op jit(solution)/shard_map/ppermute | solution.py:33
  71.3 2.4 %collective-permute-start.18 = (bf16[1280,256]{1,0:T(8,128)(2,1)S(1)}, bf16[1280,256]{1,0:T(8,128)(2,1)S(1)}, u32[]{:S(2)}, u32[]{:S(2)}) collective-permute-start(bf16[1280,256]{1,0:T(8,128)(2,1)S(1)} %shard_map.45.refs_1_), channel_id=1, source_target_pairs={{0,1},{1,0},{2,3},{3,2},{4,5},{5,4},{6,7},{7,6},{8,9},{9,8},{10,11... | collective-permute-start | bytes 1966088 | tf_op jit(solution)/shard_map/ppermute | solution.py:41
  78.6 13.8 %all-to-all-start.1 = ((bf16[16,40,256]{2,1,0:T(8,128)(2,1)}), bf16[16,40,256]{2,1,0:T(8,128)(2,1)S(1)}, u32[]{:S(2)}, u32[]{:S(2)}) async-start(bf16[16,40,256]{2,1,0:T(8,128)(2,1)} %bitcast), calls=%async_computation.1 | async-start | bytes 655360 | tf_op jit(solution)/shard_map/all_to_all | solution.py:346
  82.6 6.5 %collective-permute-start.19 = (bf16[40,256]{1,0:T(8,128)(2,1)S(1)}, bf16[40,256]{1,0:T(8,128)(2,1)S(1)}, u32[]{:S(2)}, u32[]{:S(2)}) collective-permute-start(bf16[40,256]{1,0:T(8,128)(2,1)S(1)} %get-tuple-element.52), channel_id=1, source_target_pairs={{0,96},{32,0},{64,32},{96,64},{1,97},{33,1},{65,33},{97,65},{2,98}... | collective-permute-start | bytes 61448 | tf_op jit(solution)/shard_map/ppermute | solution.py:37
  85.8 5.1 %collective-permute-start.20 = (bf16[40,256]{1,0:T(8,128)(2,1)S(1)}, bf16[40,256]{1,0:T(8,128)(2,1)S(1)}, u32[]{:S(2)}, u32[]{:S(2)}) collective-permute-start(bf16[40,256]{1,0:T(8,128)(2,1)S(1)} %get-tuple-element.53), channel_id=1, source_target_pairs={{0,32},{32,64},{64,96},{96,0},{1,33},{33,65},{65,97},{97,1},{2,34}... | collective-permute-start | bytes 61448 | tf_op jit(solution)/shard_map/ppermute | solution.py:37
  85.8 5.3 %collective-permute-start.21 = (bf16[40,256]{1,0:T(8,128)(2,1)S(1)}, bf16[40,256]{1,0:T(8,128)(2,1)S(1)}, u32[]{:S(2)}, u32[]{:S(2)}) collective-permute-start(bf16[40,256]{1,0:T(8,128)(2,1)S(1)} %get-tuple-element.54), channel_id=1, source_target_pairs={{0,64},{32,96},{64,0},{96,32},{1,65},{33,97},{65,1},{97,33},{2,66}... | collective-permute-start | bytes 61448 | tf_op jit(solution)/shard_map/ppermute | solution.py:37

commit v2 on v1

--- a/solution.py
+++ b/solution.py
@@ -225,32 +225,39 @@
     )(*pieces)
 
 
-def sort_kernel(got, *refs):
-    xkvs, xqs, (kv, both, q, xq) = refs[:4], refs[4:8], refs[8:]
-    n = COLUMNS * KV_ROWS
+def sort_kernel(got, kv, q):
     for i in range(COLUMNS):
-        here = slice(i * KV_ROWS, (i + 1) * KV_ROWS)
-        block = got[i, :KV_ROWS, :]
-        kv[here, :] = block
-        both[here, :] = block
+        kv[i * KV_ROWS : (i + 1) * KV_ROWS, :] = got[i, :KV_ROWS, :]
         q[i * Q_ROWS : (i + 1) * Q_ROWS, :] = got[i, KV_ROWS:, :]
-    for i in range(4):
-        rows = xkvs[i].shape[0]
-        both[n + i * rows : n + (i + 1) * rows, :] = xkvs[i][...]
-        rows = xqs[i].shape[0]
-        xq[i * rows : (i + 1) * rows, :] = xqs[i][...]
-
-
-def sort(got, xkvs, xqs):
-    kv, q = COLUMNS * KV_ROWS, COLUMNS * Q_ROWS
+
+
+def sort(got):
     return pl.pallas_call(
         sort_kernel,
-        out_shape=[jax.ShapeDtypeStruct((rows, PAIR), jnp.bfloat16) for rows in (kv, 2 * kv, q, q)],
-        in_specs=[VMEM] * 9,
-        out_specs=[VMEM] * 4,
-        compiler_params=pltpu.CompilerParams(vmem_limit_bytes=16 * 2**20),
-        cost_estimate=pl.CostEstimate(flops=0, bytes_accessed=2**20, transcendentals=0),
-    )(got, *xkvs, *xqs)
+        out_shape=[jax.ShapeDtypeStruct((COLUMNS * rows, PAIR), jnp.bfloat16) for rows in (KV_ROWS, Q_ROWS)],
+        in_specs=[VMEM],
+        out_specs=[VMEM] * 2,
+        compiler_params=pltpu.CompilerParams(vmem_limit_bytes=12 * 2**20),
+        cost_estimate=pl.CostEstimate(flops=0, bytes_accessed=2**20, transcendentals=0),
+    )(got)
+
+
+def stack_kernel(*refs):
+    out, start = refs[-1], 0
+    for ref in refs[:-1]:
+        out[start : start + ref.shape[0], :] = ref[...]
+        start += ref.shape[0]
+
+
+def stack(*pieces, flops=0):
+    return pl.pallas_call(
+        stack_kernel,
+        out_shape=jax.ShapeDtypeStruct((sum(piece.shape[0] for piece in pieces), PAIR), jnp.bfloat16),
+        in_specs=[VMEM] * len(pieces),
+        out_specs=VMEM,
+        compiler_params=pltpu.CompilerParams(vmem_limit_bytes=12 * 2**20),
+        cost_estimate=pl.CostEstimate(flops=flops, bytes_accessed=2**20, transcendentals=0),
+    )(*pieces)
 
 
 def beside_kernel(a, b, *refs):
@@ -263,7 +270,7 @@
 
 
 def beside(a, b, *after):
-    rows = (2 * a.shape[0], 3 * K_BLOCK, a.shape[0] - 3 * K_BLOCK)
+    rows = (2 * a.shape[0], a.shape[0] // 2, a.shape[0] // 2)
     return pl.pallas_call(
         beside_kernel,
         out_shape=[jax.ShapeDtypeStruct((count, PAIR), jnp.bfloat16) for count in rows],
@@ -325,11 +332,13 @@
     extra = [extra[0]] + [along("x", a, step) for a, step in zip(extra[1:], STEPS, strict=True)]
     xkv, xq = gather(extra)
     xqs = [xq] + [along("y", xq, step) for step in STEPS]
-    xkvs = [xkv] + [along_z(xkv, step) for step in STEPS]
+    xkvs = [xkv, along_z(xkv, 1), along_z(xkv, 3)]
+    xkvs.append(along_z(xkvs[1], 1))
 
     got = lax.all_to_all(sent, ("x", "y"), 0, 0, tiled=True)
-    kv, both, q, xq = sort(got, xkvs, xqs)
+    kv, q = sort(got)
     kv_next, kv_before = along_z(kv, 1), along_z(kv, 3)
+    both, xq = stack(kv, *xkvs), stack(*xqs, flops=2 * 10**10)
     other = other_core(both)
 
     rows = kv.shape[0]

time: 93.6 us -> 88.4 us (0.944)
  waiting for transfers between devices: 24.7 us -> 19.1 us
    ppermute x12, waiting for transfers between devices: 12.7 us -> 5.28 us  [along(): return lax.ppermute(a, axis, [(i, (i + step) % 4) for i in range(4)])]
    all_to_all x1, waiting for transfers between devices: 0.01 us -> 2.65 us  [local(): got = lax.all_to_all(sent, ('x', 'y'), 0, 0, tiled=True)]
    ppermute x7, starting transfers between devices: 13.3 us -> 11.5 us  [along_z(): return lax.ppermute(a, ('zl', 'zh'), pairs)]
    ppermute x12, starting transfers between devices: 18.8 us -> 20.1 us  [along(): return lax.ppermute(a, axis, [(i, (i + step) % 4) for i in range(4)])]
    all_to_all x1, starting transfers between devices: 4.02 us -> 5.03 us  [local(): lax.all_to_all(out.reshape(COLUMNS, Q_ROWS, PAIR), ('x', 'y'), 0, 0, tile...]
    ppermute x7, waiting for transfers between devices: 8.98 us -> 8.04 us  [along_z(): return lax.ppermute(a, ('zl', 'zh'), pairs)]
  transfers between devices with their start and end apart: 24 -> 24, of which waited for: 10 -> 12; matrix products, arithmetic and copies ran while one was open for 0% -> 0% of each run, Pallas kernels for 19% -> 20%
where the time goes in v2:
time: 88.4 us; the launch traced here: 88.1 us
  starting transfers between devices  43 us (49%)
  Pallas kernels  25.7 us (29%)
  waiting for transfers between devices  19.1 us (22%)
    pallas_call x4, Pallas kernels, attend(): pl.pallas_call(functools.partial(attend_kernel, len(kvs), len(after), sta...  21.1 us
    ppermute x12, starting transfers between devices, along(): return lax.ppermute(a, axis, [(i, (i + step) % 4) for i in range(4)])  20.1 us
    ppermute x7, starting transfers between devices, along_z(): return lax.ppermute(a, ('zl', 'zh'), pairs)  11.5 us
    ppermute x7, waiting for transfers between devices, along_z(): return lax.ppermute(a, ('zl', 'zh'), pairs)  8.04 us
    all_to_all x1, starting transfers between devices, local(): got = lax.all_to_all(sent, ('x', 'y'), 0, 0, tiled=True)  5.87 us
    ppermute x12, waiting for transfers between devices, along(): return lax.ppermute(a, axis, [(i, (i + step) % 4) for i in range(4)])  5.28 us
    all_to_all x1, starting transfers between devices, local(): lax.all_to_all(out.reshape(COLUMNS, Q_ROWS, PAIR), ('x', 'y'), 0, 0, tile...  5.03 us
    pallas_call x2, Pallas kernels, packed(): pl.pallas_call(kernel, out_shape=[jax.ShapeDtypeStruct(shape, jnp.bfloat1...  3.06 us
  transfers between devices with their start and end apart: 24, of which 12 were waited for; matrix products, arithmetic and copies ran while one was open for 0% of the time, Pallas kernels for 20%

profile of v2, /device:TPU:0, one launch (start us, length us, event | category | flops | bytes accessed | tf_op | source)
XLA Modules:
  0.0 88.1 jit_solution(5099578035424172446)
XLA Ops:
  0.0 1.8 %shard_map.39 = (bf16[120,256]{1,0:T(8,128)(2,1)}, bf16[120,256]{1,0:T(8,128)(2,1)}, bf16[120,256]{1,0:T(8,128)(2,1)}, bf16[120,256]{1,0:T(8,128)(2,1)}) custom-call(bf16[80,2560]{1,0:T(8,128)(2,1)} %refs_0_.3, bf16[80,2560]{1,0:T(8,128)(2,1)} %refs_1_.3, bf16[80,2560]{1,0:T(8,128)(2,1)} %refs_2_.3), custom_call_target="tpu_custom_call" | custom-call | bytes 1048576 | tf_op jit(solution)/shard_map/pallas_call | solution.py:199
  1.8 1.6 %collective-permute-start.2 = (bf16[120,256]{1,0:T(8,128)(2,1)}, bf16[120,256]{1,0:T(8,128)(2,1)S(1)}, u32[]{:S(2)}, u32[]{:S(2)}) collective-permute-start(bf16[120,256]{1,0:T(8,128)(2,1)} %get-tuple-element.31), channel_id=1, source_target_pairs={{0,32},{32,64},{64,96},{96,0},{1,33},{33,65},{65,97},{97,1},{2,34}... | collective-permute-start | bytes 184328 | tf_op jit(solution)/shard_map/ppermute | solution.py:37
  3.5 1.7 %collective-permute-start.3 = (bf16[120,256]{1,0:T(8,128)(2,1)}, bf16[120,256]{1,0:T(8,128)(2,1)S(1)}, u32[]{:S(2)}, u32[]{:S(2)}) collective-permute-start(bf16[120,256]{1,0:T(8,128)(2,1)} %get-tuple-element.32), channel_id=1, source_target_pairs={{0,96},{32,0},{64,32},{96,64},{1,97},{33,1},{65,33},{97,65},{2,98}... | collective-permute-start | bytes 184328 | tf_op jit(solution)/shard_map/ppermute | solution.py:37
  5.1 1.9 %collective-permute-start.4 = (bf16[120,256]{1,0:T(8,128)(2,1)}, bf16[120,256]{1,0:T(8,128)(2,1)S(1)}, u32[]{:S(2)}, u32[]{:S(2)}) collective-permute-start(bf16[120,256]{1,0:T(8,128)(2,1)} %get-tuple-element.33), channel_id=1, source_target_pairs={{0,64},{32,96},{64,0},{96,32},{1,65},{33,97},{65,1},{97,33},{2,66}... | collective-permute-start | bytes 184328 | tf_op jit(solution)/shard_map/ppermute | solution.py:37
  7.1 1.2 %shard_map.37 = bf16[16,120,256]{2,1,0:T(8,128)(2,1)} custom-call(bf16[80,2560]{1,0:T(8,128)(2,1)S(1)} %copy-done, bf16[80,2560]{1,0:T(8,128)(2,1)S(1)} %copy-done.1, bf16[80,2560]{1,0:T(8,128)(2,1)S(1)} %copy-done.2), custom_call_target="tpu_custom_call" | custom-call | bytes 1048576 | tf_op jit(solution)/shard_map/pallas_call | solution.py:199
  8.3 0.0 copy-start.3
  8.3 5.9 %all-to-all-start = ((bf16[16,120,256]{2,1,0:T(8,128)(2,1)}), bf16[16,120,256]{2,1,0:T(8,128)(2,1)S(1)}, u32[]{:S(2)}, u32[]{:S(2)}) async-start(bf16[16,120,256]{2,1,0:T(8,128)(2,1)} %shard_map.37), calls=%async_computation | async-start | bytes 1966080 | tf_op jit(solution)/shard_map/all_to_all | solution.py:338
  14.2 0.0 collective-permute-done.2.refs_1_
  14.2 0.0 collective-permute-done.3.refs_2_
  14.3 2.0 %collective-permute-start.5 = (bf16[320,256]{1,0:T(8,128)(2,1)S(1)}, bf16[320,256]{1,0:T(8,128)(2,1)S(1)}, u32[]{:S(2)}, u32[]{:S(2)}) collective-permute-start(bf16[320,256]{1,0:T(8,128)(2,1)S(1)} %get-tuple-element.34.refs_1_), channel_id=1, source_target_pairs={{0,16},{2,18},{16,2},{18,0},{1,17},{3,19},{17,3},{19,1},{4,20},{6,... | collective-permute-start | bytes 491528 | tf_op jit(solution)/shard_map/ppermute | solution.py:33
  16.2 2.2 %collective-permute-start.6 = (bf16[320,256]{1,0:T(8,128)(2,1)S(1)}, bf16[320,256]{1,0:T(8,128)(2,1)S(1)}, u32[]{:S(2)}, u32[]{:S(2)}) collective-permute-start(bf16[320,256]{1,0:T(8,128)(2,1)S(1)} %get-tuple-element.34.refs_1_), channel_id=1, source_target_pairs={{0,18},{2,16},{16,0},{18,2},{1,19},{3,17},{17,1},{19,3},{4,22},{6,... | collective-permute-start | bytes 491528 | tf_op jit(solution)/shard_map/ppermute | solution.py:33
  18.4 3.2 %collective-permute-done.5.refs_2_ = bf16[320,256]{1,0:T(8,128)(2,1)S(1)} collective-permute-done((bf16[320,256]{1,0:T(8,128)(2,1)S(1)}, bf16[320,256]{1,0:T(8,128)(2,1)S(1)}, u32[]{:S(2)}, u32[]{:S(2)}) %collective-permute-start.5) | collective-permute-done | bytes 163872 | tf_op jit(solution)/shard_map/ppermute | solution.py:33
  21.7 3.4 %collective-permute-start.11 = (bf16[160,256]{1,0:T(8,128)(2,1)S(1)}, bf16[160,256]{1,0:T(8,128)(2,1)S(1)}, u32[]{:S(2)}, u32[]{:S(2)}) collective-permute-start(bf16[160,256]{1,0:T(8,128)(2,1)S(1)} %get-tuple-element.36.refs_0_), channel_id=1, source_target_pairs={{0,8},{4,12},{8,0},{12,4},{1,9},{5,13},{9,1},{13,5},{2,10},{6,14},... | collective-permute-start | bytes 245768 | tf_op jit(solution)/shard_map/ppermute | solution.py:37
  25.1 1.2 %collective-permute-start.10 = (bf16[160,256]{1,0:T(8,128)(2,1)S(1)}, bf16[160,256]{1,0:T(8,128)(2,1)S(1)}, u32[]{:S(2)}, u32[]{:S(2)}) collective-permute-start(bf16[160,256]{1,0:T(8,128)(2,1)S(1)} %get-tuple-element.36.refs_0_), channel_id=1, source_target_pairs={{0,12},{4,0},{8,4},{12,8},{1,13},{5,1},{9,5},{13,9},{2,14},{6,2},{... | collective-permute-start | bytes 245768 | tf_op jit(solution)/shard_map/ppermute | solution.py:37
  26.3 0.9 collective-permute-start.9
  27.1 2.7 %all-to-all-done.got = bf16[16,120,256]{2,1,0:T(8,128)(2,1)S(1)} async-done(((bf16[16,120,256]{2,1,0:T(8,128)(2,1)}), bf16[16,120,256]{2,1,0:T(8,128)(2,1)S(1)}, u32[]{:S(2)}, u32[]{:S(2)}) %all-to-all-start) | async-done | bytes 983072 | tf_op jit(solution)/shard_map/all_to_all | solution.py:338
  29.8 0.1 shard_map.38
  29.9 0.1 shard_map.41
  30.0 0.1 collective-permute-start.8
  30.1 1.4 %collective-permute-done.11.refs_3_ = bf16[160,256]{1,0:T(8,128)(2,1)S(1)} collective-permute-done((bf16[160,256]{1,0:T(8,128)(2,1)S(1)}, bf16[160,256]{1,0:T(8,128)(2,1)S(1)}, u32[]{:S(2)}, u32[]{:S(2)}) %collective-permute-start.11) | collective-permute-done | bytes 81952 | tf_op jit(solution)/shard_map/ppermute | solution.py:37
  31.4 0.9 %collective-permute-done.9.refs_1_ = bf16[160,256]{1,0:T(8,128)(2,1)S(1)} collective-permute-done((bf16[160,256]{1,0:T(8,128)(2,1)S(1)}, bf16[160,256]{1,0:T(8,128)(2,1)S(1)}, u32[]{:S(2)}, u32[]{:S(2)}) %collective-permute-start.9) | collective-permute-done | bytes 81952 | tf_op jit(solution)/shard_map/ppermute | solution.py:37
  32.4 4.0 %collective-permute-start.1 = (bf16[1280,256]{1,0:T(8,128)(2,1)S(1)}, bf16[1280,256]{1,0:T(8,128)(2,1)S(1)}, u32[]{:S(2)}, u32[]{:S(2)}) collective-permute-start(bf16[1280,256]{1,0:T(8,128)(2,1)S(1)} %get-tuple-element.29.refs_0_.refs_1_), channel_id=1, source_target_pairs={{0,18},{2,16},{16,0},{18,2},{1,19},{3,17},{17,1},{19,3},{4,22},{6,... | collective-permute-start | bytes 1966088 | tf_op jit(solution)/shard_map/ppermute | solution.py:33
  36.4 0.1 fusion
  36.5 4.4 %shard_map.44 = (bf16[160,512]{1,0:T(8,128)(2,1)S(1)}, bf16[160,512]{1,0:T(8,128)(2,1)S(1)}, bf16[160,512]{1,0:T(8,128)(2,1)S(1)}, bf16[160,512]{1,0:T(8,128)(2,1)S(1)}) custom-call(bf16[640,256]{1,0:T(8,128)(2,1)S(1)} %shard_map.43.refs_0_, bf16[1280,256]{1,0:T(8,128)(2,1)S(1)} %slice.13.refs_1_, bf16[1280,256]{1,0:T(8,128)(2,1)S(1)} %get-tuple-element.51.refs_2_), custom_call_target="tpu_custom_call" | custom-call | flops 209715200 | bytes 1310720 | tf_op jit(solution)/shard_map/pallas_call | solution.py:122
  40.9 1.6 %collective-permute-start.12 = (bf16[160,512]{1,0:T(8,128)(2,1)S(1)}, bf16[160,512]{1,0:T(8,128)(2,1)S(1)}, u32[]{:S(2)}, u32[]{:S(2)}) collective-permute-start(bf16[160,512]{1,0:T(8,128)(2,1)S(1)} %get-tuple-element.37), channel_id=1, source_target_pairs={{0,12},{4,0},{8,4},{12,8},{1,13},{5,1},{9,5},{13,9},{2,14},{6,2},{... | collective-permute-start | bytes 491528 | tf_op jit(solution)/shard_map/ppermute | solution.py:37
  42.6 0.5 collective-permute-start.13
  43.0 1.9 %collective-permute-start.14 = (bf16[160,512]{1,0:T(8,128)(2,1)S(1)}, bf16[160,512]{1,0:T(8,128)(2,1)S(1)}, u32[]{:S(2)}, u32[]{:S(2)}) collective-permute-start(bf16[160,512]{1,0:T(8,128)(2,1)S(1)} %get-tuple-element.39), channel_id=1, source_target_pairs={{0,8},{4,12},{8,0},{12,4},{1,9},{5,13},{9,1},{13,5},{2,10},{6,14},... | collective-permute-start | bytes 491528 | tf_op jit(solution)/shard_map/ppermute | solution.py:37
  45.0 4.1 %shard_map.42 = (f32[1280,256]{1,0:T(8,128)S(1)}, f32[1280,128]{1,0:T(8,128)S(1)}) custom-call(bf16[640,256]{1,0:T(8,128)(2,1)S(1)} %get-tuple-element.28.refs_0_, bf16[1280,256]{1,0:T(8,128)(2,1)S(1)} %get-tuple-element.29.refs_0_.refs_1_, bf16[1280,256]{1,0:T(8,128)(2,1)S(1)} %get-tuple-element.52.refs_2_), custom_call_target="tpu_custom_call" | custom-call | flops 209715200 | bytes 1310720 | tf_op jit(solution)/shard_map/pallas_call | solution.py:122
  49.1 1.0 %collective-permute-done.1.b = bf16[1280,256]{1,0:T(8,128)(2,1)S(1)} collective-permute-done((bf16[1280,256]{1,0:T(8,128)(2,1)S(1)}, bf16[1280,256]{1,0:T(8,128)(2,1)S(1)}, u32[]{:S(2)}, u32[]{:S(2)}) %collective-permute-start.1) | collective-permute-done | bytes 655392 | tf_op jit(solution)/shard_map/ppermute | solution.py:33
  50.1 3.4 %collective-permute-done.a = bf16[1280,256]{1,0:T(8,128)(2,1)S(1)} collective-permute-done((bf16[1280,256]{1,0:T(8,128)(2,1)S(1)}, bf16[1280,256]{1,0:T(8,128)(2,1)S(1)}, u32[]{:S(2)}, u32[]{:S(2)}) %collective-permute-start) | collective-permute-done | bytes 655392 | tf_op jit(solution)/shard_map/ppermute | solution.py:33
  53.5 0.1 shard_map.45
  53.6 0.1 collective-permute-start.17
  53.7 0.1 collective-permute-start.15
  53.8 3.2 %collective-permute-start.16 = (bf16[640,256]{1,0:T(8,128)(2,1)S(1)}, bf16[640,256]{1,0:T(8,128)(2,1)S(1)}, u32[]{:S(2)}, u32[]{:S(2)}) collective-permute-start(bf16[640,256]{1,0:T(8,128)(2,1)S(1)} %get-tuple-element.41), channel_id=1, source_target_pairs={{0,18},{2,16},{16,0},{18,2},{1,19},{3,17},{17,1},{19,3},{4,22},{6,... | collective-permute-start | bytes 983048 | tf_op jit(solution)/shard_map/ppermute | solution.py:33
  57.0 7.6 %shard_map.46 = (f32[1280,256]{1,0:T(8,128)S(1)}, f32[1280,128]{1,0:T(8,128)S(1)}) custom-call(bf16[640,256]{1,0:T(8,128)(2,1)S(1)} %get-tuple-element.28.refs_0_, bf16[2560,256]{1,0:T(8,128)(2,1)S(1)} %get-tuple-element.42.refs_1_, bf16[2560,256]{1,0:T(8,128)(2,1)S(1)} %collective-permute-done.17.refs_2_, ...), custom_call_target="tpu_custom_call" | custom-call | flops 419430400 | bytes 2621440 | tf_op jit(solution)/shard_map/pallas_call | solution.py:122
  64.6 0.4 collective-permute-done.15.a
  65.1 0.3 collective-permute-start.18
  65.4 0.3 shard_map.48
  65.8 1.8 %collective-permute-done.18.refs_2_ = bf16[1280,256]{1,0:T(8,128)(2,1)S(1)} collective-permute-done((bf16[1280,256]{1,0:T(8,128)(2,1)S(1)}, bf16[1280,256]{1,0:T(8,128)(2,1)S(1)}, u32[]{:S(2)}, u32[]{:S(2)}) %collective-permute-start.18) | collective-permute-done | bytes 655392 | tf_op jit(solution)/shard_map/ppermute | solution.py:41
  67.5 4.9 %shard_map.49 = bf16[640,256]{1,0:T(8,128)(2,1)} custom-call(bf16[640,256]{1,0:T(8,128)(2,1)S(1)} %get-tuple-element.28.refs_0_, bf16[1280,256]{1,0:T(8,128)(2,1)S(1)} %shard_map.47.refs_1_, bf16[1280,256]{1,0:T(8,128)(2,1)S(1)} %collective-permute-done.18.refs_2_, f32[1280,256]{1,0:T(8,128)S(1)} %get-tuple-element.44.after.refs_3_, ...), custom_call_target="tpu_custom_call" | custom-call | flops 209715200 | bytes 1310720 | tf_op jit(solution)/shard_map/pallas_call | solution.py:122
  72.5 5.0 %all-to-all-start.1 = ((bf16[16,40,256]{2,1,0:T(8,128)(2,1)}), bf16[16,40,256]{2,1,0:T(8,128)(2,1)S(1)}, u32[]{:S(2)}, u32[]{:S(2)}) async-start(bf16[16,40,256]{2,1,0:T(8,128)(2,1)} %bitcast), calls=%async_computation.1 | async-start | bytes 655360 | tf_op jit(solution)/shard_map/all_to_all | solution.py:355
  77.5 3.1 %collective-permute-start.19 = (bf16[40,256]{1,0:T(8,128)(2,1)S(1)}, bf16[40,256]{1,0:T(8,128)(2,1)S(1)}, u32[]{:S(2)}, u32[]{:S(2)}) collective-permute-start(bf16[40,256]{1,0:T(8,128)(2,1)S(1)} %get-tuple-element.48), channel_id=1, source_target_pairs={{0,96},{32,0},{64,32},{96,64},{1,97},{33,1},{65,33},{97,65},{2,98}... | collective-permute-start | bytes 61448 | tf_op jit(solution)/shard_map/ppermute | solution.py:37
  80.7 2.3 %collective-permute-start.21 = (bf16[40,256]{1,0:T(8,128)(2,1)S(1)}, bf16[40,256]{1,0:T(8,128)(2,1)S(1)}, u32[]{:S(2)}, u32[]{:S(2)}) collective-permute-start(bf16[40,256]{1,0:T(8,128)(2,1)S(1)} %get-tuple-element.50), channel_id=1, source_target_pairs={{0,64},{32,96},{64,0},{96,32},{1,65},{33,97},{65,1},{97,33},{2,66}... | collective-permute-start | bytes 61448 | tf_op jit(solution)/shard_map/ppermute | solution.py:37
  83.0 1.0 %collective-permute-done.19.refs_1_ = bf16[40,256]{1,0:T(8,128)(2,1)S(1)} collective-permute-done((bf16[40,256]{1,0:T(8,128)(2,1)S(1)}, bf16[40,256]{1,0:T(8,128)(2,1)S(1)}, u32[]{:S(2)}, u32[]{:S(2)}) %collective-permute-start.19) | collective-permute-done | bytes 20512 | tf_op jit(solution)/shard_map/ppermute | solution.py:37
  84.0 1.7 %collective-permute-done.20.refs_2_ = bf16[40,256]{1,0:T(8,128)(2,1)S(1)} collective-permute-done((bf16[40,256]{1,0:T(8,128)(2,1)S(1)}, bf16[40,256]{1,0:T(8,128)(2,1)S(1)}, u32[]{:S(2)}, u32[]{:S(2)}) %collective-permute-start.20) | collective-permute-done | bytes 20512 | tf_op jit(solution)/shard_map/ppermute | solution.py:37
  85.7 0.2 collective-permute-done.21.refs_3_
  86.0 1.3 %all-to-all-done.1.main = bf16[16,40,256]{2,1,0:T(8,128)(2,1)S(1)} async-done(((bf16[16,40,256]{2,1,0:T(8,128)(2,1)}), bf16[16,40,256]{2,1,0:T(8,128)(2,1)S(1)}, u32[]{:S(2)}, u32[]{:S(2)}) %all-to-all-start.1) | async-done | bytes 327712 | tf_op jit(solution)/shard_map/all_to_all | solution.py:355
  87.3 0.8 shard_map.50
  (24 shorter events, 0.2 us)
Async XLA Ops:
  0.0 7.0 %copy-start.2 = (bf16[80,2560]{1,0:T(8,128)(2,1)S(1)}, bf16[80,2560]{1,0:T(8,128)(2,1)}, u32[]{:S(2)}) copy-start(bf16[80,2560]{1,0:T(8,128)(2,1)} %refs_2_.3) | copy-start | bytes 1228804
  0.0 7.0 %copy-start.1 = (bf16[80,2560]{1,0:T(8,128)(2,1)S(1)}, bf16[80,2560]{1,0:T(8,128)(2,1)}, u32[]{:S(2)}) copy-start(bf16[80,2560]{1,0:T(8,128)(2,1)} %refs_1_.3) | copy-start | bytes 1228804
  0.0 7.0 %copy-start = (bf16[80,2560]{1,0:T(8,128)(2,1)S(1)}, bf16[80,2560]{1,0:T(8,128)(2,1)}, u32[]{:S(2)}) copy-start(bf16[80,2560]{1,0:T(8,128)(2,1)} %refs_0_.3) | copy-start | bytes 1228804
  1.8 12.4 %collective-permute-start.2 = (bf16[120,256]{1,0:T(8,128)(2,1)}, bf16[120,256]{1,0:T(8,128)(2,1)S(1)}, u32[]{:S(2)}, u32[]{:S(2)}) collective-permute-start(bf16[120,256]{1,0:T(8,128)(2,1)} %get-tuple-element.31), channel_id=1, source_target_pairs={{0,32},{32,64},{64,96},{96,0},{1,33},{33,65},{65,97},{97,1},{2,34}... | collective-permute-start | bytes 184328 | tf_op jit(solution)/shard_map/ppermute | solution.py:37
  3.5 10.7 %collective-permute-start.3 = (bf16[120,256]{1,0:T(8,128)(2,1)}, bf16[120,256]{1,0:T(8,128)(2,1)S(1)}, u32[]{:S(2)}, u32[]{:S(2)}) collective-permute-start(bf16[120,256]{1,0:T(8,128)(2,1)} %get-tuple-element.32), channel_id=1, source_target_pairs={{0,96},{32,0},{64,32},{96,64},{1,97},{33,1},{65,33},{97,65},{2,98}... | collective-permute-start | bytes 184328 | tf_op jit(solution)/shard_map/ppermute | solution.py:37
  5.1 9.1 %collective-permute-start.4 = (bf16[120,256]{1,0:T(8,128)(2,1)}, bf16[120,256]{1,0:T(8,128)(2,1)S(1)}, u32[]{:S(2)}, u32[]{:S(2)}) collective-permute-start(bf16[120,256]{1,0:T(8,128)(2,1)} %get-tuple-element.33), channel_id=1, source_target_pairs={{0,64},{32,96},{64,0},{96,32},{1,65},{33,97},{65,1},{97,33},{2,66}... | collective-permute-start | bytes 184328 | tf_op jit(solution)/shard_map/ppermute | solution.py:37
  8.3 5.9 %copy-start.3 = (bf16[120,256]{1,0:T(8,128)(2,1)S(1)}, bf16[120,256]{1,0:T(8,128)(2,1)}, u32[]{:S(2)}) copy-start(bf16[120,256]{1,0:T(8,128)(2,1)} %get-tuple-element.30.refs_0_) | copy-start | bytes 184324
  8.3 21.5 %all-to-all-start = ((bf16[16,120,256]{2,1,0:T(8,128)(2,1)}), bf16[16,120,256]{2,1,0:T(8,128)(2,1)S(1)}, u32[]{:S(2)}, u32[]{:S(2)}) async-start(bf16[16,120,256]{2,1,0:T(8,128)(2,1)} %shard_map.37), calls=%async_computation | async-start | bytes 1966080 | tf_op jit(solution)/shard_map/all_to_all | solution.py:338
  14.3 7.4 %collective-permute-start.5 = (bf16[320,256]{1,0:T(8,128)(2,1)S(1)}, bf16[320,256]{1,0:T(8,128)(2,1)S(1)}, u32[]{:S(2)}, u32[]{:S(2)}) collective-permute-start(bf16[320,256]{1,0:T(8,128)(2,1)S(1)} %get-tuple-element.34.refs_1_), channel_id=1, source_target_pairs={{0,16},{2,18},{16,2},{18,0},{1,17},{3,19},{17,3},{19,1},{4,20},{6,... | collective-permute-start | bytes 491528 | tf_op jit(solution)/shard_map/ppermute | solution.py:33
  16.2 13.6 %collective-permute-start.6 = (bf16[320,256]{1,0:T(8,128)(2,1)S(1)}, bf16[320,256]{1,0:T(8,128)(2,1)S(1)}, u32[]{:S(2)}, u32[]{:S(2)}) collective-permute-start(bf16[320,256]{1,0:T(8,128)(2,1)S(1)} %get-tuple-element.34.refs_1_), channel_id=1, source_target_pairs={{0,18},{2,16},{16,0},{18,2},{1,19},{3,17},{17,1},{19,3},{4,22},{6,... | collective-permute-start | bytes 491528 | tf_op jit(solution)/shard_map/ppermute | solution.py:33
  21.7 8.2 %collective-permute-start.7 = (bf16[320,256]{1,0:T(8,128)(2,1)S(1)}, bf16[320,256]{1,0:T(8,128)(2,1)S(1)}, u32[]{:S(2)}, u32[]{:S(2)}) collective-permute-start(bf16[320,256]{1,0:T(8,128)(2,1)S(1)} %collective-permute-done.5.refs_2_), channel_id=1, source_target_pairs={{0,16},{2,18},{16,2},{18,0},{1,17},{3,19},{17,3},{19,1},{4,20},{6,... | collective-permute-start | bytes 491528 | tf_op jit(solution)/shard_map/ppermute | solution.py:33
  21.7 9.7 %collective-permute-start.11 = (bf16[160,256]{1,0:T(8,128)(2,1)S(1)}, bf16[160,256]{1,0:T(8,128)(2,1)S(1)}, u32[]{:S(2)}, u32[]{:S(2)}) collective-permute-start(bf16[160,256]{1,0:T(8,128)(2,1)S(1)} %get-tuple-element.36.refs_0_), channel_id=1, source_target_pairs={{0,8},{4,12},{8,0},{12,4},{1,9},{5,13},{9,1},{13,5},{2,10},{6,14},... | collective-permute-start | bytes 245768 | tf_op jit(solution)/shard_map/ppermute | solution.py:37
  25.1 6.3 %collective-permute-start.10 = (bf16[160,256]{1,0:T(8,128)(2,1)S(1)}, bf16[160,256]{1,0:T(8,128)(2,1)S(1)}, u32[]{:S(2)}, u32[]{:S(2)}) collective-permute-start(bf16[160,256]{1,0:T(8,128)(2,1)S(1)} %get-tuple-element.36.refs_0_), channel_id=1, source_target_pairs={{0,12},{4,0},{8,4},{12,8},{1,13},{5,1},{9,5},{13,9},{2,14},{6,2},{... | collective-permute-start | bytes 245768 | tf_op jit(solution)/shard_map/ppermute | solution.py:37
  26.3 6.1 %collective-permute-start.9 = (bf16[160,256]{1,0:T(8,128)(2,1)S(1)}, bf16[160,256]{1,0:T(8,128)(2,1)S(1)}, u32[]{:S(2)}, u32[]{:S(2)}) collective-permute-start(bf16[160,256]{1,0:T(8,128)(2,1)S(1)} %get-tuple-element.36.refs_0_), channel_id=1, source_target_pairs={{0,4},{4,8},{8,12},{12,0},{1,5},{5,9},{9,13},{13,1},{2,6},{6,10},{... | collective-permute-start | bytes 245768 | tf_op jit(solution)/shard_map/ppermute | solution.py:37
  30.0 6.5 %collective-permute-start.8 = (bf16[2560,256]{1,0:T(8,128)(2,1)S(1)}, bf16[2560,256]{1,0:T(8,128)(2,1)S(1)}, u32[]{:S(2)}, u32[]{:S(2)}) collective-permute-start(bf16[2560,256]{1,0:T(8,128)(2,1)S(1)} %shard_map.41), channel_id=1, source_target_pairs={{0,1},{1,0},{2,3},{3,2},{4,5},{5,4},{6,7},{7,6},{8,9},{9,8},{10,11... | collective-permute-start | bytes 3932168 | tf_op jit(solution)/shard_map/ppermute | solution.py:41
  32.4 17.7 %collective-permute-start.1 = (bf16[1280,256]{1,0:T(8,128)(2,1)S(1)}, bf16[1280,256]{1,0:T(8,128)(2,1)S(1)}, u32[]{:S(2)}, u32[]{:S(2)}) collective-permute-start(bf16[1280,256]{1,0:T(8,128)(2,1)S(1)} %get-tuple-element.29.refs_0_.refs_1_), channel_id=1, source_target_pairs={{0,18},{2,16},{16,0},{18,2},{1,19},{3,17},{17,1},{19,3},{4,22},{6,... | collective-permute-start | bytes 1966088 | tf_op jit(solution)/shard_map/ppermute | solution.py:33
  36.4 17.1 %collective-permute-start = (bf16[1280,256]{1,0:T(8,128)(2,1)S(1)}, bf16[1280,256]{1,0:T(8,128)(2,1)S(1)}, u32[]{:S(2)}, u32[]{:S(2)}) collective-permute-start(bf16[1280,256]{1,0:T(8,128)(2,1)S(1)} %get-tuple-element.29.refs_0_.refs_1_), channel_id=1, source_target_pairs={{0,16},{2,18},{16,2},{18,0},{1,17},{3,19},{17,3},{19,1},{4,20},{6,... | collective-permute-start | bytes 1966088 | tf_op jit(solution)/shard_map/ppermute | solution.py:33
  40.9 12.6 %collective-permute-start.12 = (bf16[160,512]{1,0:T(8,128)(2,1)S(1)}, bf16[160,512]{1,0:T(8,128)(2,1)S(1)}, u32[]{:S(2)}, u32[]{:S(2)}) collective-permute-start(bf16[160,512]{1,0:T(8,128)(2,1)S(1)} %get-tuple-element.37), channel_id=1, source_target_pairs={{0,12},{4,0},{8,4},{12,8},{1,13},{5,1},{9,5},{13,9},{2,14},{6,2},{... | collective-permute-start | bytes 491528 | tf_op jit(solution)/shard_map/ppermute | solution.py:37
  42.6 10.9 %collective-permute-start.13 = (bf16[160,512]{1,0:T(8,128)(2,1)S(1)}, bf16[160,512]{1,0:T(8,128)(2,1)S(1)}, u32[]{:S(2)}, u32[]{:S(2)}) collective-permute-start(bf16[160,512]{1,0:T(8,128)(2,1)S(1)} %get-tuple-element.38), channel_id=1, source_target_pairs={{0,4},{4,8},{8,12},{12,0},{1,5},{5,9},{9,13},{13,1},{2,6},{6,10},{... | collective-permute-start | bytes 491528 | tf_op jit(solution)/shard_map/ppermute | solution.py:37
  43.0 10.5 %collective-permute-start.14 = (bf16[160,512]{1,0:T(8,128)(2,1)S(1)}, bf16[160,512]{1,0:T(8,128)(2,1)S(1)}, u32[]{:S(2)}, u32[]{:S(2)}) collective-permute-start(bf16[160,512]{1,0:T(8,128)(2,1)S(1)} %get-tuple-element.39), channel_id=1, source_target_pairs={{0,8},{4,12},{8,0},{12,4},{1,9},{5,13},{9,1},{13,5},{2,10},{6,14},... | collective-permute-start | bytes 491528 | tf_op jit(solution)/shard_map/ppermute | solution.py:37
  53.6 3.4 %collective-permute-start.17 = (bf16[2560,256]{1,0:T(8,128)(2,1)S(1)}, bf16[2560,256]{1,0:T(8,128)(2,1)S(1)}, u32[]{:S(2)}, u32[]{:S(2)}) collective-permute-start(bf16[2560,256]{1,0:T(8,128)(2,1)S(1)} %get-tuple-element.42.refs_1_), channel_id=1, source_target_pairs={{0,1},{1,0},{2,3},{3,2},{4,5},{5,4},{6,7},{7,6},{8,9},{9,8},{10,11... | collective-permute-start | bytes 3932168 | tf_op jit(solution)/shard_map/ppermute | solution.py:41
  53.7 11.3 %collective-permute-start.15 = (bf16[640,256]{1,0:T(8,128)(2,1)S(1)}, bf16[640,256]{1,0:T(8,128)(2,1)S(1)}, u32[]{:S(2)}, u32[]{:S(2)}) collective-permute-start(bf16[640,256]{1,0:T(8,128)(2,1)S(1)} %get-tuple-element.40), channel_id=1, source_target_pairs={{0,16},{2,18},{16,2},{18,0},{1,17},{3,19},{17,3},{19,1},{4,20},{6,... | collective-permute-start | bytes 983048 | tf_op jit(solution)/shard_map/ppermute | solution.py:33
  53.8 11.3 %collective-permute-start.16 = (bf16[640,256]{1,0:T(8,128)(2,1)S(1)}, bf16[640,256]{1,0:T(8,128)(2,1)S(1)}, u32[]{:S(2)}, u32[]{:S(2)}) collective-permute-start(bf16[640,256]{1,0:T(8,128)(2,1)S(1)} %get-tuple-element.41), channel_id=1, source_target_pairs={{0,18},{2,16},{16,0},{18,2},{1,19},{3,17},{17,1},{19,3},{4,22},{6,... | collective-permute-start | bytes 983048 | tf_op jit(solution)/shard_map/ppermute | solution.py:33
  65.1 2.4 %collective-permute-start.18 = (bf16[1280,256]{1,0:T(8,128)(2,1)S(1)}, bf16[1280,256]{1,0:T(8,128)(2,1)S(1)}, u32[]{:S(2)}, u32[]{:S(2)}) collective-permute-start(bf16[1280,256]{1,0:T(8,128)(2,1)S(1)} %shard_map.47.refs_1_), channel_id=1, source_target_pairs={{0,1},{1,0},{2,3},{3,2},{4,5},{5,4},{6,7},{7,6},{8,9},{9,8},{10,11... | collective-permute-start | bytes 1966088 | tf_op jit(solution)/shard_map/ppermute | solution.py:41
  72.5 14.8 %all-to-all-start.1 = ((bf16[16,40,256]{2,1,0:T(8,128)(2,1)}), bf16[16,40,256]{2,1,0:T(8,128)(2,1)S(1)}, u32[]{:S(2)}, u32[]{:S(2)}) async-start(bf16[16,40,256]{2,1,0:T(8,128)(2,1)} %bitcast), calls=%async_computation.1 | async-start | bytes 655360 | tf_op jit(solution)/shard_map/all_to_all | solution.py:355
  77.5 6.5 %collective-permute-start.19 = (bf16[40,256]{1,0:T(8,128)(2,1)S(1)}, bf16[40,256]{1,0:T(8,128)(2,1)S(1)}, u32[]{:S(2)}, u32[]{:S(2)}) collective-permute-start(bf16[40,256]{1,0:T(8,128)(2,1)S(1)} %get-tuple-element.48), channel_id=1, source_target_pairs={{0,96},{32,0},{64,32},{96,64},{1,97},{33,1},{65,33},{97,65},{2,98}... | collective-permute-start | bytes 61448 | tf_op jit(solution)/shard_map/ppermute | solution.py:37
  80.6 5.1 %collective-permute-start.20 = (bf16[40,256]{1,0:T(8,128)(2,1)S(1)}, bf16[40,256]{1,0:T(8,128)(2,1)S(1)}, u32[]{:S(2)}, u32[]{:S(2)}) collective-permute-start(bf16[40,256]{1,0:T(8,128)(2,1)S(1)} %get-tuple-element.49), channel_id=1, source_target_pairs={{0,32},{32,64},{64,96},{96,0},{1,33},{33,65},{65,97},{97,1},{2,34}... | collective-permute-start | bytes 61448 | tf_op jit(solution)/shard_map/ppermute | solution.py:37
  80.7 5.3 %collective-permute-start.21 = (bf16[40,256]{1,0:T(8,128)(2,1)S(1)}, bf16[40,256]{1,0:T(8,128)(2,1)S(1)}, u32[]{:S(2)}, u32[]{:S(2)}) collective-permute-start(bf16[40,256]{1,0:T(8,128)(2,1)S(1)} %get-tuple-element.50), channel_id=1, source_target_pairs={{0,64},{32,96},{64,0},{96,32},{1,65},{33,97},{65,1},{97,33},{2,66}... | collective-permute-start | bytes 61448 | tf_op jit(solution)/shard_map/ppermute | solution.py:37

commit v3 on v2

--- a/solution.py
+++ b/solution.py
@@ -17,6 +17,7 @@
 TOKENS = 80
 EXTRA = HEADS - COLUMNS
 K_BLOCK = 256
+CODE_ROWS = 16
 STEPS = (1, 3, 2)
 NT = (((1,), (1,)), ((), ()))
 KV_ROWS, Q_ROWS = TOKENS, TOKENS // 2
@@ -37,6 +38,14 @@
     return lax.ppermute(a, axis, [(i, (i + step) % 4) for i in range(4)])
 
 
+def key_partner(a):
+    return lax.ppermute(a, "zl", [(0, 1), (1, 0)])
+
+
+def query_partner(a):
+    return lax.ppermute(a, ("zl", "zh"), [(0, 3), (3, 0), (1, 2), (2, 1)])
+
+
 def other_core(a):
     return lax.ppermute(a, "c", [(0, 1), (1, 0)])
 
@@ -46,6 +55,32 @@
     high = full.astype(jnp.bfloat16)
     low = (full - high.astype(jnp.float32)).astype(jnp.bfloat16)
     return jnp.concatenate([high, low], axis=1)
+
+
+def diagonal():
+    shape = (HEAD_DIM, HEAD_DIM)
+    return lax.broadcasted_iota(jnp.int32, shape, 0) == lax.broadcasted_iota(jnp.int32, shape, 1)
+
+
+def coded_rows(level):
+    blocks = level.shape[0] // HEAD_DIM
+    row = lax.broadcasted_iota(jnp.int32, (CODE_ROWS, HEAD_DIM), 0)
+    coded = jnp.zeros((CODE_ROWS, HEAD_DIM), jnp.float32)
+    for i in range(blocks):
+        block = jnp.where(diagonal(), level[i * HEAD_DIM : (i + 1) * HEAD_DIM, :], 0.0)
+        rest = jnp.sum(block, axis=0, keepdims=True)
+        for term in range(3):
+            rounded = rest.astype(jnp.bfloat16).astype(jnp.float32)
+            coded = jnp.where(row == term * blocks + i, rounded, coded)
+            rest = rest - rounded
+    return coded
+
+
+def decoded_column(coded, i, blocks):
+    row = lax.broadcasted_iota(jnp.int32, coded.shape, 0)
+    mine = (row == i) | (row == blocks + i) | (row == 2 * blocks + i)
+    numbers = jnp.sum(jnp.where(mine, coded, 0.0), axis=0, keepdims=True)
+    return jnp.sum(jnp.where(diagonal(), numbers, 0.0), axis=1, keepdims=True)
 
 
 def attend_kernel(n_kv, n_after, first, last, *refs):
@@ -81,32 +116,24 @@
                     weights, jnp.concatenate([v, ones], axis=1), preferred_element_type=jnp.float32
                 )
                 top = fresh
-        if last == "out":
-            refs[0][:, lanes] = (acc[:, :HEAD_DIM] / acc[:, HEAD_DIM:]).astype(jnp.bfloat16)
+        if last == "send":
+            total = acc[:, HEAD_DIM:]
+            refs[0][:rows, lanes] = (acc[:, :HEAD_DIM] / total).astype(jnp.bfloat16)
+            refs[0][rows:, lanes] = coded_rows(top + jnp.log2(total)).astype(jnp.bfloat16)
         elif last == "part":
             total = acc[:, HEAD_DIM:]
             part = (acc[:, :HEAD_DIM] / total).astype(jnp.bfloat16)
-            level = top + jnp.log2(total)
-            high = level.astype(jnp.bfloat16)
-            rest = level - high.astype(jnp.float32)
-            middle = rest.astype(jnp.bfloat16)
-            low = (rest - middle.astype(jnp.float32)).astype(jnp.bfloat16)
-            lane = lax.broadcasted_iota(jnp.int32, level.shape, 1)
-            zero = jnp.zeros_like(level)
-            coded = jnp.where(lane == 0, high.astype(jnp.float32), zero)
-            coded = jnp.where(lane == 1, middle.astype(jnp.float32), coded)
-            coded = jnp.where(lane == 2, low.astype(jnp.float32), coded)
-            coded = coded.astype(jnp.bfloat16)
+            coded = coded_rows(top + jnp.log2(total)).astype(jnp.bfloat16)
+            some = rows // 4
             for i, ref in enumerate(refs):
-                some = slice(i * ref.shape[0], (i + 1) * ref.shape[0])
-                ref[:, lanes] = part[some, :]
-                ref[:, PAIR + half * HEAD_DIM : PAIR + (half + 1) * HEAD_DIM] = coded[some, :]
+                ref[:some, lanes] = part[i * some : (i + 1) * some, :]
+                ref[some:, lanes] = coded
         else:
             refs[0][here, :] = acc
             refs[1][here, :] = jnp.broadcast_to(top, (rows, HEAD_DIM))
 
 
-def attend(q, kvs, state, last, after=()):
+def attend(q, kvs, state, last, after=(), flops=0):
     rows = q.shape[0]
     keys = sum(kv.shape[0] for kv in kvs)
     if last is None:
@@ -115,9 +142,9 @@
             jax.ShapeDtypeStruct((2 * rows, HEAD_DIM), jnp.float32),
         )
     elif last == "part":
-        out_shape = (jax.ShapeDtypeStruct((rows // 4, 2 * PAIR), jnp.bfloat16),) * 4
+        out_shape = (jax.ShapeDtypeStruct((rows // 4 + CODE_ROWS, PAIR), jnp.bfloat16),) * 4
     else:
-        out_shape = (jax.ShapeDtypeStruct((rows, PAIR), jnp.bfloat16),)
+        out_shape = (jax.ShapeDtypeStruct((rows + CODE_ROWS, PAIR), jnp.bfloat16),)
     args = (q, *kvs, *(state or ()))
     result = pl.pallas_call(
         functools.partial(attend_kernel, len(kvs), len(after), state is None, last),
@@ -126,23 +153,29 @@
         out_specs=(VMEM,) * len(out_shape),
         compiler_params=pltpu.CompilerParams(vmem_limit_bytes=20 * 2**20),
         cost_estimate=pl.CostEstimate(
-            flops=rows * keys * HEAD_DIM, bytes_accessed=4 * keys * HEAD_DIM, transcendentals=0
+            flops=flops, bytes_accessed=4 * keys * HEAD_DIM, transcendentals=0
         ),
     )(*args, *after)
-    return result[0] if last == "out" else result
+    return result[0] if last == "send" else result
 
 
 def combine_kernel(*refs):
     parts, outs = refs[:4], refs[4:]
+    rows = parts[0].shape[0] - CODE_ROWS
+    blocks = 4 * rows // HEAD_DIM
     for half in range(2):
         lanes = slice(half * HEAD_DIM, (half + 1) * HEAD_DIM)
-        coded = slice(PAIR + half * HEAD_DIM, PAIR + (half + 1) * HEAD_DIM)
-        levels = [jnp.sum(p[:, coded].astype(jnp.float32), axis=1, keepdims=True) for p in parts]
+        levels = []
+        for i, part in enumerate(parts):
+            first, start = divmod(i * rows, HEAD_DIM)
+            coded = part[rows:, lanes].astype(jnp.float32)
+            column = jnp.concatenate([decoded_column(coded, first + j, blocks) for j in range(2)], axis=0)
+            levels.append(column[start : start + rows, :])
         top = functools.reduce(jnp.maximum, levels)
         shares = [jnp.exp2(level - top) for level in levels]
         total = functools.reduce(jnp.add, shares)
         summed = functools.reduce(
-            jnp.add, [share * p[:, lanes].astype(jnp.float32) for share, p in zip(shares, parts, strict=True)]
+            jnp.add, [share * p[:rows, lanes].astype(jnp.float32) for share, p in zip(shares, parts, strict=True)]
         )
         whole = (summed / total).astype(jnp.bfloat16)
         for i, out in enumerate(outs):
@@ -260,41 +293,48 @@
     )(*pieces)
 
 
-def beside_kernel(a, b, *refs):
-    both, first, second = refs[-3:]
-    rows = a.shape[0]
-    both[:rows, :] = a[...]
-    both[rows:, :] = b[...]
-    first[...] = a[: first.shape[0], :]
-    second[...] = b[first.shape[0] :, :]
-
-
-def beside(a, b, *after):
-    rows = (2 * a.shape[0], a.shape[0] // 2, a.shape[0] // 2)
-    return pl.pallas_call(
-        beside_kernel,
-        out_shape=[jax.ShapeDtypeStruct((count, PAIR), jnp.bfloat16) for count in rows],
-        in_specs=[VMEM, VMEM] + [HBM] * len(after),
-        out_specs=[VMEM] * 3,
+def hold_kernel(a, *refs):
+    refs[-1][...] = a[...]
+
+
+def hold(a, *after):
+    return pl.pallas_call(
+        hold_kernel,
+        out_shape=jax.ShapeDtypeStruct(a.shape, a.dtype),
+        in_specs=[VMEM] + [HBM] * len(after),
+        out_specs=VMEM,
         compiler_params=pltpu.CompilerParams(vmem_limit_bytes=12 * 2**20),
         cost_estimate=pl.CostEstimate(flops=0, bytes_accessed=2**20, transcendentals=0),
-    )(a, b, *after)
-
-
-def join_kernel(a, b, after, out):
-    out[: a.shape[0], :] = a[...]
-    out[a.shape[0] :, :] = b[...]
-
-
-def join(a, b, after):
-    return pl.pallas_call(
-        join_kernel,
-        out_shape=jax.ShapeDtypeStruct((a.shape[0] + b.shape[0], PAIR), jnp.bfloat16),
-        in_specs=[VMEM, VMEM, HBM],
+    )(a, *after)
+
+
+def merge_kernel(acc, top, sent, out):
+    rows = out.shape[0]
+    blocks = rows // HEAD_DIM
+    for half in range(2):
+        lanes = slice(half * HEAD_DIM, (half + 1) * HEAD_DIM)
+        coded = sent[rows:, lanes].astype(jnp.float32)
+        for i in range(blocks):
+            there = slice(i * HEAD_DIM, (i + 1) * HEAD_DIM)
+            here = slice(half * rows + i * HEAD_DIM, half * rows + (i + 1) * HEAD_DIM)
+            total = acc[here, HEAD_DIM:]
+            level = top[here, :] + jnp.log2(total)
+            other = decoded_column(coded, i, blocks)
+            largest = jnp.maximum(level, other)
+            share, other = jnp.exp2(level - largest), jnp.exp2(other - largest)
+            summed = acc[here, :HEAD_DIM] / total * share + sent[there, lanes].astype(jnp.float32) * other
+            out[there, lanes] = (summed / (share + other)).astype(jnp.bfloat16)
+
+
+def merge(acc, top, sent):
+    return pl.pallas_call(
+        merge_kernel,
+        out_shape=jax.ShapeDtypeStruct((acc.shape[0] // 2, PAIR), jnp.bfloat16),
+        in_specs=[VMEM] * 3,
         out_specs=VMEM,
-        compiler_params=pltpu.CompilerParams(vmem_limit_bytes=8 * 2**20),
+        compiler_params=pltpu.CompilerParams(vmem_limit_bytes=12 * 2**20),
         cost_estimate=pl.CostEstimate(flops=0, bytes_accessed=2**20, transcendentals=0),
-    )(a, b, after)
+    )(acc, top, sent)
 
 
 def unpack_kernel(main, *refs):
@@ -337,21 +377,22 @@
 
     got = lax.all_to_all(sent, ("x", "y"), 0, 0, tiled=True)
     kv, q = sort(got)
-    kv_next, kv_before = along_z(kv, 1), along_z(kv, 3)
+    near = key_partner(kv)
+    near_q = query_partner(q)
     both, xq = stack(kv, *xkvs), stack(*xqs, flops=2 * 10**10)
     other = other_core(both)
 
     rows = kv.shape[0]
     parts = attend(xq, [both[rows:], other[rows:]], None, "part")
     back = [along("y", part, -step) for part, step in zip(parts[1:], STEPS, strict=True)]
-    state = attend(q, [kv, other[:rows]], None, None)
     xout = combine([parts[0], *back])
 
-    near, first, second = beside(kv_next, kv_before, state[0], *back)
-    first, second = along_z(first, 1), along_z(second, 3)
-    state = attend(q, [near, other_core(near)], state, None)
-    across = join(first, second, state[0])
-    out = attend(q, [across, other_core(across)], state, "out", xout[:1])
+    near = hold(near, parts[0])
+    near_other = other_core(near)
+    state = attend(near_q, [kv, other[:rows]], None, None, (near,), flops=2 * 10**10)
+    sent = attend(near_q, [near, near_other], state, "send", back)
+    state = attend(q, [kv, other[:rows], near, near_other], None, None, (sent, xout[0]))
+    out = merge(*state, query_partner(sent))
     out = lax.all_to_all(out.reshape(COLUMNS, Q_ROWS, PAIR), ("x", "y"), 0, 0, tiled=True)
     xout = [xout[0]] + [along("x", a, -step) for a, step in zip(xout[1:], STEPS, strict=True)]
     return unpack(out, xout)

time: 88.4 us -> 82.6 us (0.934)
  waiting for transfers between devices: 19.1 us -> 10.7 us
  starting transfers between devices: 43 us -> 44.8 us
    ppermute x0 -> x3, starting transfers between devices: none -> 9.8 us  [the longest x2 7.81 us: query_partner(): return lax.ppermute(a, ('zl', 'zh'), [(0, 3), (3, 0), (1, 2), (2, 1)])]
    ppermute x7 -> x3, starting transfers between devices: 11.5 us -> 4.19 us  [along_z(): return lax.ppermute(a, ('zl', 'zh'), pairs)]
    ppermute x7 -> x3, waiting for transfers between devices: 8.04 us -> 3.22 us  [along_z(): return lax.ppermute(a, ('zl', 'zh'), pairs)]
    ppermute x12, waiting for transfers between devices: 5.28 us -> 3.3 us  [along(): return lax.ppermute(a, axis, [(i, (i + step) % 4) for i in range(4)])]
    ppermute x3 -> x2, waiting for transfers between devices: 1.77 us -> 0.01 us  [other_core(): return lax.ppermute(a, 'c', [(0, 1), (1, 0)])]
    pallas_call x2, Pallas kernels: 0.17 us -> 1.28 us  [the longest x1 1.24 us: merge(): pl.pallas_call(merge_kernel, out_shape=jax.ShapeDtypeStruct((acc.shape[0]...]
  transfers between devices with their start and end apart: 24 -> 22, of which waited for: 12 -> 8; matrix products, arithmetic and copies ran while one was open for 0% -> 0% of each run, Pallas kernels for 20% -> 22%
where the time goes in v3:
time: 82.6 us; the launch traced here: 82.3 us
  starting transfers between devices  44.8 us (54%)
  Pallas kernels  26.5 us (32%)
  waiting for transfers between devices  10.7 us (13%)
    pallas_call x4, Pallas kernels, attend(): pl.pallas_call(functools.partial(attend_kernel, len(kvs), len(after), sta...  20.6 us
    ppermute x12, starting transfers between devices, along(): return lax.ppermute(a, axis, [(i, (i + step) % 4) for i in range(4)])  20.1 us
    ppermute x2, starting transfers between devices, query_partner(): return lax.ppermute(a, ('zl', 'zh'), [(0, 3), (3, 0), (1, 2), (2, 1)])  7.81 us
    all_to_all x1, starting transfers between devices, local(): got = lax.all_to_all(sent, ('x', 'y'), 0, 0, tiled=True)  5.87 us
    all_to_all x1, starting transfers between devices, local(): lax.all_to_all(out.reshape(COLUMNS, Q_ROWS, PAIR), ('x', 'y'), 0, 0, tile...  4.41 us
    ppermute x3, starting transfers between devices, along_z(): return lax.ppermute(a, ('zl', 'zh'), pairs)  4.19 us
    ppermute x12, waiting for transfers between devices, along(): return lax.ppermute(a, axis, [(i, (i + step) % 4) for i in range(4)])  3.3 us
    ppermute x3, waiting for transfers between devices, along_z(): return lax.ppermute(a, ('zl', 'zh'), pairs)  3.22 us
  transfers between devices with their start and end apart: 22, of which 8 were waited for; matrix products, arithmetic and copies ran while one was open for 0% of the time, Pallas kernels for 22%

profile of v3, /device:TPU:0, one launch (start us, length us, event | category | flops | bytes accessed | tf_op | source)
XLA Modules:
  0.0 82.3 jit_solution(10776552046177054330)
XLA Ops:
  0.0 1.8 %shard_map.39 = (bf16[120,256]{1,0:T(8,128)(2,1)}, bf16[120,256]{1,0:T(8,128)(2,1)}, bf16[120,256]{1,0:T(8,128)(2,1)}, bf16[120,256]{1,0:T(8,128)(2,1)}) custom-call(bf16[80,2560]{1,0:T(8,128)(2,1)} %refs_0_.3, bf16[80,2560]{1,0:T(8,128)(2,1)} %refs_1_.3, bf16[80,2560]{1,0:T(8,128)(2,1)} %refs_2_.3), custom_call_target="tpu_custom_call" | custom-call | bytes 1048576 | tf_op jit(solution)/shard_map/pallas_call | solution.py:232
  1.8 1.6 %collective-permute-start = (bf16[120,256]{1,0:T(8,128)(2,1)}, bf16[120,256]{1,0:T(8,128)(2,1)S(1)}, u32[]{:S(2)}, u32[]{:S(2)}) collective-permute-start(bf16[120,256]{1,0:T(8,128)(2,1)} %get-tuple-element.28), channel_id=1, source_target_pairs={{0,32},{32,64},{64,96},{96,0},{1,33},{33,65},{65,97},{97,1},{2,34}... | collective-permute-start | bytes 184328 | tf_op jit(solution)/shard_map/ppermute | solution.py:38
  3.5 1.7 %collective-permute-start.1 = (bf16[120,256]{1,0:T(8,128)(2,1)}, bf16[120,256]{1,0:T(8,128)(2,1)S(1)}, u32[]{:S(2)}, u32[]{:S(2)}) collective-permute-start(bf16[120,256]{1,0:T(8,128)(2,1)} %get-tuple-element.29), channel_id=1, source_target_pairs={{0,96},{32,0},{64,32},{96,64},{1,97},{33,1},{65,33},{97,65},{2,98}... | collective-permute-start | bytes 184328 | tf_op jit(solution)/shard_map/ppermute | solution.py:38
  5.1 1.9 %collective-permute-start.2 = (bf16[120,256]{1,0:T(8,128)(2,1)}, bf16[120,256]{1,0:T(8,128)(2,1)S(1)}, u32[]{:S(2)}, u32[]{:S(2)}) collective-permute-start(bf16[120,256]{1,0:T(8,128)(2,1)} %get-tuple-element.30), channel_id=1, source_target_pairs={{0,64},{32,96},{64,0},{96,32},{1,65},{33,97},{65,1},{97,33},{2,66}... | collective-permute-start | bytes 184328 | tf_op jit(solution)/shard_map/ppermute | solution.py:38
  7.0 1.2 %shard_map.37 = bf16[16,120,256]{2,1,0:T(8,128)(2,1)} custom-call(bf16[80,2560]{1,0:T(8,128)(2,1)S(1)} %copy-done, bf16[80,2560]{1,0:T(8,128)(2,1)S(1)} %copy-done.1, bf16[80,2560]{1,0:T(8,128)(2,1)S(1)} %copy-done.2), custom_call_target="tpu_custom_call" | custom-call | bytes 1048576 | tf_op jit(solution)/shard_map/pallas_call | solution.py:232
  8.3 0.0 copy-start.3
  8.3 5.9 %all-to-all-start = ((bf16[16,120,256]{2,1,0:T(8,128)(2,1)}), bf16[16,120,256]{2,1,0:T(8,128)(2,1)S(1)}, u32[]{:S(2)}, u32[]{:S(2)}) async-start(bf16[16,120,256]{2,1,0:T(8,128)(2,1)} %shard_map.37), calls=%async_computation | async-start | bytes 1966080 | tf_op jit(solution)/shard_map/all_to_all | solution.py:378
  14.2 0.0 collective-permute-done.2.refs_3_
  14.2 2.0 %collective-permute-start.3 = (bf16[320,256]{1,0:T(8,128)(2,1)S(1)}, bf16[320,256]{1,0:T(8,128)(2,1)S(1)}, u32[]{:S(2)}, u32[]{:S(2)}) collective-permute-start(bf16[320,256]{1,0:T(8,128)(2,1)S(1)} %get-tuple-element.31.refs_1_), channel_id=1, source_target_pairs={{0,16},{2,18},{16,2},{18,0},{1,17},{3,19},{17,3},{19,1},{4,20},{6,... | collective-permute-start | bytes 491528 | tf_op jit(solution)/shard_map/ppermute | solution.py:34
  16.2 2.2 %collective-permute-start.4 = (bf16[320,256]{1,0:T(8,128)(2,1)S(1)}, bf16[320,256]{1,0:T(8,128)(2,1)S(1)}, u32[]{:S(2)}, u32[]{:S(2)}) collective-permute-start(bf16[320,256]{1,0:T(8,128)(2,1)S(1)} %get-tuple-element.31.refs_1_), channel_id=1, source_target_pairs={{0,18},{2,16},{16,0},{18,2},{1,19},{3,17},{17,1},{19,3},{4,22},{6,... | collective-permute-start | bytes 491528 | tf_op jit(solution)/shard_map/ppermute | solution.py:34
  18.4 3.2 %collective-permute-done.3.refs_2_ = bf16[320,256]{1,0:T(8,128)(2,1)S(1)} collective-permute-done((bf16[320,256]{1,0:T(8,128)(2,1)S(1)}, bf16[320,256]{1,0:T(8,128)(2,1)S(1)}, u32[]{:S(2)}, u32[]{:S(2)}) %collective-permute-start.3) | collective-permute-done | bytes 163872 | tf_op jit(solution)/shard_map/ppermute | solution.py:34
  21.6 0.0 collective-permute-start.5
  21.6 3.4 %collective-permute-start.10 = (bf16[160,256]{1,0:T(8,128)(2,1)S(1)}, bf16[160,256]{1,0:T(8,128)(2,1)S(1)}, u32[]{:S(2)}, u32[]{:S(2)}) collective-permute-start(bf16[160,256]{1,0:T(8,128)(2,1)S(1)} %get-tuple-element.32.refs_0_), channel_id=1, source_target_pairs={{0,8},{4,12},{8,0},{12,4},{1,9},{5,13},{9,1},{13,5},{2,10},{6,14},... | collective-permute-start | bytes 245768 | tf_op jit(solution)/shard_map/ppermute | solution.py:38
  25.1 1.2 %collective-permute-start.9 = (bf16[160,256]{1,0:T(8,128)(2,1)S(1)}, bf16[160,256]{1,0:T(8,128)(2,1)S(1)}, u32[]{:S(2)}, u32[]{:S(2)}) collective-permute-start(bf16[160,256]{1,0:T(8,128)(2,1)S(1)} %get-tuple-element.32.refs_0_), channel_id=1, source_target_pairs={{0,12},{4,0},{8,4},{12,8},{1,13},{5,1},{9,5},{13,9},{2,14},{6,2},{... | collective-permute-start | bytes 245768 | tf_op jit(solution)/shard_map/ppermute | solution.py:38
  26.2 0.9 %collective-permute-start.8 = (bf16[160,256]{1,0:T(8,128)(2,1)S(1)}, bf16[160,256]{1,0:T(8,128)(2,1)S(1)}, u32[]{:S(2)}, u32[]{:S(2)}) collective-permute-start(bf16[160,256]{1,0:T(8,128)(2,1)S(1)} %get-tuple-element.32.refs_0_), channel_id=1, source_target_pairs={{0,4},{4,8},{8,12},{12,0},{1,5},{5,9},{9,13},{13,1},{2,6},{6,10},{... | collective-permute-start | bytes 245768 | tf_op jit(solution)/shard_map/ppermute | solution.py:38
  27.1 2.7 %all-to-all-done.got = bf16[16,120,256]{2,1,0:T(8,128)(2,1)S(1)} async-done(((bf16[16,120,256]{2,1,0:T(8,128)(2,1)}), bf16[16,120,256]{2,1,0:T(8,128)(2,1)S(1)}, u32[]{:S(2)}, u32[]{:S(2)}) %all-to-all-start) | async-done | bytes 983072 | tf_op jit(solution)/shard_map/all_to_all | solution.py:378
  29.8 0.1 shard_map.38
  29.8 0.0 collective-permute-done.4.refs_3_
  29.8 2.0 %collective-permute-start.7 = (bf16[1280,256]{1,0:T(8,128)(2,1)S(1)}, bf16[1280,256]{1,0:T(8,128)(2,1)S(1)}, u32[]{:S(2)}, u32[]{:S(2)}) collective-permute-start(bf16[1280,256]{1,0:T(8,128)(2,1)S(1)} %get-tuple-element.26.refs_0_.refs_1_), channel_id=1, source_target_pairs={{0,16},{16,0},{1,17},{17,1},{2,18},{18,2},{3,19},{19,3},{4,20},{20... | collective-permute-start | bytes 1966088 | tf_op jit(solution)/shard_map/ppermute | solution.py:42
  31.8 0.1 shard_map.41
  31.9 0.1 collective-permute-start.6
  32.0 0.0 collective-permute-done.10.refs_3_
  32.0 0.0 collective-permute-done.9.refs_2_
  32.0 0.3 collective-permute-done.8.refs_1_
  32.4 4.0 %collective-permute-start.12 = (bf16[640,256]{1,0:T(8,128)(2,1)S(1)}, bf16[640,256]{1,0:T(8,128)(2,1)S(1)}, u32[]{:S(2)}, u32[]{:S(2)}) collective-permute-start(bf16[640,256]{1,0:T(8,128)(2,1)S(1)} %get-tuple-element.25.refs_0_), channel_id=1, source_target_pairs={{0,18},{18,0},{2,16},{16,2},{1,19},{19,1},{3,17},{17,3},{4,22},{22... | collective-permute-start | bytes 983048 | tf_op jit(solution)/shard_map/ppermute | solution.py:46
  36.4 0.1 fusion
  36.5 4.2 %shard_map.43 = (bf16[176,256]{1,0:T(8,128)(2,1)S(1)}, bf16[176,256]{1,0:T(8,128)(2,1)S(1)}, bf16[176,256]{1,0:T(8,128)(2,1)S(1)}, bf16[176,256]{1,0:T(8,128)(2,1)S(1)}) custom-call(bf16[640,256]{1,0:T(8,128)(2,1)S(1)} %shard_map.42.refs_0_, bf16[1280,256]{1,0:T(8,128)(2,1)S(1)} %slice.14.refs_1_, bf16[1280,256]{1,0:T(8,128)(2,1)S(1)} %get-tuple-element.45.refs_2_), custom_call_target="tpu_custom_call" | custom-call | bytes 1310720 | tf_op jit(solution)/shard_map/pallas_call | solution.py:149
  40.7 1.6 %collective-permute-start.13 = (bf16[176,256]{1,0:T(8,128)(2,1)S(1)}, bf16[176,256]{1,0:T(8,128)(2,1)S(1)}, u32[]{:S(2)}, u32[]{:S(2)}) collective-permute-start(bf16[176,256]{1,0:T(8,128)(2,1)S(1)} %get-tuple-element.36), channel_id=1, source_target_pairs={{0,12},{4,0},{8,4},{12,8},{1,13},{5,1},{9,5},{13,9},{2,14},{6,2},{... | collective-permute-start | bytes 270344 | tf_op jit(solution)/shard_map/ppermute | solution.py:38
  42.4 0.5 collective-permute-start.14
  42.8 1.9 %collective-permute-start.15 = (bf16[176,256]{1,0:T(8,128)(2,1)S(1)}, bf16[176,256]{1,0:T(8,128)(2,1)S(1)}, u32[]{:S(2)}, u32[]{:S(2)}) collective-permute-start(bf16[176,256]{1,0:T(8,128)(2,1)S(1)} %get-tuple-element.38), channel_id=1, source_target_pairs={{0,8},{4,12},{8,0},{12,4},{1,9},{5,13},{9,1},{13,5},{2,10},{6,14},... | collective-permute-start | bytes 270344 | tf_op jit(solution)/shard_map/ppermute | solution.py:38
  44.8 0.0 collective-permute-done.7.a
  44.8 0.3 collective-permute-start.11
  45.1 4.3 %shard_map.45 = (f32[1280,256]{1,0:T(8,128)S(1)}, f32[1280,128]{1,0:T(8,128)S(1)}) custom-call(bf16[640,256]{1,0:T(8,128)(2,1)S(1)} %collective-permute-done.12.refs_0_, bf16[1280,256]{1,0:T(8,128)(2,1)S(1)} %get-tuple-element.26.refs_0_.refs_1_, bf16[1280,256]{1,0:T(8,128)(2,1)S(1)} %get-tuple-element.46.refs_2_, ...), custom_call_target="tpu_custom_call" | custom-call | flops 20000000000 | bytes 1310720 | tf_op jit(solution)/shard_map/pallas_call | solution.py:149
  49.4 0.0 collective-permute-done.14.refs_6_.refs_2_
  49.4 4.4 %shard_map.46.refs_5_ = bf16[656,256]{1,0:T(8,128)(2,1)S(1)} custom-call(bf16[640,256]{1,0:T(8,128)(2,1)S(1)} %collective-permute-done.12.refs_0_, bf16[1280,256]{1,0:T(8,128)(2,1)S(1)} %shard_map.44.refs_3_.refs_1_, bf16[1280,256]{1,0:T(8,128)(2,1)S(1)} %collective-permute-done.11.refs_2_.refs_4_, f32[1280,256]{1,0:T(8,128)S(1)} %get-tuple-element.34.refs_3_, ...), custom_call_target="tpu_custom_call" | custom-call | bytes 1310720 | tf_op jit(solution)/shard_map/pallas_call | solution.py:149
  53.8 3.8 %collective-permute-start.16 = (bf16[656,256]{1,0:T(8,128)(2,1)S(1)}, bf16[656,256]{1,0:T(8,128)(2,1)S(1)}, u32[]{:S(2)}, u32[]{:S(2)}) collective-permute-start(bf16[656,256]{1,0:T(8,128)(2,1)S(1)} %shard_map.46.refs_5_), channel_id=1, source_target_pairs={{0,18},{18,0},{2,16},{16,2},{1,19},{19,1},{3,17},{17,3},{4,22},{22... | collective-permute-start | bytes 1007624 | tf_op jit(solution)/shard_map/ppermute | solution.py:46
  57.6 0.5 shard_map.47
  58.1 7.7 %shard_map.48 = (f32[1280,256]{1,0:T(8,128)S(1)}, f32[1280,128]{1,0:T(8,128)S(1)}) custom-call(bf16[640,256]{1,0:T(8,128)(2,1)S(1)} %get-tuple-element.25.refs_0_, bf16[1280,256]{1,0:T(8,128)(2,1)S(1)} %get-tuple-element.26.refs_0_.refs_1_, bf16[1280,256]{1,0:T(8,128)(2,1)S(1)} %get-tuple-element.46.refs_2_, ...), custom_call_target="tpu_custom_call" | custom-call | bytes 2621440 | tf_op jit(solution)/shard_map/pallas_call | solution.py:149
  65.9 0.3 collective-permute-done.16.sent
  66.2 1.2 %shard_map.49 = bf16[640,256]{1,0:T(8,128)(2,1)} custom-call(f32[1280,256]{1,0:T(8,128)S(1)} %get-tuple-element.40.acc, f32[1280,128]{1,0:T(8,128)S(1)} %get-tuple-element.41.top, bf16[656,256]{1,0:T(8,128)(2,1)S(1)} %collective-permute-done.16.sent), custom_call_target="tpu_custom_call" | custom-call | bytes 1048576 | tf_op jit(solution)/shard_map/pallas_call | solution.py:330
  67.4 4.4 %all-to-all-start.1 = ((bf16[16,40,256]{2,1,0:T(8,128)(2,1)}), bf16[16,40,256]{2,1,0:T(8,128)(2,1)S(1)}, u32[]{:S(2)}, u32[]{:S(2)}) async-start(bf16[16,40,256]{2,1,0:T(8,128)(2,1)} %bitcast), calls=%async_computation.1 | async-start | bytes 655360 | tf_op jit(solution)/shard_map/all_to_all | solution.py:396
  71.8 3.1 %collective-permute-start.17 = (bf16[40,256]{1,0:T(8,128)(2,1)S(1)}, bf16[40,256]{1,0:T(8,128)(2,1)S(1)}, u32[]{:S(2)}, u32[]{:S(2)}) collective-permute-start(bf16[40,256]{1,0:T(8,128)(2,1)S(1)} %get-tuple-element.42), channel_id=1, source_target_pairs={{0,96},{32,0},{64,32},{96,64},{1,97},{33,1},{65,33},{97,65},{2,98}... | collective-permute-start | bytes 61448 | tf_op jit(solution)/shard_map/ppermute | solution.py:38
  75.0 2.3 %collective-permute-start.19 = (bf16[40,256]{1,0:T(8,128)(2,1)S(1)}, bf16[40,256]{1,0:T(8,128)(2,1)S(1)}, u32[]{:S(2)}, u32[]{:S(2)}) collective-permute-start(bf16[40,256]{1,0:T(8,128)(2,1)S(1)} %get-tuple-element.44), channel_id=1, source_target_pairs={{0,64},{32,96},{64,0},{96,32},{1,65},{33,97},{65,1},{97,33},{2,66}... | collective-permute-start | bytes 61448 | tf_op jit(solution)/shard_map/ppermute | solution.py:38
  77.3 0.8 %collective-permute-done.17.refs_1_ = bf16[40,256]{1,0:T(8,128)(2,1)S(1)} collective-permute-done((bf16[40,256]{1,0:T(8,128)(2,1)S(1)}, bf16[40,256]{1,0:T(8,128)(2,1)S(1)}, u32[]{:S(2)}, u32[]{:S(2)}) %collective-permute-start.17) | collective-permute-done | bytes 20512 | tf_op jit(solution)/shard_map/ppermute | solution.py:38
  78.1 1.8 %collective-permute-done.18.refs_2_ = bf16[40,256]{1,0:T(8,128)(2,1)S(1)} collective-permute-done((bf16[40,256]{1,0:T(8,128)(2,1)S(1)}, bf16[40,256]{1,0:T(8,128)(2,1)S(1)}, u32[]{:S(2)}, u32[]{:S(2)}) %collective-permute-start.18) | collective-permute-done | bytes 20512 | tf_op jit(solution)/shard_map/ppermute | solution.py:38
  80.0 0.3 collective-permute-done.19.refs_3_
  80.3 1.2 %all-to-all-done.1.main = bf16[16,40,256]{2,1,0:T(8,128)(2,1)S(1)} async-done(((bf16[16,40,256]{2,1,0:T(8,128)(2,1)}), bf16[16,40,256]{2,1,0:T(8,128)(2,1)S(1)}, u32[]{:S(2)}, u32[]{:S(2)}) %all-to-all-start.1) | async-done | bytes 327712 | tf_op jit(solution)/shard_map/all_to_all | solution.py:396
  81.5 0.8 %shard_map.50 = bf16[80,2560]{1,0:T(8,128)(2,1)} custom-call(bf16[16,40,256]{2,1,0:T(8,128)(2,1)S(1)} %all-to-all-done.1.main, bf16[40,256]{1,0:T(8,128)(2,1)S(1)} %get-tuple-element.39.refs_6_.refs_0_, bf16[40,256]{1,0:T(8,128)(2,1)S(1)} %collective-permute-done.17.refs_1_, bf16[40,256]{1,0:T(8,128)(2,1)S(1)} %collective-permute-done.18.refs_2_, ...), custom_call_target="tpu_custom_call" | custom-call | bytes 1048576 | tf_op jit(solution)/shard_map/pallas_call | solution.py:356
  (20 shorter events, 0.2 us)
Async XLA Ops:
  0.0 7.0 %copy-start.2 = (bf16[80,2560]{1,0:T(8,128)(2,1)S(1)}, bf16[80,2560]{1,0:T(8,128)(2,1)}, u32[]{:S(2)}) copy-start(bf16[80,2560]{1,0:T(8,128)(2,1)} %refs_2_.3) | copy-start | bytes 1228804
  0.0 7.0 %copy-start.1 = (bf16[80,2560]{1,0:T(8,128)(2,1)S(1)}, bf16[80,2560]{1,0:T(8,128)(2,1)}, u32[]{:S(2)}) copy-start(bf16[80,2560]{1,0:T(8,128)(2,1)} %refs_1_.3) | copy-start | bytes 1228804
  0.0 7.0 %copy-start = (bf16[80,2560]{1,0:T(8,128)(2,1)S(1)}, bf16[80,2560]{1,0:T(8,128)(2,1)}, u32[]{:S(2)}) copy-start(bf16[80,2560]{1,0:T(8,128)(2,1)} %refs_0_.3) | copy-start | bytes 1228804
  1.8 12.4 %collective-permute-start = (bf16[120,256]{1,0:T(8,128)(2,1)}, bf16[120,256]{1,0:T(8,128)(2,1)S(1)}, u32[]{:S(2)}, u32[]{:S(2)}) collective-permute-start(bf16[120,256]{1,0:T(8,128)(2,1)} %get-tuple-element.28), channel_id=1, source_target_pairs={{0,32},{32,64},{64,96},{96,0},{1,33},{33,65},{65,97},{97,1},{2,34}... | collective-permute-start | bytes 184328 | tf_op jit(solution)/shard_map/ppermute | solution.py:38
  3.5 10.7 %collective-permute-start.1 = (bf16[120,256]{1,0:T(8,128)(2,1)}, bf16[120,256]{1,0:T(8,128)(2,1)S(1)}, u32[]{:S(2)}, u32[]{:S(2)}) collective-permute-start(bf16[120,256]{1,0:T(8,128)(2,1)} %get-tuple-element.29), channel_id=1, source_target_pairs={{0,96},{32,0},{64,32},{96,64},{1,97},{33,1},{65,33},{97,65},{2,98}... | collective-permute-start | bytes 184328 | tf_op jit(solution)/shard_map/ppermute | solution.py:38
  5.1 9.1 %collective-permute-start.2 = (bf16[120,256]{1,0:T(8,128)(2,1)}, bf16[120,256]{1,0:T(8,128)(2,1)S(1)}, u32[]{:S(2)}, u32[]{:S(2)}) collective-permute-start(bf16[120,256]{1,0:T(8,128)(2,1)} %get-tuple-element.30), channel_id=1, source_target_pairs={{0,64},{32,96},{64,0},{96,32},{1,65},{33,97},{65,1},{97,33},{2,66}... | collective-permute-start | bytes 184328 | tf_op jit(solution)/shard_map/ppermute | solution.py:38
  8.3 5.9 %copy-start.3 = (bf16[120,256]{1,0:T(8,128)(2,1)S(1)}, bf16[120,256]{1,0:T(8,128)(2,1)}, u32[]{:S(2)}) copy-start(bf16[120,256]{1,0:T(8,128)(2,1)} %get-tuple-element.27.refs_0_) | copy-start | bytes 184324
  8.3 21.5 %all-to-all-start = ((bf16[16,120,256]{2,1,0:T(8,128)(2,1)}), bf16[16,120,256]{2,1,0:T(8,128)(2,1)S(1)}, u32[]{:S(2)}, u32[]{:S(2)}) async-start(bf16[16,120,256]{2,1,0:T(8,128)(2,1)} %shard_map.37), calls=%async_computation | async-start | bytes 1966080 | tf_op jit(solution)/shard_map/all_to_all | solution.py:378
  14.2 7.4 %collective-permute-start.3 = (bf16[320,256]{1,0:T(8,128)(2,1)S(1)}, bf16[320,256]{1,0:T(8,128)(2,1)S(1)}, u32[]{:S(2)}, u32[]{:S(2)}) collective-permute-start(bf16[320,256]{1,0:T(8,128)(2,1)S(1)} %get-tuple-element.31.refs_1_), channel_id=1, source_target_pairs={{0,16},{2,18},{16,2},{18,0},{1,17},{3,19},{17,3},{19,1},{4,20},{6,... | collective-permute-start | bytes 491528 | tf_op jit(solution)/shard_map/ppermute | solution.py:34
  16.2 13.6 %collective-permute-start.4 = (bf16[320,256]{1,0:T(8,128)(2,1)S(1)}, bf16[320,256]{1,0:T(8,128)(2,1)S(1)}, u32[]{:S(2)}, u32[]{:S(2)}) collective-permute-start(bf16[320,256]{1,0:T(8,128)(2,1)S(1)} %get-tuple-element.31.refs_1_), channel_id=1, source_target_pairs={{0,18},{2,16},{16,0},{18,2},{1,19},{3,17},{17,1},{19,3},{4,22},{6,... | collective-permute-start | bytes 491528 | tf_op jit(solution)/shard_map/ppermute | solution.py:34
  21.6 10.2 %collective-permute-start.5 = (bf16[320,256]{1,0:T(8,128)(2,1)S(1)}, bf16[320,256]{1,0:T(8,128)(2,1)S(1)}, u32[]{:S(2)}, u32[]{:S(2)}) collective-permute-start(bf16[320,256]{1,0:T(8,128)(2,1)S(1)} %collective-permute-done.3.refs_2_), channel_id=1, source_target_pairs={{0,16},{2,18},{16,2},{18,0},{1,17},{3,19},{17,3},{19,1},{4,20},{6,... | collective-permute-start | bytes 491528 | tf_op jit(solution)/shard_map/ppermute | solution.py:34
  21.6 10.4 %collective-permute-start.10 = (bf16[160,256]{1,0:T(8,128)(2,1)S(1)}, bf16[160,256]{1,0:T(8,128)(2,1)S(1)}, u32[]{:S(2)}, u32[]{:S(2)}) collective-permute-start(bf16[160,256]{1,0:T(8,128)(2,1)S(1)} %get-tuple-element.32.refs_0_), channel_id=1, source_target_pairs={{0,8},{4,12},{8,0},{12,4},{1,9},{5,13},{9,1},{13,5},{2,10},{6,14},... | collective-permute-start | bytes 245768 | tf_op jit(solution)/shard_map/ppermute | solution.py:38
  25.1 7.0 %collective-permute-start.9 = (bf16[160,256]{1,0:T(8,128)(2,1)S(1)}, bf16[160,256]{1,0:T(8,128)(2,1)S(1)}, u32[]{:S(2)}, u32[]{:S(2)}) collective-permute-start(bf16[160,256]{1,0:T(8,128)(2,1)S(1)} %get-tuple-element.32.refs_0_), channel_id=1, source_target_pairs={{0,12},{4,0},{8,4},{12,8},{1,13},{5,1},{9,5},{13,9},{2,14},{6,2},{... | collective-permute-start | bytes 245768 | tf_op jit(solution)/shard_map/ppermute | solution.py:38
  26.2 6.1 %collective-permute-start.8 = (bf16[160,256]{1,0:T(8,128)(2,1)S(1)}, bf16[160,256]{1,0:T(8,128)(2,1)S(1)}, u32[]{:S(2)}, u32[]{:S(2)}) collective-permute-start(bf16[160,256]{1,0:T(8,128)(2,1)S(1)} %get-tuple-element.32.refs_0_), channel_id=1, source_target_pairs={{0,4},{4,8},{8,12},{12,0},{1,5},{5,9},{9,13},{13,1},{2,6},{6,10},{... | collective-permute-start | bytes 245768 | tf_op jit(solution)/shard_map/ppermute | solution.py:38
  29.8 14.9 %collective-permute-start.7 = (bf16[1280,256]{1,0:T(8,128)(2,1)S(1)}, bf16[1280,256]{1,0:T(8,128)(2,1)S(1)}, u32[]{:S(2)}, u32[]{:S(2)}) collective-permute-start(bf16[1280,256]{1,0:T(8,128)(2,1)S(1)} %get-tuple-element.26.refs_0_.refs_1_), channel_id=1, source_target_pairs={{0,16},{16,0},{1,17},{17,1},{2,18},{18,2},{3,19},{19,3},{4,20},{20... | collective-permute-start | bytes 1966088 | tf_op jit(solution)/shard_map/ppermute | solution.py:42
  31.9 4.5 %collective-permute-start.6 = (bf16[2560,256]{1,0:T(8,128)(2,1)S(1)}, bf16[2560,256]{1,0:T(8,128)(2,1)S(1)}, u32[]{:S(2)}, u32[]{:S(2)}) collective-permute-start(bf16[2560,256]{1,0:T(8,128)(2,1)S(1)} %shard_map.41), channel_id=1, source_target_pairs={{0,1},{1,0},{2,3},{3,2},{4,5},{5,4},{6,7},{7,6},{8,9},{9,8},{10,11... | collective-permute-start | bytes 3932168 | tf_op jit(solution)/shard_map/ppermute | solution.py:50
  32.4 12.7 %collective-permute-start.12 = (bf16[640,256]{1,0:T(8,128)(2,1)S(1)}, bf16[640,256]{1,0:T(8,128)(2,1)S(1)}, u32[]{:S(2)}, u32[]{:S(2)}) collective-permute-start(bf16[640,256]{1,0:T(8,128)(2,1)S(1)} %get-tuple-element.25.refs_0_), channel_id=1, source_target_pairs={{0,18},{18,0},{2,16},{16,2},{1,19},{19,1},{3,17},{17,3},{4,22},{22... | collective-permute-start | bytes 983048 | tf_op jit(solution)/shard_map/ppermute | solution.py:46
  40.7 8.6 %collective-permute-start.13 = (bf16[176,256]{1,0:T(8,128)(2,1)S(1)}, bf16[176,256]{1,0:T(8,128)(2,1)S(1)}, u32[]{:S(2)}, u32[]{:S(2)}) collective-permute-start(bf16[176,256]{1,0:T(8,128)(2,1)S(1)} %get-tuple-element.36), channel_id=1, source_target_pairs={{0,12},{4,0},{8,4},{12,8},{1,13},{5,1},{9,5},{13,9},{2,14},{6,2},{... | collective-permute-start | bytes 270344 | tf_op jit(solution)/shard_map/ppermute | solution.py:38
  42.4 7.1 %collective-permute-start.14 = (bf16[176,256]{1,0:T(8,128)(2,1)S(1)}, bf16[176,256]{1,0:T(8,128)(2,1)S(1)}, u32[]{:S(2)}, u32[]{:S(2)}) collective-permute-start(bf16[176,256]{1,0:T(8,128)(2,1)S(1)} %get-tuple-element.37), channel_id=1, source_target_pairs={{0,4},{4,8},{8,12},{12,0},{1,5},{5,9},{9,13},{13,1},{2,6},{6,10},{... | collective-permute-start | bytes 270344 | tf_op jit(solution)/shard_map/ppermute | solution.py:38
  42.8 6.6 %collective-permute-start.15 = (bf16[176,256]{1,0:T(8,128)(2,1)S(1)}, bf16[176,256]{1,0:T(8,128)(2,1)S(1)}, u32[]{:S(2)}, u32[]{:S(2)}) collective-permute-start(bf16[176,256]{1,0:T(8,128)(2,1)S(1)} %get-tuple-element.38), channel_id=1, source_target_pairs={{0,8},{4,12},{8,0},{12,4},{1,9},{5,13},{9,1},{13,5},{2,10},{6,14},... | collective-permute-start | bytes 270344 | tf_op jit(solution)/shard_map/ppermute | solution.py:38
  44.8 4.6 %collective-permute-start.11 = (bf16[1280,256]{1,0:T(8,128)(2,1)S(1)}, bf16[1280,256]{1,0:T(8,128)(2,1)S(1)}, u32[]{:S(2)}, u32[]{:S(2)}) collective-permute-start(bf16[1280,256]{1,0:T(8,128)(2,1)S(1)} %shard_map.44.refs_3_.refs_1_), channel_id=1, source_target_pairs={{0,1},{1,0},{2,3},{3,2},{4,5},{5,4},{6,7},{7,6},{8,9},{9,8},{10,11... | collective-permute-start | bytes 1966088 | tf_op jit(solution)/shard_map/ppermute | solution.py:50
  53.8 12.3 %collective-permute-start.16 = (bf16[656,256]{1,0:T(8,128)(2,1)S(1)}, bf16[656,256]{1,0:T(8,128)(2,1)S(1)}, u32[]{:S(2)}, u32[]{:S(2)}) collective-permute-start(bf16[656,256]{1,0:T(8,128)(2,1)S(1)} %shard_map.46.refs_5_), channel_id=1, source_target_pairs={{0,18},{18,0},{2,16},{16,2},{1,19},{19,1},{3,17},{17,3},{4,22},{22... | collective-permute-start | bytes 1007624 | tf_op jit(solution)/shard_map/ppermute | solution.py:46
  67.4 14.1 %all-to-all-start.1 = ((bf16[16,40,256]{2,1,0:T(8,128)(2,1)}), bf16[16,40,256]{2,1,0:T(8,128)(2,1)S(1)}, u32[]{:S(2)}, u32[]{:S(2)}) async-start(bf16[16,40,256]{2,1,0:T(8,128)(2,1)} %bitcast), calls=%async_computation.1 | async-start | bytes 655360 | tf_op jit(solution)/shard_map/all_to_all | solution.py:396
  71.8 6.3 %collective-permute-start.17 = (bf16[40,256]{1,0:T(8,128)(2,1)S(1)}, bf16[40,256]{1,0:T(8,128)(2,1)S(1)}, u32[]{:S(2)}, u32[]{:S(2)}) collective-permute-start(bf16[40,256]{1,0:T(8,128)(2,1)S(1)} %get-tuple-element.42), channel_id=1, source_target_pairs={{0,96},{32,0},{64,32},{96,64},{1,97},{33,1},{65,33},{97,65},{2,98}... | collective-permute-start | bytes 61448 | tf_op jit(solution)/shard_map/ppermute | solution.py:38
  75.0 5.0 %collective-permute-start.18 = (bf16[40,256]{1,0:T(8,128)(2,1)S(1)}, bf16[40,256]{1,0:T(8,128)(2,1)S(1)}, u32[]{:S(2)}, u32[]{:S(2)}) collective-permute-start(bf16[40,256]{1,0:T(8,128)(2,1)S(1)} %get-tuple-element.43), channel_id=1, source_target_pairs={{0,32},{32,64},{64,96},{96,0},{1,33},{33,65},{65,97},{97,1},{2,34}... | collective-permute-start | bytes 61448 | tf_op jit(solution)/shard_map/ppermute | solution.py:38
  75.0 5.3 %collective-permute-start.19 = (bf16[40,256]{1,0:T(8,128)(2,1)S(1)}, bf16[40,256]{1,0:T(8,128)(2,1)S(1)}, u32[]{:S(2)}, u32[]{:S(2)}) collective-permute-start(bf16[40,256]{1,0:T(8,128)(2,1)S(1)} %get-tuple-element.44), channel_id=1, source_target_pairs={{0,64},{32,96},{64,0},{96,32},{1,65},{33,97},{65,1},{97,33},{2,66}... | collective-permute-start | bytes 61448 | tf_op jit(solution)/shard_map/ppermute | solution.py:38

commit v4 on v3

--- a/solution.py
+++ b/solution.py
@@ -92,30 +92,32 @@
     refs = refs[n_after:]
     rows = q_ref.shape[0]
     ones = jnp.ones((K_BLOCK, HEAD_DIM), jnp.bfloat16)
+    q = jnp.concatenate([scaled_halves(q_ref[:, :HEAD_DIM]), scaled_halves(q_ref[:, HEAD_DIM:])], axis=0)
+    if first:
+        top = jnp.full((2 * rows, 1), -1e30, jnp.float32)
+        acc = jnp.zeros((2 * rows, PAIR), jnp.float32)
+    else:
+        top = jnp.max(top_in[...], axis=1, keepdims=True)
+        acc = acc_in[...]
+    for kv_ref in kv_refs:
+        for j in range(kv_ref.shape[0] // K_BLOCK):
+            there = slice(j * K_BLOCK, (j + 1) * K_BLOCK)
+            k = kv_ref[there, :HEAD_DIM]
+            v = kv_ref[there, HEAD_DIM:]
+            scores = lax.dot_general(
+                q, jnp.concatenate([k, k], axis=1), NT, preferred_element_type=jnp.float32
+            )
+            fresh = jnp.maximum(top, jnp.max(scores, axis=1, keepdims=True))
+            weights = jnp.exp2(scores - fresh).astype(jnp.bfloat16)
+            acc = acc * jnp.exp2(top - fresh) + jnp.dot(
+                weights, jnp.concatenate([v, ones], axis=1), preferred_element_type=jnp.float32
+            )
+            top = fresh
+    whole_top, whole_acc = top, acc
     for half in range(2):
         lanes = slice(half * HEAD_DIM, (half + 1) * HEAD_DIM)
         here = slice(half * rows, (half + 1) * rows)
-        q = scaled_halves(q_ref[:, lanes])
-        if first:
-            top = jnp.full((rows, 1), -1e30, jnp.float32)
-            acc = jnp.zeros((rows, PAIR), jnp.float32)
-        else:
-            top = jnp.max(top_in[here, :], axis=1, keepdims=True)
-            acc = acc_in[here, :]
-        for kv_ref in kv_refs:
-            for j in range(kv_ref.shape[0] // K_BLOCK):
-                there = slice(j * K_BLOCK, (j + 1) * K_BLOCK)
-                k = kv_ref[there, :HEAD_DIM]
-                v = kv_ref[there, HEAD_DIM:]
-                scores = lax.dot_general(
-                    q, jnp.concatenate([k, k], axis=1), NT, preferred_element_type=jnp.float32
-                )
-                fresh = jnp.maximum(top, jnp.max(scores, axis=1, keepdims=True))
-                weights = jnp.exp2(scores - fresh).astype(jnp.bfloat16)
-                acc = acc * jnp.exp2(top - fresh) + jnp.dot(
-                    weights, jnp.concatenate([v, ones], axis=1), preferred_element_type=jnp.float32
-                )
-                top = fresh
+        top, acc = whole_top[here, :], whole_acc[here, :]
         if last == "send":
             total = acc[:, HEAD_DIM:]
             refs[0][:rows, lanes] = (acc[:, :HEAD_DIM] / total).astype(jnp.bfloat16)
@@ -317,13 +319,11 @@
         for i in range(blocks):
             there = slice(i * HEAD_DIM, (i + 1) * HEAD_DIM)
             here = slice(half * rows + i * HEAD_DIM, half * rows + (i + 1) * HEAD_DIM)
-            total = acc[here, HEAD_DIM:]
-            level = top[here, :] + jnp.log2(total)
             other = decoded_column(coded, i, blocks)
-            largest = jnp.maximum(level, other)
-            share, other = jnp.exp2(level - largest), jnp.exp2(other - largest)
-            summed = acc[here, :HEAD_DIM] / total * share + sent[there, lanes].astype(jnp.float32) * other
-            out[there, lanes] = (summed / (share + other)).astype(jnp.bfloat16)
+            largest = jnp.maximum(top[here, :], other)
+            share, other = jnp.exp2(top[here, :] - largest), jnp.exp2(other - largest)
+            summed = acc[here, :HEAD_DIM] * share + sent[there, lanes].astype(jnp.float32) * other
+            out[there, lanes] = (summed / (acc[here, HEAD_DIM:] * share + other)).astype(jnp.bfloat16)
 
 
 def merge(acc, top, sent):

time: 82.6 us -> 82.2 us (level)
  transfers between devices with their start and end apart: 22 -> 22, of which waited for: 8 -> 9; matrix products, arithmetic and copies ran while one was open for 0% -> 0% of each run, Pallas kernels for 22% -> 22%
where the time goes in v4:
time: 82.2 us; the launch traced here: 81.9 us
  starting transfers between devices  44.7 us (54%)
  Pallas kernels  25.9 us (32%)
  waiting for transfers between devices  11 us (13%)
    ppermute x12, starting transfers between devices, along(): return lax.ppermute(a, axis, [(i, (i + step) % 4) for i in range(4)])  20.1 us
    pallas_call x4, Pallas kernels, attend(): pl.pallas_call(functools.partial(attend_kernel, len(kvs), len(after), sta...  20.1 us
    ppermute x2, starting transfers between devices, query_partner(): return lax.ppermute(a, ('zl', 'zh'), [(0, 3), (3, 0), (1, 2), (2, 1)])  7.72 us
    all_to_all x1, starting transfers between devices, local(): got = lax.all_to_all(sent, ('x', 'y'), 0, 0, tiled=True)  5.87 us
    all_to_all x1, starting transfers between devices, local(): lax.all_to_all(out.reshape(COLUMNS, Q_ROWS, PAIR), ('x', 'y'), 0, 0, tile...  4.41 us
    ppermute x3, starting transfers between devices, along_z(): return lax.ppermute(a, ('zl', 'zh'), pairs)  4.19 us
    ppermute x12, waiting for transfers between devices, along(): return lax.ppermute(a, axis, [(i, (i + step) % 4) for i in range(4)])  3.44 us
    ppermute x3, waiting for transfers between devices, along_z(): return lax.ppermute(a, ('zl', 'zh'), pairs)  3.22 us
  transfers between devices with their start and end apart: 22, of which 9 were waited for; matrix products, arithmetic and copies ran while one was open for 0% of the time, Pallas kernels for 22%

profile of v4, /device:TPU:0, one launch (start us, length us, event | category | flops | bytes accessed | tf_op | source)
XLA Modules:
  0.0 81.9 jit_solution(16986260723506045179)
XLA Ops:
  0.0 1.8 %shard_map.39 = (bf16[120,256]{1,0:T(8,128)(2,1)}, bf16[120,256]{1,0:T(8,128)(2,1)}, bf16[120,256]{1,0:T(8,128)(2,1)}, bf16[120,256]{1,0:T(8,128)(2,1)}) custom-call(bf16[80,2560]{1,0:T(8,128)(2,1)} %refs_0_.3, bf16[80,2560]{1,0:T(8,128)(2,1)} %refs_1_.3, bf16[80,2560]{1,0:T(8,128)(2,1)} %refs_2_.3), custom_call_target="tpu_custom_call" | custom-call | bytes 1048576 | tf_op jit(solution)/shard_map/pallas_call | solution.py:234
  1.8 1.6 %collective-permute-start = (bf16[120,256]{1,0:T(8,128)(2,1)}, bf16[120,256]{1,0:T(8,128)(2,1)S(1)}, u32[]{:S(2)}, u32[]{:S(2)}) collective-permute-start(bf16[120,256]{1,0:T(8,128)(2,1)} %get-tuple-element.28), channel_id=1, source_target_pairs={{0,32},{32,64},{64,96},{96,0},{1,33},{33,65},{65,97},{97,1},{2,34}... | collective-permute-start | bytes 184328 | tf_op jit(solution)/shard_map/ppermute | solution.py:38
  3.5 1.7 %collective-permute-start.1 = (bf16[120,256]{1,0:T(8,128)(2,1)}, bf16[120,256]{1,0:T(8,128)(2,1)S(1)}, u32[]{:S(2)}, u32[]{:S(2)}) collective-permute-start(bf16[120,256]{1,0:T(8,128)(2,1)} %get-tuple-element.29), channel_id=1, source_target_pairs={{0,96},{32,0},{64,32},{96,64},{1,97},{33,1},{65,33},{97,65},{2,98}... | collective-permute-start | bytes 184328 | tf_op jit(solution)/shard_map/ppermute | solution.py:38
  5.1 1.9 %collective-permute-start.2 = (bf16[120,256]{1,0:T(8,128)(2,1)}, bf16[120,256]{1,0:T(8,128)(2,1)S(1)}, u32[]{:S(2)}, u32[]{:S(2)}) collective-permute-start(bf16[120,256]{1,0:T(8,128)(2,1)} %get-tuple-element.30), channel_id=1, source_target_pairs={{0,64},{32,96},{64,0},{96,32},{1,65},{33,97},{65,1},{97,33},{2,66}... | collective-permute-start | bytes 184328 | tf_op jit(solution)/shard_map/ppermute | solution.py:38
  7.0 1.2 %shard_map.37 = bf16[16,120,256]{2,1,0:T(8,128)(2,1)} custom-call(bf16[80,2560]{1,0:T(8,128)(2,1)S(1)} %copy-done, bf16[80,2560]{1,0:T(8,128)(2,1)S(1)} %copy-done.1, bf16[80,2560]{1,0:T(8,128)(2,1)S(1)} %copy-done.2), custom_call_target="tpu_custom_call" | custom-call | bytes 1048576 | tf_op jit(solution)/shard_map/pallas_call | solution.py:234
  8.3 0.0 copy-start.3
  8.3 5.9 %all-to-all-start = ((bf16[16,120,256]{2,1,0:T(8,128)(2,1)}), bf16[16,120,256]{2,1,0:T(8,128)(2,1)S(1)}, u32[]{:S(2)}, u32[]{:S(2)}) async-start(bf16[16,120,256]{2,1,0:T(8,128)(2,1)} %shard_map.37), calls=%async_computation | async-start | bytes 1966080 | tf_op jit(solution)/shard_map/all_to_all | solution.py:378
  14.2 0.0 collective-permute-done.refs_1_
  14.2 0.0 collective-permute-done.1.refs_2_
  14.2 2.0 %collective-permute-start.3 = (bf16[320,256]{1,0:T(8,128)(2,1)S(1)}, bf16[320,256]{1,0:T(8,128)(2,1)S(1)}, u32[]{:S(2)}, u32[]{:S(2)}) collective-permute-start(bf16[320,256]{1,0:T(8,128)(2,1)S(1)} %get-tuple-element.31.refs_1_), channel_id=1, source_target_pairs={{0,16},{2,18},{16,2},{18,0},{1,17},{3,19},{17,3},{19,1},{4,20},{6,... | collective-permute-start | bytes 491528 | tf_op jit(solution)/shard_map/ppermute | solution.py:34
  16.2 2.2 %collective-permute-start.4 = (bf16[320,256]{1,0:T(8,128)(2,1)S(1)}, bf16[320,256]{1,0:T(8,128)(2,1)S(1)}, u32[]{:S(2)}, u32[]{:S(2)}) collective-permute-start(bf16[320,256]{1,0:T(8,128)(2,1)S(1)} %get-tuple-element.31.refs_1_), channel_id=1, source_target_pairs={{0,18},{2,16},{16,0},{18,2},{1,19},{3,17},{17,1},{19,3},{4,22},{6,... | collective-permute-start | bytes 491528 | tf_op jit(solution)/shard_map/ppermute | solution.py:34
  18.4 3.2 %collective-permute-done.3.refs_2_ = bf16[320,256]{1,0:T(8,128)(2,1)S(1)} collective-permute-done((bf16[320,256]{1,0:T(8,128)(2,1)S(1)}, bf16[320,256]{1,0:T(8,128)(2,1)S(1)}, u32[]{:S(2)}, u32[]{:S(2)}) %collective-permute-start.3) | collective-permute-done | bytes 163872 | tf_op jit(solution)/shard_map/ppermute | solution.py:34
  21.6 3.4 %collective-permute-start.10 = (bf16[160,256]{1,0:T(8,128)(2,1)S(1)}, bf16[160,256]{1,0:T(8,128)(2,1)S(1)}, u32[]{:S(2)}, u32[]{:S(2)}) collective-permute-start(bf16[160,256]{1,0:T(8,128)(2,1)S(1)} %get-tuple-element.32.refs_0_), channel_id=1, source_target_pairs={{0,8},{4,12},{8,0},{12,4},{1,9},{5,13},{9,1},{13,5},{2,10},{6,14},... | collective-permute-start | bytes 245768 | tf_op jit(solution)/shard_map/ppermute | solution.py:38
  25.1 1.2 %collective-permute-start.9 = (bf16[160,256]{1,0:T(8,128)(2,1)S(1)}, bf16[160,256]{1,0:T(8,128)(2,1)S(1)}, u32[]{:S(2)}, u32[]{:S(2)}) collective-permute-start(bf16[160,256]{1,0:T(8,128)(2,1)S(1)} %get-tuple-element.32.refs_0_), channel_id=1, source_target_pairs={{0,12},{4,0},{8,4},{12,8},{1,13},{5,1},{9,5},{13,9},{2,14},{6,2},{... | collective-permute-start | bytes 245768 | tf_op jit(solution)/shard_map/ppermute | solution.py:38
  26.2 0.9 %collective-permute-start.8 = (bf16[160,256]{1,0:T(8,128)(2,1)S(1)}, bf16[160,256]{1,0:T(8,128)(2,1)S(1)}, u32[]{:S(2)}, u32[]{:S(2)}) collective-permute-start(bf16[160,256]{1,0:T(8,128)(2,1)S(1)} %get-tuple-element.32.refs_0_), channel_id=1, source_target_pairs={{0,4},{4,8},{8,12},{12,0},{1,5},{5,9},{9,13},{13,1},{2,6},{6,10},{... | collective-permute-start | bytes 245768 | tf_op jit(solution)/shard_map/ppermute | solution.py:38
  27.1 2.7 %all-to-all-done.got = bf16[16,120,256]{2,1,0:T(8,128)(2,1)S(1)} async-done(((bf16[16,120,256]{2,1,0:T(8,128)(2,1)}), bf16[16,120,256]{2,1,0:T(8,128)(2,1)S(1)}, u32[]{:S(2)}, u32[]{:S(2)}) %all-to-all-start) | async-done | bytes 983072 | tf_op jit(solution)/shard_map/all_to_all | solution.py:378
  29.8 0.1 shard_map.38
  29.8 2.0 %collective-permute-start.7 = (bf16[1280,256]{1,0:T(8,128)(2,1)S(1)}, bf16[1280,256]{1,0:T(8,128)(2,1)S(1)}, u32[]{:S(2)}, u32[]{:S(2)}) collective-permute-start(bf16[1280,256]{1,0:T(8,128)(2,1)S(1)} %get-tuple-element.26.refs_0_.refs_1_), channel_id=1, source_target_pairs={{0,16},{16,0},{1,17},{17,1},{2,18},{18,2},{3,19},{19,3},{4,20},{20... | collective-permute-start | bytes 1966088 | tf_op jit(solution)/shard_map/ppermute | solution.py:42
  31.8 0.0 collective-permute-done.5.refs_4_
  31.8 0.1 shard_map.41
  31.9 0.1 collective-permute-start.6
  32.0 0.0 collective-permute-done.10.refs_3_
  32.0 0.3 collective-permute-done.8.refs_1_
  32.4 4.0 %collective-permute-start.12 = (bf16[640,256]{1,0:T(8,128)(2,1)S(1)}, bf16[640,256]{1,0:T(8,128)(2,1)S(1)}, u32[]{:S(2)}, u32[]{:S(2)}) collective-permute-start(bf16[640,256]{1,0:T(8,128)(2,1)S(1)} %get-tuple-element.25.refs_0_), channel_id=1, source_target_pairs={{0,18},{18,0},{2,16},{16,2},{1,19},{19,1},{3,17},{17,3},{4,22},{22... | collective-permute-start | bytes 983048 | tf_op jit(solution)/shard_map/ppermute | solution.py:46
  36.4 0.0 collective-permute-done.6
  36.4 0.1 fusion
  36.5 4.2 %shard_map.43 = (bf16[176,256]{1,0:T(8,128)(2,1)S(1)}, bf16[176,256]{1,0:T(8,128)(2,1)S(1)}, bf16[176,256]{1,0:T(8,128)(2,1)S(1)}, bf16[176,256]{1,0:T(8,128)(2,1)S(1)}) custom-call(bf16[640,256]{1,0:T(8,128)(2,1)S(1)} %shard_map.42.refs_0_, bf16[1280,256]{1,0:T(8,128)(2,1)S(1)} %slice.14.refs_1_, bf16[1280,256]{1,0:T(8,128)(2,1)S(1)} %get-tuple-element.45.refs_2_), custom_call_target="tpu_custom_call" | custom-call | bytes 1310720 | tf_op jit(solution)/shard_map/pallas_call | solution.py:151
  40.7 1.6 %collective-permute-start.13 = (bf16[176,256]{1,0:T(8,128)(2,1)S(1)}, bf16[176,256]{1,0:T(8,128)(2,1)S(1)}, u32[]{:S(2)}, u32[]{:S(2)}) collective-permute-start(bf16[176,256]{1,0:T(8,128)(2,1)S(1)} %get-tuple-element.36), channel_id=1, source_target_pairs={{0,12},{4,0},{8,4},{12,8},{1,13},{5,1},{9,5},{13,9},{2,14},{6,2},{... | collective-permute-start | bytes 270344 | tf_op jit(solution)/shard_map/ppermute | solution.py:38
  42.3 0.5 collective-permute-start.14
  42.8 1.9 %collective-permute-start.15 = (bf16[176,256]{1,0:T(8,128)(2,1)S(1)}, bf16[176,256]{1,0:T(8,128)(2,1)S(1)}, u32[]{:S(2)}, u32[]{:S(2)}) collective-permute-start(bf16[176,256]{1,0:T(8,128)(2,1)S(1)} %get-tuple-element.38), channel_id=1, source_target_pairs={{0,8},{4,12},{8,0},{12,4},{1,9},{5,13},{9,1},{13,5},{2,10},{6,14},... | collective-permute-start | bytes 270344 | tf_op jit(solution)/shard_map/ppermute | solution.py:38
  44.8 0.3 collective-permute-start.11
  45.0 0.0 collective-permute-done.12.refs_0_
  45.1 4.1 %shard_map.45 = (f32[1280,256]{1,0:T(8,128)S(1)}, f32[1280,128]{1,0:T(8,128)S(1)}) custom-call(bf16[640,256]{1,0:T(8,128)(2,1)S(1)} %collective-permute-done.12.refs_0_, bf16[1280,256]{1,0:T(8,128)(2,1)S(1)} %get-tuple-element.26.refs_0_.refs_1_, bf16[1280,256]{1,0:T(8,128)(2,1)S(1)} %get-tuple-element.46.refs_2_, ...), custom_call_target="tpu_custom_call" | custom-call | flops 20000000000 | bytes 1310720 | tf_op jit(solution)/shard_map/pallas_call | solution.py:151
  49.2 0.2 collective-permute-done.14.refs_6_.refs_2_
  49.4 4.2 %shard_map.46.refs_5_ = bf16[656,256]{1,0:T(8,128)(2,1)S(1)} custom-call(bf16[640,256]{1,0:T(8,128)(2,1)S(1)} %collective-permute-done.12.refs_0_, bf16[1280,256]{1,0:T(8,128)(2,1)S(1)} %shard_map.44.refs_3_.refs_1_, bf16[1280,256]{1,0:T(8,128)(2,1)S(1)} %collective-permute-done.11.refs_2_.refs_4_, f32[1280,256]{1,0:T(8,128)S(1)} %get-tuple-element.34.refs_3_, ...), custom_call_target="tpu_custom_call" | custom-call | bytes 1310720 | tf_op jit(solution)/shard_map/pallas_call | solution.py:151
  53.6 3.7 %collective-permute-start.16 = (bf16[656,256]{1,0:T(8,128)(2,1)S(1)}, bf16[656,256]{1,0:T(8,128)(2,1)S(1)}, u32[]{:S(2)}, u32[]{:S(2)}) collective-permute-start(bf16[656,256]{1,0:T(8,128)(2,1)S(1)} %shard_map.46.refs_5_), channel_id=1, source_target_pairs={{0,18},{18,0},{2,16},{16,2},{1,19},{19,1},{3,17},{17,3},{4,22},{22... | collective-permute-start | bytes 1007624 | tf_op jit(solution)/shard_map/ppermute | solution.py:46
  57.3 0.5 shard_map.47
  57.8 7.6 %shard_map.48 = (f32[1280,256]{1,0:T(8,128)S(1)}, f32[1280,128]{1,0:T(8,128)S(1)}) custom-call(bf16[640,256]{1,0:T(8,128)(2,1)S(1)} %get-tuple-element.25.refs_0_, bf16[1280,256]{1,0:T(8,128)(2,1)S(1)} %get-tuple-element.26.refs_0_.refs_1_, bf16[1280,256]{1,0:T(8,128)(2,1)S(1)} %get-tuple-element.46.refs_2_, ...), custom_call_target="tpu_custom_call" | custom-call | bytes 2621440 | tf_op jit(solution)/shard_map/pallas_call | solution.py:151
  65.4 0.4 collective-permute-done.16.sent
  65.8 1.1 %shard_map.49 = bf16[640,256]{1,0:T(8,128)(2,1)} custom-call(f32[1280,256]{1,0:T(8,128)S(1)} %get-tuple-element.40.acc, f32[1280,128]{1,0:T(8,128)S(1)} %get-tuple-element.41.top, bf16[656,256]{1,0:T(8,128)(2,1)S(1)} %collective-permute-done.16.sent), custom_call_target="tpu_custom_call" | custom-call | bytes 1048576 | tf_op jit(solution)/shard_map/pallas_call | solution.py:330
  67.0 4.4 %all-to-all-start.1 = ((bf16[16,40,256]{2,1,0:T(8,128)(2,1)}), bf16[16,40,256]{2,1,0:T(8,128)(2,1)S(1)}, u32[]{:S(2)}, u32[]{:S(2)}) async-start(bf16[16,40,256]{2,1,0:T(8,128)(2,1)} %bitcast), calls=%async_computation.1 | async-start | bytes 655360 | tf_op jit(solution)/shard_map/all_to_all | solution.py:396
  71.4 3.1 %collective-permute-start.17 = (bf16[40,256]{1,0:T(8,128)(2,1)S(1)}, bf16[40,256]{1,0:T(8,128)(2,1)S(1)}, u32[]{:S(2)}, u32[]{:S(2)}) collective-permute-start(bf16[40,256]{1,0:T(8,128)(2,1)S(1)} %get-tuple-element.42), channel_id=1, source_target_pairs={{0,96},{32,0},{64,32},{96,64},{1,97},{33,1},{65,33},{97,65},{2,98}... | collective-permute-start | bytes 61448 | tf_op jit(solution)/shard_map/ppermute | solution.py:38
  74.6 2.3 %collective-permute-start.19 = (bf16[40,256]{1,0:T(8,128)(2,1)S(1)}, bf16[40,256]{1,0:T(8,128)(2,1)S(1)}, u32[]{:S(2)}, u32[]{:S(2)}) collective-permute-start(bf16[40,256]{1,0:T(8,128)(2,1)S(1)} %get-tuple-element.44), channel_id=1, source_target_pairs={{0,64},{32,96},{64,0},{96,32},{1,65},{33,97},{65,1},{97,33},{2,66}... | collective-permute-start | bytes 61448 | tf_op jit(solution)/shard_map/ppermute | solution.py:38
  76.9 0.8 %collective-permute-done.17.refs_1_ = bf16[40,256]{1,0:T(8,128)(2,1)S(1)} collective-permute-done((bf16[40,256]{1,0:T(8,128)(2,1)S(1)}, bf16[40,256]{1,0:T(8,128)(2,1)S(1)}, u32[]{:S(2)}, u32[]{:S(2)}) %collective-permute-start.17) | collective-permute-done | bytes 20512 | tf_op jit(solution)/shard_map/ppermute | solution.py:38
  77.7 1.9 %collective-permute-done.18.refs_2_ = bf16[40,256]{1,0:T(8,128)(2,1)S(1)} collective-permute-done((bf16[40,256]{1,0:T(8,128)(2,1)S(1)}, bf16[40,256]{1,0:T(8,128)(2,1)S(1)}, u32[]{:S(2)}, u32[]{:S(2)}) %collective-permute-start.18) | collective-permute-done | bytes 20512 | tf_op jit(solution)/shard_map/ppermute | solution.py:38
  79.5 0.3 collective-permute-done.19.refs_3_
  79.8 1.2 %all-to-all-done.1.main = bf16[16,40,256]{2,1,0:T(8,128)(2,1)S(1)} async-done(((bf16[16,40,256]{2,1,0:T(8,128)(2,1)}), bf16[16,40,256]{2,1,0:T(8,128)(2,1)S(1)}, u32[]{:S(2)}, u32[]{:S(2)}) %all-to-all-start.1) | async-done | bytes 327712 | tf_op jit(solution)/shard_map/all_to_all | solution.py:396
  81.0 0.8 %shard_map.50 = bf16[80,2560]{1,0:T(8,128)(2,1)} custom-call(bf16[16,40,256]{2,1,0:T(8,128)(2,1)S(1)} %all-to-all-done.1.main, bf16[40,256]{1,0:T(8,128)(2,1)S(1)} %get-tuple-element.39.refs_6_.refs_0_, bf16[40,256]{1,0:T(8,128)(2,1)S(1)} %collective-permute-done.17.refs_1_, bf16[40,256]{1,0:T(8,128)(2,1)S(1)} %collective-permute-done.18.refs_2_, ...), custom_call_target="tpu_custom_call" | custom-call | bytes 1048576 | tf_op jit(solution)/shard_map/pallas_call | solution.py:356
  (20 shorter events, 0.2 us)
Async XLA Ops:
  0.0 7.0 %copy-start.2 = (bf16[80,2560]{1,0:T(8,128)(2,1)S(1)}, bf16[80,2560]{1,0:T(8,128)(2,1)}, u32[]{:S(2)}) copy-start(bf16[80,2560]{1,0:T(8,128)(2,1)} %refs_2_.3) | copy-start | bytes 1228804
  0.0 7.0 %copy-start.1 = (bf16[80,2560]{1,0:T(8,128)(2,1)S(1)}, bf16[80,2560]{1,0:T(8,128)(2,1)}, u32[]{:S(2)}) copy-start(bf16[80,2560]{1,0:T(8,128)(2,1)} %refs_1_.3) | copy-start | bytes 1228804
  0.0 7.0 %copy-start = (bf16[80,2560]{1,0:T(8,128)(2,1)S(1)}, bf16[80,2560]{1,0:T(8,128)(2,1)}, u32[]{:S(2)}) copy-start(bf16[80,2560]{1,0:T(8,128)(2,1)} %refs_0_.3) | copy-start | bytes 1228804
  1.8 12.4 %collective-permute-start = (bf16[120,256]{1,0:T(8,128)(2,1)}, bf16[120,256]{1,0:T(8,128)(2,1)S(1)}, u32[]{:S(2)}, u32[]{:S(2)}) collective-permute-start(bf16[120,256]{1,0:T(8,128)(2,1)} %get-tuple-element.28), channel_id=1, source_target_pairs={{0,32},{32,64},{64,96},{96,0},{1,33},{33,65},{65,97},{97,1},{2,34}... | collective-permute-start | bytes 184328 | tf_op jit(solution)/shard_map/ppermute | solution.py:38
  3.5 10.7 %collective-permute-start.1 = (bf16[120,256]{1,0:T(8,128)(2,1)}, bf16[120,256]{1,0:T(8,128)(2,1)S(1)}, u32[]{:S(2)}, u32[]{:S(2)}) collective-permute-start(bf16[120,256]{1,0:T(8,128)(2,1)} %get-tuple-element.29), channel_id=1, source_target_pairs={{0,96},{32,0},{64,32},{96,64},{1,97},{33,1},{65,33},{97,65},{2,98}... | collective-permute-start | bytes 184328 | tf_op jit(solution)/shard_map/ppermute | solution.py:38
  5.1 9.1 %collective-permute-start.2 = (bf16[120,256]{1,0:T(8,128)(2,1)}, bf16[120,256]{1,0:T(8,128)(2,1)S(1)}, u32[]{:S(2)}, u32[]{:S(2)}) collective-permute-start(bf16[120,256]{1,0:T(8,128)(2,1)} %get-tuple-element.30), channel_id=1, source_target_pairs={{0,64},{32,96},{64,0},{96,32},{1,65},{33,97},{65,1},{97,33},{2,66}... | collective-permute-start | bytes 184328 | tf_op jit(solution)/shard_map/ppermute | solution.py:38
  8.3 5.9 %copy-start.3 = (bf16[120,256]{1,0:T(8,128)(2,1)S(1)}, bf16[120,256]{1,0:T(8,128)(2,1)}, u32[]{:S(2)}) copy-start(bf16[120,256]{1,0:T(8,128)(2,1)} %get-tuple-element.27.refs_0_) | copy-start | bytes 184324
  8.3 21.5 %all-to-all-start = ((bf16[16,120,256]{2,1,0:T(8,128)(2,1)}), bf16[16,120,256]{2,1,0:T(8,128)(2,1)S(1)}, u32[]{:S(2)}, u32[]{:S(2)}) async-start(bf16[16,120,256]{2,1,0:T(8,128)(2,1)} %shard_map.37), calls=%async_computation | async-start | bytes 1966080 | tf_op jit(solution)/shard_map/all_to_all | solution.py:378
  14.2 7.4 %collective-permute-start.3 = (bf16[320,256]{1,0:T(8,128)(2,1)S(1)}, bf16[320,256]{1,0:T(8,128)(2,1)S(1)}, u32[]{:S(2)}, u32[]{:S(2)}) collective-permute-start(bf16[320,256]{1,0:T(8,128)(2,1)S(1)} %get-tuple-element.31.refs_1_), channel_id=1, source_target_pairs={{0,16},{2,18},{16,2},{18,0},{1,17},{3,19},{17,3},{19,1},{4,20},{6,... | collective-permute-start | bytes 491528 | tf_op jit(solution)/shard_map/ppermute | solution.py:34
  16.2 13.6 %collective-permute-start.4 = (bf16[320,256]{1,0:T(8,128)(2,1)S(1)}, bf16[320,256]{1,0:T(8,128)(2,1)S(1)}, u32[]{:S(2)}, u32[]{:S(2)}) collective-permute-start(bf16[320,256]{1,0:T(8,128)(2,1)S(1)} %get-tuple-element.31.refs_1_), channel_id=1, source_target_pairs={{0,18},{2,16},{16,0},{18,2},{1,19},{3,17},{17,1},{19,3},{4,22},{6,... | collective-permute-start | bytes 491528 | tf_op jit(solution)/shard_map/ppermute | solution.py:34
  21.6 10.2 %collective-permute-start.5 = (bf16[320,256]{1,0:T(8,128)(2,1)S(1)}, bf16[320,256]{1,0:T(8,128)(2,1)S(1)}, u32[]{:S(2)}, u32[]{:S(2)}) collective-permute-start(bf16[320,256]{1,0:T(8,128)(2,1)S(1)} %collective-permute-done.3.refs_2_), channel_id=1, source_target_pairs={{0,16},{2,18},{16,2},{18,0},{1,17},{3,19},{17,3},{19,1},{4,20},{6,... | collective-permute-start | bytes 491528 | tf_op jit(solution)/shard_map/ppermute | solution.py:34
  21.6 10.4 %collective-permute-start.10 = (bf16[160,256]{1,0:T(8,128)(2,1)S(1)}, bf16[160,256]{1,0:T(8,128)(2,1)S(1)}, u32[]{:S(2)}, u32[]{:S(2)}) collective-permute-start(bf16[160,256]{1,0:T(8,128)(2,1)S(1)} %get-tuple-element.32.refs_0_), channel_id=1, source_target_pairs={{0,8},{4,12},{8,0},{12,4},{1,9},{5,13},{9,1},{13,5},{2,10},{6,14},... | collective-permute-start | bytes 245768 | tf_op jit(solution)/shard_map/ppermute | solution.py:38
  25.1 7.0 %collective-permute-start.9 = (bf16[160,256]{1,0:T(8,128)(2,1)S(1)}, bf16[160,256]{1,0:T(8,128)(2,1)S(1)}, u32[]{:S(2)}, u32[]{:S(2)}) collective-permute-start(bf16[160,256]{1,0:T(8,128)(2,1)S(1)} %get-tuple-element.32.refs_0_), channel_id=1, source_target_pairs={{0,12},{4,0},{8,4},{12,8},{1,13},{5,1},{9,5},{13,9},{2,14},{6,2},{... | collective-permute-start | bytes 245768 | tf_op jit(solution)/shard_map/ppermute | solution.py:38
  26.2 6.1 %collective-permute-start.8 = (bf16[160,256]{1,0:T(8,128)(2,1)S(1)}, bf16[160,256]{1,0:T(8,128)(2,1)S(1)}, u32[]{:S(2)}, u32[]{:S(2)}) collective-permute-start(bf16[160,256]{1,0:T(8,128)(2,1)S(1)} %get-tuple-element.32.refs_0_), channel_id=1, source_target_pairs={{0,4},{4,8},{8,12},{12,0},{1,5},{5,9},{9,13},{13,1},{2,6},{6,10},{... | collective-permute-start | bytes 245768 | tf_op jit(solution)/shard_map/ppermute | solution.py:38
  29.8 14.9 %collective-permute-start.7 = (bf16[1280,256]{1,0:T(8,128)(2,1)S(1)}, bf16[1280,256]{1,0:T(8,128)(2,1)S(1)}, u32[]{:S(2)}, u32[]{:S(2)}) collective-permute-start(bf16[1280,256]{1,0:T(8,128)(2,1)S(1)} %get-tuple-element.26.refs_0_.refs_1_), channel_id=1, source_target_pairs={{0,16},{16,0},{1,17},{17,1},{2,18},{18,2},{3,19},{19,3},{4,20},{20... | collective-permute-start | bytes 1966088 | tf_op jit(solution)/shard_map/ppermute | solution.py:42
  31.9 4.5 %collective-permute-start.6 = (bf16[2560,256]{1,0:T(8,128)(2,1)S(1)}, bf16[2560,256]{1,0:T(8,128)(2,1)S(1)}, u32[]{:S(2)}, u32[]{:S(2)}) collective-permute-start(bf16[2560,256]{1,0:T(8,128)(2,1)S(1)} %shard_map.41), channel_id=1, source_target_pairs={{0,1},{1,0},{2,3},{3,2},{4,5},{5,4},{6,7},{7,6},{8,9},{9,8},{10,11... | collective-permute-start | bytes 3932168 | tf_op jit(solution)/shard_map/ppermute | solution.py:50
  32.4 12.7 %collective-permute-start.12 = (bf16[640,256]{1,0:T(8,128)(2,1)S(1)}, bf16[640,256]{1,0:T(8,128)(2,1)S(1)}, u32[]{:S(2)}, u32[]{:S(2)}) collective-permute-start(bf16[640,256]{1,0:T(8,128)(2,1)S(1)} %get-tuple-element.25.refs_0_), channel_id=1, source_target_pairs={{0,18},{18,0},{2,16},{16,2},{1,19},{19,1},{3,17},{17,3},{4,22},{22... | collective-permute-start | bytes 983048 | tf_op jit(solution)/shard_map/ppermute | solution.py:46
  40.7 8.5 %collective-permute-start.13 = (bf16[176,256]{1,0:T(8,128)(2,1)S(1)}, bf16[176,256]{1,0:T(8,128)(2,1)S(1)}, u32[]{:S(2)}, u32[]{:S(2)}) collective-permute-start(bf16[176,256]{1,0:T(8,128)(2,1)S(1)} %get-tuple-element.36), channel_id=1, source_target_pairs={{0,12},{4,0},{8,4},{12,8},{1,13},{5,1},{9,5},{13,9},{2,14},{6,2},{... | collective-permute-start | bytes 270344 | tf_op jit(solution)/shard_map/ppermute | solution.py:38
  42.3 7.1 %collective-permute-start.14 = (bf16[176,256]{1,0:T(8,128)(2,1)S(1)}, bf16[176,256]{1,0:T(8,128)(2,1)S(1)}, u32[]{:S(2)}, u32[]{:S(2)}) collective-permute-start(bf16[176,256]{1,0:T(8,128)(2,1)S(1)} %get-tuple-element.37), channel_id=1, source_target_pairs={{0,4},{4,8},{8,12},{12,0},{1,5},{5,9},{9,13},{13,1},{2,6},{6,10},{... | collective-permute-start | bytes 270344 | tf_op jit(solution)/shard_map/ppermute | solution.py:38
  42.8 6.6 %collective-permute-start.15 = (bf16[176,256]{1,0:T(8,128)(2,1)S(1)}, bf16[176,256]{1,0:T(8,128)(2,1)S(1)}, u32[]{:S(2)}, u32[]{:S(2)}) collective-permute-start(bf16[176,256]{1,0:T(8,128)(2,1)S(1)} %get-tuple-element.38), channel_id=1, source_target_pairs={{0,8},{4,12},{8,0},{12,4},{1,9},{5,13},{9,1},{13,5},{2,10},{6,14},... | collective-permute-start | bytes 270344 | tf_op jit(solution)/shard_map/ppermute | solution.py:38
  44.8 4.6 %collective-permute-start.11 = (bf16[1280,256]{1,0:T(8,128)(2,1)S(1)}, bf16[1280,256]{1,0:T(8,128)(2,1)S(1)}, u32[]{:S(2)}, u32[]{:S(2)}) collective-permute-start(bf16[1280,256]{1,0:T(8,128)(2,1)S(1)} %shard_map.44.refs_3_.refs_1_), channel_id=1, source_target_pairs={{0,1},{1,0},{2,3},{3,2},{4,5},{5,4},{6,7},{7,6},{8,9},{9,8},{10,11... | collective-permute-start | bytes 1966088 | tf_op jit(solution)/shard_map/ppermute | solution.py:50
  53.6 12.2 %collective-permute-start.16 = (bf16[656,256]{1,0:T(8,128)(2,1)S(1)}, bf16[656,256]{1,0:T(8,128)(2,1)S(1)}, u32[]{:S(2)}, u32[]{:S(2)}) collective-permute-start(bf16[656,256]{1,0:T(8,128)(2,1)S(1)} %shard_map.46.refs_5_), channel_id=1, source_target_pairs={{0,18},{18,0},{2,16},{16,2},{1,19},{19,1},{3,17},{17,3},{4,22},{22... | collective-permute-start | bytes 1007624 | tf_op jit(solution)/shard_map/ppermute | solution.py:46
  67.0 14.1 %all-to-all-start.1 = ((bf16[16,40,256]{2,1,0:T(8,128)(2,1)}), bf16[16,40,256]{2,1,0:T(8,128)(2,1)S(1)}, u32[]{:S(2)}, u32[]{:S(2)}) async-start(bf16[16,40,256]{2,1,0:T(8,128)(2,1)} %bitcast), calls=%async_computation.1 | async-start | bytes 655360 | tf_op jit(solution)/shard_map/all_to_all | solution.py:396
  71.4 6.3 %collective-permute-start.17 = (bf16[40,256]{1,0:T(8,128)(2,1)S(1)}, bf16[40,256]{1,0:T(8,128)(2,1)S(1)}, u32[]{:S(2)}, u32[]{:S(2)}) collective-permute-start(bf16[40,256]{1,0:T(8,128)(2,1)S(1)} %get-tuple-element.42), channel_id=1, source_target_pairs={{0,96},{32,0},{64,32},{96,64},{1,97},{33,1},{65,33},{97,65},{2,98}... | collective-permute-start | bytes 61448 | tf_op jit(solution)/shard_map/ppermute | solution.py:38
  74.6 5.0 %collective-permute-start.18 = (bf16[40,256]{1,0:T(8,128)(2,1)S(1)}, bf16[40,256]{1,0:T(8,128)(2,1)S(1)}, u32[]{:S(2)}, u32[]{:S(2)}) collective-permute-start(bf16[40,256]{1,0:T(8,128)(2,1)S(1)} %get-tuple-element.43), channel_id=1, source_target_pairs={{0,32},{32,64},{64,96},{96,0},{1,33},{33,65},{65,97},{97,1},{2,34}... | collective-permute-start | bytes 61448 | tf_op jit(solution)/shard_map/ppermute | solution.py:38
  74.6 5.3 %collective-permute-start.19 = (bf16[40,256]{1,0:T(8,128)(2,1)S(1)}, bf16[40,256]{1,0:T(8,128)(2,1)S(1)}, u32[]{:S(2)}, u32[]{:S(2)}) collective-permute-start(bf16[40,256]{1,0:T(8,128)(2,1)S(1)} %get-tuple-element.44), channel_id=1, source_target_pairs={{0,64},{32,96},{64,0},{96,32},{1,65},{33,97},{65,1},{97,33},{2,66}... | collective-permute-start | bytes 61448 | tf_op jit(solution)/shard_map/ppermute | solution.py:38

commit v5 on v4

--- a/solution.py
+++ b/solution.py
@@ -280,19 +280,20 @@
 def stack_kernel(*refs):
     out, start = refs[-1], 0
     for ref in refs[:-1]:
-        out[start : start + ref.shape[0], :] = ref[...]
-        start += ref.shape[0]
-
-
-def stack(*pieces, flops=0):
+        if start < out.shape[0]:
+            out[start : start + ref.shape[0], :] = ref[...]
+            start += ref.shape[0]
+
+
+def stack(*pieces, after=(), flops=0):
     return pl.pallas_call(
         stack_kernel,
         out_shape=jax.ShapeDtypeStruct((sum(piece.shape[0] for piece in pieces), PAIR), jnp.bfloat16),
-        in_specs=[VMEM] * len(pieces),
+        in_specs=[VMEM] * len(pieces) + [HBM] * len(after),
         out_specs=VMEM,
         compiler_params=pltpu.CompilerParams(vmem_limit_bytes=12 * 2**20),
         cost_estimate=pl.CostEstimate(flops=flops, bytes_accessed=2**20, transcendentals=0),
-    )(*pieces)
+    )(*pieces, *after)
 
 
 def hold_kernel(a, *refs):
@@ -310,7 +311,8 @@
     )(a, *after)
 
 
-def merge_kernel(acc, top, sent, out):
+def merge_kernel(acc, top, sent, *refs):
+    out = refs[-1]
     rows = out.shape[0]
     blocks = rows // HEAD_DIM
     for half in range(2):
@@ -326,15 +328,15 @@
             out[there, lanes] = (summed / (acc[here, HEAD_DIM:] * share + other)).astype(jnp.bfloat16)
 
 
-def merge(acc, top, sent):
+def merge(acc, top, sent, *after):
     return pl.pallas_call(
         merge_kernel,
         out_shape=jax.ShapeDtypeStruct((acc.shape[0] // 2, PAIR), jnp.bfloat16),
-        in_specs=[VMEM] * 3,
+        in_specs=[VMEM] * 3 + [HBM] * len(after),
         out_specs=VMEM,
         compiler_params=pltpu.CompilerParams(vmem_limit_bytes=12 * 2**20),
         cost_estimate=pl.CostEstimate(flops=0, bytes_accessed=2**20, transcendentals=0),
-    )(acc, top, sent)
+    )(acc, top, sent, *after)
 
 
 def unpack_kernel(main, *refs):
@@ -379,20 +381,22 @@
     kv, q = sort(got)
     near = key_partner(kv)
     near_q = query_partner(q)
-    both, xq = stack(kv, *xkvs), stack(*xqs, flops=2 * 10**10)
+    both = stack(kv, *xkvs)
     other = other_core(both)
 
     rows = kv.shape[0]
-    parts = attend(xq, [both[rows:], other[rows:]], None, "part")
+    own = attend(q, [kv, other[:rows]], None, None)
+    xq = stack(*xqs, flops=2 * 10**10)
+    parts = attend(xq, [both[rows:], other[rows:]], None, "part", own[:1])
+
+    near = hold(near, parts[0], near_q)
+    near_other = other_core(near)
+    state = attend(near_q, [kv, other[:rows]], None, None, (near,))
+    sent = attend(near_q, [near, near_other], state, "send")
     back = [along("y", part, -step) for part, step in zip(parts[1:], STEPS, strict=True)]
+    own = attend(q, [near, near_other], own, None, (sent,))
+    out = merge(*own, query_partner(sent), *back)
     xout = combine([parts[0], *back])
-
-    near = hold(near, parts[0])
-    near_other = other_core(near)
-    state = attend(near_q, [kv, other[:rows]], None, None, (near,), flops=2 * 10**10)
-    sent = attend(near_q, [near, near_other], state, "send", back)
-    state = attend(q, [kv, other[:rows], near, near_other], None, None, (sent, xout[0]))
-    out = merge(*state, query_partner(sent))
     out = lax.all_to_all(out.reshape(COLUMNS, Q_ROWS, PAIR), ("x", "y"), 0, 0, tiled=True)
     xout = [xout[0]] + [along("x", a, -step) for a, step in zip(xout[1:], STEPS, strict=True)]
     return unpack(out, xout)

time: 82.2 us -> 81.8 us (level)
  starting transfers between devices: 44.7 us -> 43.6 us
    ppermute x12, waiting for transfers between devices: 3.44 us -> 4.57 us  [along(): return lax.ppermute(a, axis, [(i, (i + step) % 4) for i in range(4)])]
    ppermute x12, starting transfers between devices: 20.1 us -> 19.1 us  [along(): return lax.ppermute(a, axis, [(i, (i + step) % 4) for i in range(4)])]
    all_to_all x1, waiting for transfers between devices: 1.21 us -> 0.32 us  [local(): lax.all_to_all(out.reshape(COLUMNS, Q_ROWS, PAIR), ('x', 'y'), 0, 0, tile...]
    pallas_call x4 -> x5, Pallas kernels: 20.1 us -> 20.8 us  [attend(): pl.pallas_call(functools.partial(attend_kernel, len(kvs), len(after), sta...]
  transfers between devices with their start and end apart: 22 -> 22, of which waited for: 9 -> 9; matrix products, arithmetic and copies ran while one was open for 0% -> 0% of each run, Pallas kernels for 22% -> 23%
where the time goes in v5:
time: 81.8 us; the launch traced here: 81.4 us
  starting transfers between devices  43.6 us (53%)
  Pallas kernels  26.6 us (33%)
  waiting for transfers between devices  10.9 us (13%)
    pallas_call x5, Pallas kernels, attend(): pl.pallas_call(functools.partial(attend_kernel, len(kvs), len(after), sta...  20.8 us
    ppermute x12, starting transfers between devices, along(): return lax.ppermute(a, axis, [(i, (i + step) % 4) for i in range(4)])  19.1 us
    ppermute x2, starting transfers between devices, query_partner(): return lax.ppermute(a, ('zl', 'zh'), [(0, 3), (3, 0), (1, 2), (2, 1)])  7.55 us
    all_to_all x1, starting transfers between devices, local(): got = lax.all_to_all(sent, ('x', 'y'), 0, 0, tiled=True)  5.87 us
    ppermute x12, waiting for transfers between devices, along(): return lax.ppermute(a, axis, [(i, (i + step) % 4) for i in range(4)])  4.57 us
    all_to_all x1, starting transfers between devices, local(): lax.all_to_all(out.reshape(COLUMNS, Q_ROWS, PAIR), ('x', 'y'), 0, 0, tile...  4.46 us
    ppermute x3, starting transfers between devices, along_z(): return lax.ppermute(a, ('zl', 'zh'), pairs)  4.19 us
    ppermute x3, waiting for transfers between devices, along_z(): return lax.ppermute(a, ('zl', 'zh'), pairs)  3.22 us
  transfers between devices with their start and end apart: 22, of which 9 were waited for; matrix products, arithmetic and copies ran while one was open for 0% of the time, Pallas kernels for 23%

profile of v5, /device:TPU:0, one launch (start us, length us, event | category | flops | bytes accessed | tf_op | source)
XLA Modules:
  0.0 81.4 jit_solution(780412513139003454)
XLA Ops:
  0.0 1.8 %shard_map.39 = (bf16[120,256]{1,0:T(8,128)(2,1)}, bf16[120,256]{1,0:T(8,128)(2,1)}, bf16[120,256]{1,0:T(8,128)(2,1)}, bf16[120,256]{1,0:T(8,128)(2,1)}) custom-call(bf16[80,2560]{1,0:T(8,128)(2,1)} %refs_0_.3, bf16[80,2560]{1,0:T(8,128)(2,1)} %refs_1_.3, bf16[80,2560]{1,0:T(8,128)(2,1)} %refs_2_.3), custom_call_target="tpu_custom_call" | custom-call | bytes 1048576 | tf_op jit(solution)/shard_map/pallas_call | solution.py:234
  1.8 1.6 %collective-permute-start.1 = (bf16[120,256]{1,0:T(8,128)(2,1)}, bf16[120,256]{1,0:T(8,128)(2,1)S(1)}, u32[]{:S(2)}, u32[]{:S(2)}) collective-permute-start(bf16[120,256]{1,0:T(8,128)(2,1)} %get-tuple-element.30), channel_id=1, source_target_pairs={{0,32},{32,64},{64,96},{96,0},{1,33},{33,65},{65,97},{97,1},{2,34}... | collective-permute-start | bytes 184328 | tf_op jit(solution)/shard_map/ppermute | solution.py:38
  3.5 1.7 %collective-permute-start.2 = (bf16[120,256]{1,0:T(8,128)(2,1)}, bf16[120,256]{1,0:T(8,128)(2,1)S(1)}, u32[]{:S(2)}, u32[]{:S(2)}) collective-permute-start(bf16[120,256]{1,0:T(8,128)(2,1)} %get-tuple-element.31), channel_id=1, source_target_pairs={{0,96},{32,0},{64,32},{96,64},{1,97},{33,1},{65,33},{97,65},{2,98}... | collective-permute-start | bytes 184328 | tf_op jit(solution)/shard_map/ppermute | solution.py:38
  5.1 1.9 %collective-permute-start.3 = (bf16[120,256]{1,0:T(8,128)(2,1)}, bf16[120,256]{1,0:T(8,128)(2,1)S(1)}, u32[]{:S(2)}, u32[]{:S(2)}) collective-permute-start(bf16[120,256]{1,0:T(8,128)(2,1)} %get-tuple-element.32), channel_id=1, source_target_pairs={{0,64},{32,96},{64,0},{96,32},{1,65},{33,97},{65,1},{97,33},{2,66}... | collective-permute-start | bytes 184328 | tf_op jit(solution)/shard_map/ppermute | solution.py:38
  7.0 1.2 %shard_map.37 = bf16[16,120,256]{2,1,0:T(8,128)(2,1)} custom-call(bf16[80,2560]{1,0:T(8,128)(2,1)S(1)} %copy-done, bf16[80,2560]{1,0:T(8,128)(2,1)S(1)} %copy-done.1, bf16[80,2560]{1,0:T(8,128)(2,1)S(1)} %copy-done.2), custom_call_target="tpu_custom_call" | custom-call | bytes 1048576 | tf_op jit(solution)/shard_map/pallas_call | solution.py:234
  8.3 0.0 copy-start.3
  8.3 5.9 %all-to-all-start = ((bf16[16,120,256]{2,1,0:T(8,128)(2,1)}), bf16[16,120,256]{2,1,0:T(8,128)(2,1)S(1)}, u32[]{:S(2)}, u32[]{:S(2)}) async-start(bf16[16,120,256]{2,1,0:T(8,128)(2,1)} %shard_map.37), calls=%async_computation | async-start | bytes 1966080 | tf_op jit(solution)/shard_map/all_to_all | solution.py:380
  14.2 0.0 collective-permute-done.2.refs_2_
  14.2 0.0 collective-permute-done.3.refs_3_
  14.2 2.0 %collective-permute-start.7 = (bf16[320,256]{1,0:T(8,128)(2,1)S(1)}, bf16[320,256]{1,0:T(8,128)(2,1)S(1)}, u32[]{:S(2)}, u32[]{:S(2)}) collective-permute-start(bf16[320,256]{1,0:T(8,128)(2,1)S(1)} %get-tuple-element.34.refs_1_), channel_id=1, source_target_pairs={{0,16},{2,18},{16,2},{18,0},{1,17},{3,19},{17,3},{19,1},{4,20},{6,... | collective-permute-start | bytes 491528 | tf_op jit(solution)/shard_map/ppermute | solution.py:34
  16.2 2.2 %collective-permute-start.8 = (bf16[320,256]{1,0:T(8,128)(2,1)S(1)}, bf16[320,256]{1,0:T(8,128)(2,1)S(1)}, u32[]{:S(2)}, u32[]{:S(2)}) collective-permute-start(bf16[320,256]{1,0:T(8,128)(2,1)S(1)} %get-tuple-element.34.refs_1_), channel_id=1, source_target_pairs={{0,18},{2,16},{16,0},{18,2},{1,19},{3,17},{17,1},{19,3},{4,22},{6,... | collective-permute-start | bytes 491528 | tf_op jit(solution)/shard_map/ppermute | solution.py:34
  18.4 3.2 %collective-permute-done.7.refs_2_ = bf16[320,256]{1,0:T(8,128)(2,1)S(1)} collective-permute-done((bf16[320,256]{1,0:T(8,128)(2,1)S(1)}, bf16[320,256]{1,0:T(8,128)(2,1)S(1)}, u32[]{:S(2)}, u32[]{:S(2)}) %collective-permute-start.7) | collective-permute-done | bytes 163872 | tf_op jit(solution)/shard_map/ppermute | solution.py:34
  21.7 3.4 %collective-permute-start.6 = (bf16[160,256]{1,0:T(8,128)(2,1)S(1)}, bf16[160,256]{1,0:T(8,128)(2,1)S(1)}, u32[]{:S(2)}, u32[]{:S(2)}) collective-permute-start(bf16[160,256]{1,0:T(8,128)(2,1)S(1)} %get-tuple-element.33.refs_0_), channel_id=1, source_target_pairs={{0,8},{4,12},{8,0},{12,4},{1,9},{5,13},{9,1},{13,5},{2,10},{6,14},... | collective-permute-start | bytes 245768 | tf_op jit(solution)/shard_map/ppermute | solution.py:38
  25.1 1.2 %collective-permute-start.5 = (bf16[160,256]{1,0:T(8,128)(2,1)S(1)}, bf16[160,256]{1,0:T(8,128)(2,1)S(1)}, u32[]{:S(2)}, u32[]{:S(2)}) collective-permute-start(bf16[160,256]{1,0:T(8,128)(2,1)S(1)} %get-tuple-element.33.refs_0_), channel_id=1, source_target_pairs={{0,12},{4,0},{8,4},{12,8},{1,13},{5,1},{9,5},{13,9},{2,14},{6,2},{... | collective-permute-start | bytes 245768 | tf_op jit(solution)/shard_map/ppermute | solution.py:38
  26.2 0.9 %collective-permute-start.4 = (bf16[160,256]{1,0:T(8,128)(2,1)S(1)}, bf16[160,256]{1,0:T(8,128)(2,1)S(1)}, u32[]{:S(2)}, u32[]{:S(2)}) collective-permute-start(bf16[160,256]{1,0:T(8,128)(2,1)S(1)} %get-tuple-element.33.refs_0_), channel_id=1, source_target_pairs={{0,4},{4,8},{8,12},{12,0},{1,5},{5,9},{9,13},{13,1},{2,6},{6,10},{... | collective-permute-start | bytes 245768 | tf_op jit(solution)/shard_map/ppermute | solution.py:38
  27.1 2.7 %all-to-all-done.got = bf16[16,120,256]{2,1,0:T(8,128)(2,1)S(1)} async-done(((bf16[16,120,256]{2,1,0:T(8,128)(2,1)}), bf16[16,120,256]{2,1,0:T(8,128)(2,1)S(1)}, u32[]{:S(2)}, u32[]{:S(2)}) %all-to-all-start) | async-done | bytes 983072 | tf_op jit(solution)/shard_map/all_to_all | solution.py:380
  29.8 0.1 shard_map.38
  29.8 0.0 collective-permute-done.8.refs_3_
  29.8 2.0 %collective-permute-start = (bf16[1280,256]{1,0:T(8,128)(2,1)S(1)}, bf16[1280,256]{1,0:T(8,128)(2,1)S(1)}, u32[]{:S(2)}, u32[]{:S(2)}) collective-permute-start(bf16[1280,256]{1,0:T(8,128)(2,1)S(1)} %get-tuple-element.28.refs_0_.refs_1_), channel_id=1, source_target_pairs={{0,16},{16,0},{1,17},{17,1},{2,18},{18,2},{3,19},{19,3},{4,20},{20... | collective-permute-start | bytes 1966088 | tf_op jit(solution)/shard_map/ppermute | solution.py:42
  31.8 0.1 shard_map.42
  31.9 0.1 collective-permute-start.10
  32.0 0.0 collective-permute-done.6.refs_3_
  32.0 0.3 collective-permute-done.4.refs_1_
  32.4 4.2 %collective-permute-start.11 = (bf16[640,256]{1,0:T(8,128)(2,1)S(1)}, bf16[640,256]{1,0:T(8,128)(2,1)S(1)}, u32[]{:S(2)}, u32[]{:S(2)}) collective-permute-start(bf16[640,256]{1,0:T(8,128)(2,1)S(1)} %get-tuple-element.27.refs_0_), channel_id=1, source_target_pairs={{0,18},{18,0},{2,16},{16,2},{1,19},{19,1},{3,17},{17,3},{4,22},{22... | collective-permute-start | bytes 983048 | tf_op jit(solution)/shard_map/ppermute | solution.py:46
  36.6 0.0 collective-permute-done.10
  36.6 0.1 fusion
  36.7 4.1 %shard_map.43 = (f32[1280,256]{1,0:T(8,128)S(1)}, f32[1280,128]{1,0:T(8,128)S(1)}) custom-call(bf16[640,256]{1,0:T(8,128)(2,1)S(1)} %get-tuple-element.27.refs_0_, bf16[1280,256]{1,0:T(8,128)(2,1)S(1)} %get-tuple-element.28.refs_0_.refs_1_, bf16[1280,256]{1,0:T(8,128)(2,1)S(1)} %get-tuple-element.49.refs_2_), custom_call_target="tpu_custom_call" | custom-call | bytes 1310720 | tf_op jit(solution)/shard_map/pallas_call | solution.py:151
  40.8 4.2 %shard_map.44 = (bf16[176,256]{1,0:T(8,128)(2,1)S(1)}, bf16[176,256]{1,0:T(8,128)(2,1)S(1)}, bf16[176,256]{1,0:T(8,128)(2,1)S(1)}, bf16[176,256]{1,0:T(8,128)(2,1)S(1)}) custom-call(bf16[640,256]{1,0:T(8,128)(2,1)S(1)} %shard_map.41.refs_0_, bf16[1280,256]{1,0:T(8,128)(2,1)S(1)} %slice.13.refs_1_, bf16[1280,256]{1,0:T(8,128)(2,1)S(1)} %get-tuple-element.50.refs_2_, ...), custom_call_target="tpu_custom_call" | custom-call | bytes 1310720 | tf_op jit(solution)/shard_map/pallas_call | solution.py:151
  45.0 0.3 collective-permute-start.12
  45.4 4.1 %shard_map.46 = (f32[1280,256]{1,0:T(8,128)S(1)}, f32[1280,128]{1,0:T(8,128)S(1)}) custom-call(bf16[640,256]{1,0:T(8,128)(2,1)S(1)} %collective-permute-done.11.refs_1_.refs_0_, bf16[1280,256]{1,0:T(8,128)(2,1)S(1)} %get-tuple-element.28.refs_0_.refs_1_, bf16[1280,256]{1,0:T(8,128)(2,1)S(1)} %get-tuple-element.49.refs_2_, ...), custom_call_target="tpu_custom_call" | custom-call | bytes 1310720 | tf_op jit(solution)/shard_map/pallas_call | solution.py:151
  49.5 4.3 %shard_map.47.refs_5_ = bf16[656,256]{1,0:T(8,128)(2,1)S(1)} custom-call(bf16[640,256]{1,0:T(8,128)(2,1)S(1)} %collective-permute-done.11.refs_1_.refs_0_, bf16[1280,256]{1,0:T(8,128)(2,1)S(1)} %shard_map.45.refs_3_.refs_1_, bf16[1280,256]{1,0:T(8,128)(2,1)S(1)} %collective-permute-done.12.refs_2_, f32[1280,256]{1,0:T(8,128)S(1)} %get-tuple-element.38.refs_3_, ...), custom_call_target="tpu_custom_call" | custom-call | bytes 1310720 | tf_op jit(solution)/shard_map/pallas_call | solution.py:151
  53.7 3.4 %collective-permute-start.13 = (bf16[656,256]{1,0:T(8,128)(2,1)S(1)}, bf16[656,256]{1,0:T(8,128)(2,1)S(1)}, u32[]{:S(2)}, u32[]{:S(2)}) collective-permute-start(bf16[656,256]{1,0:T(8,128)(2,1)S(1)} %shard_map.47.refs_5_), channel_id=1, source_target_pairs={{0,18},{18,0},{2,16},{16,2},{1,19},{19,1},{3,17},{17,3},{4,22},{22... | collective-permute-start | bytes 1007624 | tf_op jit(solution)/shard_map/ppermute | solution.py:46
  57.1 0.7 collective-permute-start.14
  57.8 1.3 %collective-permute-start.15 = (bf16[176,256]{1,0:T(8,128)(2,1)S(1)}, bf16[176,256]{1,0:T(8,128)(2,1)S(1)}, u32[]{:S(2)}, u32[]{:S(2)}) collective-permute-start(bf16[176,256]{1,0:T(8,128)(2,1)S(1)} %get-tuple-element.43), channel_id=1, source_target_pairs={{0,4},{4,8},{8,12},{12,0},{1,5},{5,9},{9,13},{13,1},{2,6},{6,10},{... | collective-permute-start | bytes 270344 | tf_op jit(solution)/shard_map/ppermute | solution.py:38
  59.1 0.9 %collective-permute-start.16 = (bf16[176,256]{1,0:T(8,128)(2,1)S(1)}, bf16[176,256]{1,0:T(8,128)(2,1)S(1)}, u32[]{:S(2)}, u32[]{:S(2)}) collective-permute-start(bf16[176,256]{1,0:T(8,128)(2,1)S(1)} %get-tuple-element.44), channel_id=1, source_target_pairs={{0,8},{4,12},{8,0},{12,4},{1,9},{5,13},{9,1},{13,5},{2,10},{6,14},... | collective-permute-start | bytes 270344 | tf_op jit(solution)/shard_map/ppermute | solution.py:38
  60.0 4.2 %shard_map.48 = (f32[1280,256]{1,0:T(8,128)S(1)}, f32[1280,128]{1,0:T(8,128)S(1)}) custom-call(bf16[640,256]{1,0:T(8,128)(2,1)S(1)} %get-tuple-element.27.refs_0_, bf16[1280,256]{1,0:T(8,128)(2,1)S(1)} %shard_map.45.refs_3_.refs_1_, bf16[1280,256]{1,0:T(8,128)(2,1)S(1)} %collective-permute-done.12.refs_2_, f32[1280,256]{1,0:T(8,128)S(1)} %get-tuple-element.35.refs_3_, ...), custom_call_target="tpu_custom_call" | custom-call | bytes 1310720 | tf_op jit(solution)/shard_map/pallas_call | solution.py:151
  64.2 1.3 %collective-permute-done.15.refs_1_.refs_2_ = bf16[176,256]{1,0:T(8,128)(2,1)S(1)} collective-permute-done((bf16[176,256]{1,0:T(8,128)(2,1)S(1)}, bf16[176,256]{1,0:T(8,128)(2,1)S(1)}, u32[]{:S(2)}, u32[]{:S(2)}) %collective-permute-start.15) | collective-permute-done | bytes 90144 | tf_op jit(solution)/shard_map/ppermute | solution.py:38
  65.5 0.1 collective-permute-done.13.sent
  65.6 1.1 %shard_map.49 = bf16[640,256]{1,0:T(8,128)(2,1)} custom-call(f32[1280,256]{1,0:T(8,128)S(1)} %get-tuple-element.40.acc, f32[1280,128]{1,0:T(8,128)S(1)} %get-tuple-element.41.top, bf16[656,256]{1,0:T(8,128)(2,1)S(1)} %collective-permute-done.13.sent, bf16[176,256]{1,0:T(8,128)(2,1)S(1)} %collective-permute-done.14.refs_0_.refs_1_, ...), custom_call_target="tpu_custom_call" | custom-call | bytes 1048576 | tf_op jit(solution)/shard_map/pallas_call | solution.py:332
  66.8 4.5 %all-to-all-start.1 = ((bf16[16,40,256]{2,1,0:T(8,128)(2,1)}), bf16[16,40,256]{2,1,0:T(8,128)(2,1)S(1)}, u32[]{:S(2)}, u32[]{:S(2)}) async-start(bf16[16,40,256]{2,1,0:T(8,128)(2,1)} %bitcast), calls=%async_computation.1 | async-start | bytes 655360 | tf_op jit(solution)/shard_map/all_to_all | solution.py:400
  71.2 0.5 shard_map.50
  71.8 3.2 %collective-permute-start.17 = (bf16[40,256]{1,0:T(8,128)(2,1)S(1)}, bf16[40,256]{1,0:T(8,128)(2,1)S(1)}, u32[]{:S(2)}, u32[]{:S(2)}) collective-permute-start(bf16[40,256]{1,0:T(8,128)(2,1)S(1)} %get-tuple-element.46), channel_id=1, source_target_pairs={{0,96},{32,0},{64,32},{96,64},{1,97},{33,1},{65,33},{97,65},{2,98}... | collective-permute-start | bytes 61448 | tf_op jit(solution)/shard_map/ppermute | solution.py:38
  75.0 2.3 %collective-permute-start.19 = (bf16[40,256]{1,0:T(8,128)(2,1)S(1)}, bf16[40,256]{1,0:T(8,128)(2,1)S(1)}, u32[]{:S(2)}, u32[]{:S(2)}) collective-permute-start(bf16[40,256]{1,0:T(8,128)(2,1)S(1)} %get-tuple-element.48), channel_id=1, source_target_pairs={{0,64},{32,96},{64,0},{96,32},{1,65},{33,97},{65,1},{97,33},{2,66}... | collective-permute-start | bytes 61448 | tf_op jit(solution)/shard_map/ppermute | solution.py:38
  77.3 0.2 collective-permute-done.17.refs_1_
  77.5 2.5 %collective-permute-done.18.refs_2_ = bf16[40,256]{1,0:T(8,128)(2,1)S(1)} collective-permute-done((bf16[40,256]{1,0:T(8,128)(2,1)S(1)}, bf16[40,256]{1,0:T(8,128)(2,1)S(1)}, u32[]{:S(2)}, u32[]{:S(2)}) %collective-permute-start.18) | collective-permute-done | bytes 20512 | tf_op jit(solution)/shard_map/ppermute | solution.py:38
  80.0 0.3 collective-permute-done.19.refs_3_
  80.3 0.3 all-to-all-done.1.main
  80.6 0.8 %shard_map.51 = bf16[80,2560]{1,0:T(8,128)(2,1)} custom-call(bf16[16,40,256]{2,1,0:T(8,128)(2,1)S(1)} %all-to-all-done.1.main, bf16[40,256]{1,0:T(8,128)(2,1)S(1)} %get-tuple-element.45.refs_0_, bf16[40,256]{1,0:T(8,128)(2,1)S(1)} %collective-permute-done.17.refs_1_, bf16[40,256]{1,0:T(8,128)(2,1)S(1)} %collective-permute-done.18.refs_2_, ...), custom_call_target="tpu_custom_call" | custom-call | bytes 1048576 | tf_op jit(solution)/shard_map/pallas_call | solution.py:358
  (21 shorter events, 0.2 us)
Async XLA Ops:
  0.0 7.0 %copy-start.2 = (bf16[80,2560]{1,0:T(8,128)(2,1)S(1)}, bf16[80,2560]{1,0:T(8,128)(2,1)}, u32[]{:S(2)}) copy-start(bf16[80,2560]{1,0:T(8,128)(2,1)} %refs_2_.3) | copy-start | bytes 1228804
  0.0 7.0 %copy-start.1 = (bf16[80,2560]{1,0:T(8,128)(2,1)S(1)}, bf16[80,2560]{1,0:T(8,128)(2,1)}, u32[]{:S(2)}) copy-start(bf16[80,2560]{1,0:T(8,128)(2,1)} %refs_1_.3) | copy-start | bytes 1228804
  0.0 7.0 %copy-start = (bf16[80,2560]{1,0:T(8,128)(2,1)S(1)}, bf16[80,2560]{1,0:T(8,128)(2,1)}, u32[]{:S(2)}) copy-start(bf16[80,2560]{1,0:T(8,128)(2,1)} %refs_0_.3) | copy-start | bytes 1228804
  1.8 12.3 %collective-permute-start.1 = (bf16[120,256]{1,0:T(8,128)(2,1)}, bf16[120,256]{1,0:T(8,128)(2,1)S(1)}, u32[]{:S(2)}, u32[]{:S(2)}) collective-permute-start(bf16[120,256]{1,0:T(8,128)(2,1)} %get-tuple-element.30), channel_id=1, source_target_pairs={{0,32},{32,64},{64,96},{96,0},{1,33},{33,65},{65,97},{97,1},{2,34}... | collective-permute-start | bytes 184328 | tf_op jit(solution)/shard_map/ppermute | solution.py:38
  3.5 10.7 %collective-permute-start.2 = (bf16[120,256]{1,0:T(8,128)(2,1)}, bf16[120,256]{1,0:T(8,128)(2,1)S(1)}, u32[]{:S(2)}, u32[]{:S(2)}) collective-permute-start(bf16[120,256]{1,0:T(8,128)(2,1)} %get-tuple-element.31), channel_id=1, source_target_pairs={{0,96},{32,0},{64,32},{96,64},{1,97},{33,1},{65,33},{97,65},{2,98}... | collective-permute-start | bytes 184328 | tf_op jit(solution)/shard_map/ppermute | solution.py:38
  5.1 9.1 %collective-permute-start.3 = (bf16[120,256]{1,0:T(8,128)(2,1)}, bf16[120,256]{1,0:T(8,128)(2,1)S(1)}, u32[]{:S(2)}, u32[]{:S(2)}) collective-permute-start(bf16[120,256]{1,0:T(8,128)(2,1)} %get-tuple-element.32), channel_id=1, source_target_pairs={{0,64},{32,96},{64,0},{96,32},{1,65},{33,97},{65,1},{97,33},{2,66}... | collective-permute-start | bytes 184328 | tf_op jit(solution)/shard_map/ppermute | solution.py:38
  8.3 5.9 %copy-start.3 = (bf16[120,256]{1,0:T(8,128)(2,1)S(1)}, bf16[120,256]{1,0:T(8,128)(2,1)}, u32[]{:S(2)}) copy-start(bf16[120,256]{1,0:T(8,128)(2,1)} %get-tuple-element.29.refs_0_) | copy-start | bytes 184324
  8.3 21.5 %all-to-all-start = ((bf16[16,120,256]{2,1,0:T(8,128)(2,1)}), bf16[16,120,256]{2,1,0:T(8,128)(2,1)S(1)}, u32[]{:S(2)}, u32[]{:S(2)}) async-start(bf16[16,120,256]{2,1,0:T(8,128)(2,1)} %shard_map.37), calls=%async_computation | async-start | bytes 1966080 | tf_op jit(solution)/shard_map/all_to_all | solution.py:380
  14.2 7.4 %collective-permute-start.7 = (bf16[320,256]{1,0:T(8,128)(2,1)S(1)}, bf16[320,256]{1,0:T(8,128)(2,1)S(1)}, u32[]{:S(2)}, u32[]{:S(2)}) collective-permute-start(bf16[320,256]{1,0:T(8,128)(2,1)S(1)} %get-tuple-element.34.refs_1_), channel_id=1, source_target_pairs={{0,16},{2,18},{16,2},{18,0},{1,17},{3,19},{17,3},{19,1},{4,20},{6,... | collective-permute-start | bytes 491528 | tf_op jit(solution)/shard_map/ppermute | solution.py:34
  16.2 13.6 %collective-permute-start.8 = (bf16[320,256]{1,0:T(8,128)(2,1)S(1)}, bf16[320,256]{1,0:T(8,128)(2,1)S(1)}, u32[]{:S(2)}, u32[]{:S(2)}) collective-permute-start(bf16[320,256]{1,0:T(8,128)(2,1)S(1)} %get-tuple-element.34.refs_1_), channel_id=1, source_target_pairs={{0,18},{2,16},{16,0},{18,2},{1,19},{3,17},{17,1},{19,3},{4,22},{6,... | collective-permute-start | bytes 491528 | tf_op jit(solution)/shard_map/ppermute | solution.py:34
  21.7 10.2 %collective-permute-start.9 = (bf16[320,256]{1,0:T(8,128)(2,1)S(1)}, bf16[320,256]{1,0:T(8,128)(2,1)S(1)}, u32[]{:S(2)}, u32[]{:S(2)}) collective-permute-start(bf16[320,256]{1,0:T(8,128)(2,1)S(1)} %collective-permute-done.7.refs_2_), channel_id=1, source_target_pairs={{0,16},{2,18},{16,2},{18,0},{1,17},{3,19},{17,3},{19,1},{4,20},{6,... | collective-permute-start | bytes 491528 | tf_op jit(solution)/shard_map/ppermute | solution.py:34
  21.7 10.4 %collective-permute-start.6 = (bf16[160,256]{1,0:T(8,128)(2,1)S(1)}, bf16[160,256]{1,0:T(8,128)(2,1)S(1)}, u32[]{:S(2)}, u32[]{:S(2)}) collective-permute-start(bf16[160,256]{1,0:T(8,128)(2,1)S(1)} %get-tuple-element.33.refs_0_), channel_id=1, source_target_pairs={{0,8},{4,12},{8,0},{12,4},{1,9},{5,13},{9,1},{13,5},{2,10},{6,14},... | collective-permute-start | bytes 245768 | tf_op jit(solution)/shard_map/ppermute | solution.py:38
  25.1 7.0 %collective-permute-start.5 = (bf16[160,256]{1,0:T(8,128)(2,1)S(1)}, bf16[160,256]{1,0:T(8,128)(2,1)S(1)}, u32[]{:S(2)}, u32[]{:S(2)}) collective-permute-start(bf16[160,256]{1,0:T(8,128)(2,1)S(1)} %get-tuple-element.33.refs_0_), channel_id=1, source_target_pairs={{0,12},{4,0},{8,4},{12,8},{1,13},{5,1},{9,5},{13,9},{2,14},{6,2},{... | collective-permute-start | bytes 245768 | tf_op jit(solution)/shard_map/ppermute | solution.py:38
  26.2 6.1 %collective-permute-start.4 = (bf16[160,256]{1,0:T(8,128)(2,1)S(1)}, bf16[160,256]{1,0:T(8,128)(2,1)S(1)}, u32[]{:S(2)}, u32[]{:S(2)}) collective-permute-start(bf16[160,256]{1,0:T(8,128)(2,1)S(1)} %get-tuple-element.33.refs_0_), channel_id=1, source_target_pairs={{0,4},{4,8},{8,12},{12,0},{1,5},{5,9},{9,13},{13,1},{2,6},{6,10},{... | collective-permute-start | bytes 245768 | tf_op jit(solution)/shard_map/ppermute | solution.py:38
  29.8 15.1 %collective-permute-start = (bf16[1280,256]{1,0:T(8,128)(2,1)S(1)}, bf16[1280,256]{1,0:T(8,128)(2,1)S(1)}, u32[]{:S(2)}, u32[]{:S(2)}) collective-permute-start(bf16[1280,256]{1,0:T(8,128)(2,1)S(1)} %get-tuple-element.28.refs_0_.refs_1_), channel_id=1, source_target_pairs={{0,16},{16,0},{1,17},{17,1},{2,18},{18,2},{3,19},{19,3},{4,20},{20... | collective-permute-start | bytes 1966088 | tf_op jit(solution)/shard_map/ppermute | solution.py:42
  31.9 4.7 %collective-permute-start.10 = (bf16[2560,256]{1,0:T(8,128)(2,1)S(1)}, bf16[2560,256]{1,0:T(8,128)(2,1)S(1)}, u32[]{:S(2)}, u32[]{:S(2)}) collective-permute-start(bf16[2560,256]{1,0:T(8,128)(2,1)S(1)} %shard_map.42), channel_id=1, source_target_pairs={{0,1},{1,0},{2,3},{3,2},{4,5},{5,4},{6,7},{7,6},{8,9},{9,8},{10,11... | collective-permute-start | bytes 3932168 | tf_op jit(solution)/shard_map/ppermute | solution.py:50
  32.4 12.6 %collective-permute-start.11 = (bf16[640,256]{1,0:T(8,128)(2,1)S(1)}, bf16[640,256]{1,0:T(8,128)(2,1)S(1)}, u32[]{:S(2)}, u32[]{:S(2)}) collective-permute-start(bf16[640,256]{1,0:T(8,128)(2,1)S(1)} %get-tuple-element.27.refs_0_), channel_id=1, source_target_pairs={{0,18},{18,0},{2,16},{16,2},{1,19},{19,1},{3,17},{17,3},{4,22},{22... | collective-permute-start | bytes 983048 | tf_op jit(solution)/shard_map/ppermute | solution.py:46
  45.0 4.4 %collective-permute-start.12 = (bf16[1280,256]{1,0:T(8,128)(2,1)S(1)}, bf16[1280,256]{1,0:T(8,128)(2,1)S(1)}, u32[]{:S(2)}, u32[]{:S(2)}) collective-permute-start(bf16[1280,256]{1,0:T(8,128)(2,1)S(1)} %shard_map.45.refs_3_.refs_1_), channel_id=1, source_target_pairs={{0,1},{1,0},{2,3},{3,2},{4,5},{5,4},{6,7},{7,6},{8,9},{9,8},{10,11... | collective-permute-start | bytes 1966088 | tf_op jit(solution)/shard_map/ppermute | solution.py:50
  53.7 11.9 %collective-permute-start.13 = (bf16[656,256]{1,0:T(8,128)(2,1)S(1)}, bf16[656,256]{1,0:T(8,128)(2,1)S(1)}, u32[]{:S(2)}, u32[]{:S(2)}) collective-permute-start(bf16[656,256]{1,0:T(8,128)(2,1)S(1)} %shard_map.47.refs_5_), channel_id=1, source_target_pairs={{0,18},{18,0},{2,16},{16,2},{1,19},{19,1},{3,17},{17,3},{4,22},{22... | collective-permute-start | bytes 1007624 | tf_op jit(solution)/shard_map/ppermute | solution.py:46
  57.1 7.1 %collective-permute-start.14 = (bf16[176,256]{1,0:T(8,128)(2,1)S(1)}, bf16[176,256]{1,0:T(8,128)(2,1)S(1)}, u32[]{:S(2)}, u32[]{:S(2)}) collective-permute-start(bf16[176,256]{1,0:T(8,128)(2,1)S(1)} %get-tuple-element.42), channel_id=1, source_target_pairs={{0,12},{4,0},{8,4},{12,8},{1,13},{5,1},{9,5},{13,9},{2,14},{6,2},{... | collective-permute-start | bytes 270344 | tf_op jit(solution)/shard_map/ppermute | solution.py:38
  57.8 7.7 %collective-permute-start.15 = (bf16[176,256]{1,0:T(8,128)(2,1)S(1)}, bf16[176,256]{1,0:T(8,128)(2,1)S(1)}, u32[]{:S(2)}, u32[]{:S(2)}) collective-permute-start(bf16[176,256]{1,0:T(8,128)(2,1)S(1)} %get-tuple-element.43), channel_id=1, source_target_pairs={{0,4},{4,8},{8,12},{12,0},{1,5},{5,9},{9,13},{13,1},{2,6},{6,10},{... | collective-permute-start | bytes 270344 | tf_op jit(solution)/shard_map/ppermute | solution.py:38
  59.1 6.4 %collective-permute-start.16 = (bf16[176,256]{1,0:T(8,128)(2,1)S(1)}, bf16[176,256]{1,0:T(8,128)(2,1)S(1)}, u32[]{:S(2)}, u32[]{:S(2)}) collective-permute-start(bf16[176,256]{1,0:T(8,128)(2,1)S(1)} %get-tuple-element.44), channel_id=1, source_target_pairs={{0,8},{4,12},{8,0},{12,4},{1,9},{5,13},{9,1},{13,5},{2,10},{6,14},... | collective-permute-start | bytes 270344 | tf_op jit(solution)/shard_map/ppermute | solution.py:38
  66.8 13.8 %all-to-all-start.1 = ((bf16[16,40,256]{2,1,0:T(8,128)(2,1)}), bf16[16,40,256]{2,1,0:T(8,128)(2,1)S(1)}, u32[]{:S(2)}, u32[]{:S(2)}) async-start(bf16[16,40,256]{2,1,0:T(8,128)(2,1)} %bitcast), calls=%async_computation.1 | async-start | bytes 655360 | tf_op jit(solution)/shard_map/all_to_all | solution.py:400
  71.8 5.7 %collective-permute-start.17 = (bf16[40,256]{1,0:T(8,128)(2,1)S(1)}, bf16[40,256]{1,0:T(8,128)(2,1)S(1)}, u32[]{:S(2)}, u32[]{:S(2)}) collective-permute-start(bf16[40,256]{1,0:T(8,128)(2,1)S(1)} %get-tuple-element.46), channel_id=1, source_target_pairs={{0,96},{32,0},{64,32},{96,64},{1,97},{33,1},{65,33},{97,65},{2,98}... | collective-permute-start | bytes 61448 | tf_op jit(solution)/shard_map/ppermute | solution.py:38
  75.0 5.0 %collective-permute-start.18 = (bf16[40,256]{1,0:T(8,128)(2,1)S(1)}, bf16[40,256]{1,0:T(8,128)(2,1)S(1)}, u32[]{:S(2)}, u32[]{:S(2)}) collective-permute-start(bf16[40,256]{1,0:T(8,128)(2,1)S(1)} %get-tuple-element.47), channel_id=1, source_target_pairs={{0,32},{32,64},{64,96},{96,0},{1,33},{33,65},{65,97},{97,1},{2,34}... | collective-permute-start | bytes 61448 | tf_op jit(solution)/shard_map/ppermute | solution.py:38
  75.0 5.3 %collective-permute-start.19 = (bf16[40,256]{1,0:T(8,128)(2,1)S(1)}, bf16[40,256]{1,0:T(8,128)(2,1)S(1)}, u32[]{:S(2)}, u32[]{:S(2)}) collective-permute-start(bf16[40,256]{1,0:T(8,128)(2,1)S(1)} %get-tuple-element.48), channel_id=1, source_target_pairs={{0,64},{32,96},{64,0},{96,32},{1,65},{33,97},{65,1},{97,33},{2,66}... | collective-permute-start | bytes 61448 | tf_op jit(solution)/shard_map/ppermute | solution.py:38

commit v6 on v5

--- a/solution.py
+++ b/solution.py
@@ -374,8 +374,7 @@
     extra = [extra[0]] + [along("x", a, step) for a, step in zip(extra[1:], STEPS, strict=True)]
     xkv, xq = gather(extra)
     xqs = [xq] + [along("y", xq, step) for step in STEPS]
-    xkvs = [xkv, along_z(xkv, 1), along_z(xkv, 3)]
-    xkvs.append(along_z(xkvs[1], 1))
+    xkvs = [xkv] + [along_z(xkv, step) for step in STEPS]
 
     got = lax.all_to_all(sent, ("x", "y"), 0, 0, tiled=True)
     kv, q = sort(got)

time: 81.8 us -> 81.9 us (level)
  waiting for transfers between devices: 10.9 us -> 8.69 us
  starting transfers between devices: 43.6 us -> 45.7 us
    ppermute x3, waiting for transfers between devices: 3.22 us -> 0.01 us  [along_z(): return lax.ppermute(a, ('zl', 'zh'), pairs)]
    ppermute x3, starting transfers between devices: 4.19 us -> 5.98 us  [along_z(): return lax.ppermute(a, ('zl', 'zh'), pairs)]
    all_to_all x1, waiting for transfers between devices: 2.65 us -> 4.08 us  [local(): got = lax.all_to_all(sent, ('x', 'y'), 0, 0, tiled=True)]
  transfers between devices with their start and end apart: 22 -> 22, of which waited for: 9 -> 6; matrix products, arithmetic and copies ran while one was open for 0% -> 0% of each run, Pallas kernels for 23% -> 23%
where the time goes in v6:
time: 81.9 us; the launch traced here: 81.3 us
  starting transfers between devices  45.7 us (56%)
  Pallas kernels  26.6 us (32%)
  waiting for transfers between devices  8.69 us (11%)
    pallas_call x5, Pallas kernels, attend(): pl.pallas_call(functools.partial(attend_kernel, len(kvs), len(after), sta...  20.8 us
    ppermute x12, starting transfers between devices, along(): return lax.ppermute(a, axis, [(i, (i + step) % 4) for i in range(4)])  19.2 us
    ppermute x2, starting transfers between devices, query_partner(): return lax.ppermute(a, ('zl', 'zh'), [(0, 3), (3, 0), (1, 2), (2, 1)])  7.56 us
    ppermute x3, starting transfers between devices, along_z(): return lax.ppermute(a, ('zl', 'zh'), pairs)  5.98 us
    all_to_all x1, starting transfers between devices, local(): got = lax.all_to_all(sent, ('x', 'y'), 0, 0, tiled=True)  5.87 us
    all_to_all x1, starting transfers between devices, local(): lax.all_to_all(out.reshape(COLUMNS, Q_ROWS, PAIR), ('x', 'y'), 0, 0, tile...  4.68 us
    ppermute x12, waiting for transfers between devices, along(): return lax.ppermute(a, axis, [(i, (i + step) % 4) for i in range(4)])  4.46 us
    all_to_all x1, waiting for transfers between devices, local(): got = lax.all_to_all(sent, ('x', 'y'), 0, 0, tiled=True)  4.08 us
  transfers between devices with their start and end apart: 22, of which 6 were waited for; matrix products, arithmetic and copies ran while one was open for 0% of the time, Pallas kernels for 23%

profile of v6, /device:TPU:0, one launch (start us, length us, event | category | flops | bytes accessed | tf_op | source)
XLA Modules:
  0.0 81.3 jit_solution(14758064984843664305)
XLA Ops:
  0.0 1.8 %shard_map.39 = (bf16[120,256]{1,0:T(8,128)(2,1)}, bf16[120,256]{1,0:T(8,128)(2,1)}, bf16[120,256]{1,0:T(8,128)(2,1)}, bf16[120,256]{1,0:T(8,128)(2,1)}) custom-call(bf16[80,2560]{1,0:T(8,128)(2,1)} %refs_0_.3, bf16[80,2560]{1,0:T(8,128)(2,1)} %refs_1_.3, bf16[80,2560]{1,0:T(8,128)(2,1)} %refs_2_.3), custom_call_target="tpu_custom_call" | custom-call | bytes 1048576 | tf_op jit(solution)/shard_map/pallas_call | solution.py:234
  1.8 1.6 %collective-permute-start.1 = (bf16[120,256]{1,0:T(8,128)(2,1)}, bf16[120,256]{1,0:T(8,128)(2,1)S(1)}, u32[]{:S(2)}, u32[]{:S(2)}) collective-permute-start(bf16[120,256]{1,0:T(8,128)(2,1)} %get-tuple-element.30), channel_id=1, source_target_pairs={{0,32},{32,64},{64,96},{96,0},{1,33},{33,65},{65,97},{97,1},{2,34}... | collective-permute-start | bytes 184328 | tf_op jit(solution)/shard_map/ppermute | solution.py:38
  3.5 1.7 %collective-permute-start.2 = (bf16[120,256]{1,0:T(8,128)(2,1)}, bf16[120,256]{1,0:T(8,128)(2,1)S(1)}, u32[]{:S(2)}, u32[]{:S(2)}) collective-permute-start(bf16[120,256]{1,0:T(8,128)(2,1)} %get-tuple-element.31), channel_id=1, source_target_pairs={{0,96},{32,0},{64,32},{96,64},{1,97},{33,1},{65,33},{97,65},{2,98}... | collective-permute-start | bytes 184328 | tf_op jit(solution)/shard_map/ppermute | solution.py:38
  5.1 1.9 %collective-permute-start.3 = (bf16[120,256]{1,0:T(8,128)(2,1)}, bf16[120,256]{1,0:T(8,128)(2,1)S(1)}, u32[]{:S(2)}, u32[]{:S(2)}) collective-permute-start(bf16[120,256]{1,0:T(8,128)(2,1)} %get-tuple-element.32), channel_id=1, source_target_pairs={{0,64},{32,96},{64,0},{96,32},{1,65},{33,97},{65,1},{97,33},{2,66}... | collective-permute-start | bytes 184328 | tf_op jit(solution)/shard_map/ppermute | solution.py:38
  7.0 1.2 %shard_map.37 = bf16[16,120,256]{2,1,0:T(8,128)(2,1)} custom-call(bf16[80,2560]{1,0:T(8,128)(2,1)S(1)} %copy-done, bf16[80,2560]{1,0:T(8,128)(2,1)S(1)} %copy-done.1, bf16[80,2560]{1,0:T(8,128)(2,1)S(1)} %copy-done.2), custom_call_target="tpu_custom_call" | custom-call | bytes 1048576 | tf_op jit(solution)/shard_map/pallas_call | solution.py:234
  8.3 0.0 copy-start.3
  8.3 5.9 %all-to-all-start = ((bf16[16,120,256]{2,1,0:T(8,128)(2,1)}), bf16[16,120,256]{2,1,0:T(8,128)(2,1)S(1)}, u32[]{:S(2)}, u32[]{:S(2)}) async-start(bf16[16,120,256]{2,1,0:T(8,128)(2,1)} %shard_map.37), calls=%async_computation | async-start | bytes 1966080 | tf_op jit(solution)/shard_map/all_to_all | solution.py:379
  14.2 0.0 collective-permute-done.2.refs_2_
  14.2 0.0 collective-permute-done.3.refs_3_
  14.2 4.0 %collective-permute-start.9 = (bf16[320,256]{1,0:T(8,128)(2,1)S(1)}, bf16[320,256]{1,0:T(8,128)(2,1)S(1)}, u32[]{:S(2)}, u32[]{:S(2)}) collective-permute-start(bf16[320,256]{1,0:T(8,128)(2,1)S(1)} %get-tuple-element.34.refs_1_), channel_id=1, source_target_pairs={{0,2},{2,0},{16,18},{18,16},{1,3},{3,1},{17,19},{19,17},{4,6},{6,4... | collective-permute-start | bytes 491528 | tf_op jit(solution)/shard_map/ppermute | solution.py:34
  18.2 0.7 collective-permute-start.8
  18.9 1.3 %collective-permute-start.7 = (bf16[320,256]{1,0:T(8,128)(2,1)S(1)}, bf16[320,256]{1,0:T(8,128)(2,1)S(1)}, u32[]{:S(2)}, u32[]{:S(2)}) collective-permute-start(bf16[320,256]{1,0:T(8,128)(2,1)S(1)} %get-tuple-element.34.refs_1_), channel_id=1, source_target_pairs={{0,16},{2,18},{16,2},{18,0},{1,17},{3,19},{17,3},{19,1},{4,20},{6,... | collective-permute-start | bytes 491528 | tf_op jit(solution)/shard_map/ppermute | solution.py:34
  20.2 3.4 %collective-permute-start.6 = (bf16[160,256]{1,0:T(8,128)(2,1)S(1)}, bf16[160,256]{1,0:T(8,128)(2,1)S(1)}, u32[]{:S(2)}, u32[]{:S(2)}) collective-permute-start(bf16[160,256]{1,0:T(8,128)(2,1)S(1)} %get-tuple-element.33.refs_0_), channel_id=1, source_target_pairs={{0,8},{4,12},{8,0},{12,4},{1,9},{5,13},{9,1},{13,5},{2,10},{6,14},... | collective-permute-start | bytes 245768 | tf_op jit(solution)/shard_map/ppermute | solution.py:38
  23.7 1.2 %collective-permute-start.5 = (bf16[160,256]{1,0:T(8,128)(2,1)S(1)}, bf16[160,256]{1,0:T(8,128)(2,1)S(1)}, u32[]{:S(2)}, u32[]{:S(2)}) collective-permute-start(bf16[160,256]{1,0:T(8,128)(2,1)S(1)} %get-tuple-element.33.refs_0_), channel_id=1, source_target_pairs={{0,12},{4,0},{8,4},{12,8},{1,13},{5,1},{9,5},{13,9},{2,14},{6,2},{... | collective-permute-start | bytes 245768 | tf_op jit(solution)/shard_map/ppermute | solution.py:38
  24.8 0.9 %collective-permute-start.4 = (bf16[160,256]{1,0:T(8,128)(2,1)S(1)}, bf16[160,256]{1,0:T(8,128)(2,1)S(1)}, u32[]{:S(2)}, u32[]{:S(2)}) collective-permute-start(bf16[160,256]{1,0:T(8,128)(2,1)S(1)} %get-tuple-element.33.refs_0_), channel_id=1, source_target_pairs={{0,4},{4,8},{8,12},{12,0},{1,5},{5,9},{9,13},{13,1},{2,6},{6,10},{... | collective-permute-start | bytes 245768 | tf_op jit(solution)/shard_map/ppermute | solution.py:38
  25.7 4.1 %all-to-all-done.got = bf16[16,120,256]{2,1,0:T(8,128)(2,1)S(1)} async-done(((bf16[16,120,256]{2,1,0:T(8,128)(2,1)}), bf16[16,120,256]{2,1,0:T(8,128)(2,1)S(1)}, u32[]{:S(2)}, u32[]{:S(2)}) %all-to-all-start) | async-done | bytes 983072 | tf_op jit(solution)/shard_map/all_to_all | solution.py:379
  29.8 0.1 shard_map.38
  29.8 2.0 %collective-permute-start = (bf16[1280,256]{1,0:T(8,128)(2,1)S(1)}, bf16[1280,256]{1,0:T(8,128)(2,1)S(1)}, u32[]{:S(2)}, u32[]{:S(2)}) collective-permute-start(bf16[1280,256]{1,0:T(8,128)(2,1)S(1)} %get-tuple-element.28.refs_0_.refs_1_), channel_id=1, source_target_pairs={{0,16},{16,0},{1,17},{17,1},{2,18},{18,2},{3,19},{19,3},{4,20},{20... | collective-permute-start | bytes 1966088 | tf_op jit(solution)/shard_map/ppermute | solution.py:42
  31.8 0.1 shard_map.42
  31.9 0.1 collective-permute-start.10
  32.0 0.0 collective-permute-done.6.refs_3_
  32.0 0.0 collective-permute-done.5.refs_2_
  32.0 0.1 collective-permute-done.4.refs_1_
  32.3 3.9 %collective-permute-start.11 = (bf16[640,256]{1,0:T(8,128)(2,1)S(1)}, bf16[640,256]{1,0:T(8,128)(2,1)S(1)}, u32[]{:S(2)}, u32[]{:S(2)}) collective-permute-start(bf16[640,256]{1,0:T(8,128)(2,1)S(1)} %get-tuple-element.27.refs_0_), channel_id=1, source_target_pairs={{0,18},{18,0},{2,16},{16,2},{1,19},{19,1},{3,17},{17,3},{4,22},{22... | collective-permute-start | bytes 983048 | tf_op jit(solution)/shard_map/ppermute | solution.py:46
  36.2 0.0 collective-permute-done.10
  36.2 0.1 fusion
  36.3 4.1 %shard_map.43 = (f32[1280,256]{1,0:T(8,128)S(1)}, f32[1280,128]{1,0:T(8,128)S(1)}) custom-call(bf16[640,256]{1,0:T(8,128)(2,1)S(1)} %get-tuple-element.27.refs_0_, bf16[1280,256]{1,0:T(8,128)(2,1)S(1)} %get-tuple-element.28.refs_0_.refs_1_, bf16[1280,256]{1,0:T(8,128)(2,1)S(1)} %get-tuple-element.49.refs_2_), custom_call_target="tpu_custom_call" | custom-call | bytes 1310720 | tf_op jit(solution)/shard_map/pallas_call | solution.py:151
  40.4 4.2 %shard_map.44 = (bf16[176,256]{1,0:T(8,128)(2,1)S(1)}, bf16[176,256]{1,0:T(8,128)(2,1)S(1)}, bf16[176,256]{1,0:T(8,128)(2,1)S(1)}, bf16[176,256]{1,0:T(8,128)(2,1)S(1)}) custom-call(bf16[640,256]{1,0:T(8,128)(2,1)S(1)} %shard_map.41.refs_0_, bf16[1280,256]{1,0:T(8,128)(2,1)S(1)} %slice.13.refs_1_, bf16[1280,256]{1,0:T(8,128)(2,1)S(1)} %get-tuple-element.50.refs_2_, ...), custom_call_target="tpu_custom_call" | custom-call | bytes 1310720 | tf_op jit(solution)/shard_map/pallas_call | solution.py:151
  44.6 0.0 collective-permute-done.11.refs_1_.refs_0_
  44.6 0.3 collective-permute-start.12
  44.9 4.1 %shard_map.46 = (f32[1280,256]{1,0:T(8,128)S(1)}, f32[1280,128]{1,0:T(8,128)S(1)}) custom-call(bf16[640,256]{1,0:T(8,128)(2,1)S(1)} %collective-permute-done.11.refs_1_.refs_0_, bf16[1280,256]{1,0:T(8,128)(2,1)S(1)} %get-tuple-element.28.refs_0_.refs_1_, bf16[1280,256]{1,0:T(8,128)(2,1)S(1)} %get-tuple-element.49.refs_2_, ...), custom_call_target="tpu_custom_call" | custom-call | bytes 1310720 | tf_op jit(solution)/shard_map/pallas_call | solution.py:151
  49.1 4.3 %shard_map.47.refs_5_ = bf16[656,256]{1,0:T(8,128)(2,1)S(1)} custom-call(bf16[640,256]{1,0:T(8,128)(2,1)S(1)} %collective-permute-done.11.refs_1_.refs_0_, bf16[1280,256]{1,0:T(8,128)(2,1)S(1)} %shard_map.45.refs_3_.refs_1_, bf16[1280,256]{1,0:T(8,128)(2,1)S(1)} %collective-permute-done.12.refs_2_, f32[1280,256]{1,0:T(8,128)S(1)} %get-tuple-element.38.refs_3_, ...), custom_call_target="tpu_custom_call" | custom-call | bytes 1310720 | tf_op jit(solution)/shard_map/pallas_call | solution.py:151
  53.3 3.7 %collective-permute-start.13 = (bf16[656,256]{1,0:T(8,128)(2,1)S(1)}, bf16[656,256]{1,0:T(8,128)(2,1)S(1)}, u32[]{:S(2)}, u32[]{:S(2)}) collective-permute-start(bf16[656,256]{1,0:T(8,128)(2,1)S(1)} %shard_map.47.refs_5_), channel_id=1, source_target_pairs={{0,18},{18,0},{2,16},{16,2},{1,19},{19,1},{3,17},{17,3},{4,22},{22... | collective-permute-start | bytes 1007624 | tf_op jit(solution)/shard_map/ppermute | solution.py:46
  57.0 0.9 %collective-permute-start.14 = (bf16[176,256]{1,0:T(8,128)(2,1)S(1)}, bf16[176,256]{1,0:T(8,128)(2,1)S(1)}, u32[]{:S(2)}, u32[]{:S(2)}) collective-permute-start(bf16[176,256]{1,0:T(8,128)(2,1)S(1)} %get-tuple-element.42), channel_id=1, source_target_pairs={{0,12},{4,0},{8,4},{12,8},{1,13},{5,1},{9,5},{13,9},{2,14},{6,2},{... | collective-permute-start | bytes 270344 | tf_op jit(solution)/shard_map/ppermute | solution.py:38
  57.8 1.2 %collective-permute-start.15 = (bf16[176,256]{1,0:T(8,128)(2,1)S(1)}, bf16[176,256]{1,0:T(8,128)(2,1)S(1)}, u32[]{:S(2)}, u32[]{:S(2)}) collective-permute-start(bf16[176,256]{1,0:T(8,128)(2,1)S(1)} %get-tuple-element.43), channel_id=1, source_target_pairs={{0,4},{4,8},{8,12},{12,0},{1,5},{5,9},{9,13},{13,1},{2,6},{6,10},{... | collective-permute-start | bytes 270344 | tf_op jit(solution)/shard_map/ppermute | solution.py:38
  59.0 1.0 %collective-permute-start.16 = (bf16[176,256]{1,0:T(8,128)(2,1)S(1)}, bf16[176,256]{1,0:T(8,128)(2,1)S(1)}, u32[]{:S(2)}, u32[]{:S(2)}) collective-permute-start(bf16[176,256]{1,0:T(8,128)(2,1)S(1)} %get-tuple-element.44), channel_id=1, source_target_pairs={{0,8},{4,12},{8,0},{12,4},{1,9},{5,13},{9,1},{13,5},{2,10},{6,14},... | collective-permute-start | bytes 270344 | tf_op jit(solution)/shard_map/ppermute | solution.py:38
  60.0 4.2 %shard_map.48 = (f32[1280,256]{1,0:T(8,128)S(1)}, f32[1280,128]{1,0:T(8,128)S(1)}) custom-call(bf16[640,256]{1,0:T(8,128)(2,1)S(1)} %get-tuple-element.27.refs_0_, bf16[1280,256]{1,0:T(8,128)(2,1)S(1)} %shard_map.45.refs_3_.refs_1_, bf16[1280,256]{1,0:T(8,128)(2,1)S(1)} %collective-permute-done.12.refs_2_, f32[1280,256]{1,0:T(8,128)S(1)} %get-tuple-element.35.refs_3_, ...), custom_call_target="tpu_custom_call" | custom-call | bytes 1310720 | tf_op jit(solution)/shard_map/pallas_call | solution.py:151
  64.2 1.3 %collective-permute-done.15.refs_1_.refs_2_ = bf16[176,256]{1,0:T(8,128)(2,1)S(1)} collective-permute-done((bf16[176,256]{1,0:T(8,128)(2,1)S(1)}, bf16[176,256]{1,0:T(8,128)(2,1)S(1)}, u32[]{:S(2)}, u32[]{:S(2)}) %collective-permute-start.15) | collective-permute-done | bytes 90144 | tf_op jit(solution)/shard_map/ppermute | solution.py:38
  65.5 0.0 collective-permute-done.13.sent
  65.5 1.1 %shard_map.49 = bf16[640,256]{1,0:T(8,128)(2,1)} custom-call(f32[1280,256]{1,0:T(8,128)S(1)} %get-tuple-element.40.acc, f32[1280,128]{1,0:T(8,128)S(1)} %get-tuple-element.41.top, bf16[656,256]{1,0:T(8,128)(2,1)S(1)} %collective-permute-done.13.sent, bf16[176,256]{1,0:T(8,128)(2,1)S(1)} %collective-permute-done.14.refs_0_.refs_1_, ...), custom_call_target="tpu_custom_call" | custom-call | bytes 1048576 | tf_op jit(solution)/shard_map/pallas_call | solution.py:332
  66.7 4.7 %all-to-all-start.1 = ((bf16[16,40,256]{2,1,0:T(8,128)(2,1)}), bf16[16,40,256]{2,1,0:T(8,128)(2,1)S(1)}, u32[]{:S(2)}, u32[]{:S(2)}) async-start(bf16[16,40,256]{2,1,0:T(8,128)(2,1)} %bitcast), calls=%async_computation.1 | async-start | bytes 655360 | tf_op jit(solution)/shard_map/all_to_all | solution.py:399
  71.3 0.5 shard_map.50
  71.9 3.2 %collective-permute-start.17 = (bf16[40,256]{1,0:T(8,128)(2,1)S(1)}, bf16[40,256]{1,0:T(8,128)(2,1)S(1)}, u32[]{:S(2)}, u32[]{:S(2)}) collective-permute-start(bf16[40,256]{1,0:T(8,128)(2,1)S(1)} %get-tuple-element.46), channel_id=1, source_target_pairs={{0,96},{32,0},{64,32},{96,64},{1,97},{33,1},{65,33},{97,65},{2,98}... | collective-permute-start | bytes 61448 | tf_op jit(solution)/shard_map/ppermute | solution.py:38
  75.1 2.3 %collective-permute-start.19 = (bf16[40,256]{1,0:T(8,128)(2,1)S(1)}, bf16[40,256]{1,0:T(8,128)(2,1)S(1)}, u32[]{:S(2)}, u32[]{:S(2)}) collective-permute-start(bf16[40,256]{1,0:T(8,128)(2,1)S(1)} %get-tuple-element.48), channel_id=1, source_target_pairs={{0,64},{32,96},{64,0},{96,32},{1,65},{33,97},{65,1},{97,33},{2,66}... | collective-permute-start | bytes 61448 | tf_op jit(solution)/shard_map/ppermute | solution.py:38
  77.4 2.7 %collective-permute-done.18.refs_2_ = bf16[40,256]{1,0:T(8,128)(2,1)S(1)} collective-permute-done((bf16[40,256]{1,0:T(8,128)(2,1)S(1)}, bf16[40,256]{1,0:T(8,128)(2,1)S(1)}, u32[]{:S(2)}, u32[]{:S(2)}) %collective-permute-start.18) | collective-permute-done | bytes 20512 | tf_op jit(solution)/shard_map/ppermute | solution.py:38
  80.1 0.3 collective-permute-done.19.refs_3_
  80.4 0.1 all-to-all-done.1.main
  80.5 0.8 %shard_map.51 = bf16[80,2560]{1,0:T(8,128)(2,1)} custom-call(bf16[16,40,256]{2,1,0:T(8,128)(2,1)S(1)} %all-to-all-done.1.main, bf16[40,256]{1,0:T(8,128)(2,1)S(1)} %get-tuple-element.45.refs_0_, bf16[40,256]{1,0:T(8,128)(2,1)S(1)} %collective-permute-done.17.refs_1_, bf16[40,256]{1,0:T(8,128)(2,1)S(1)} %collective-permute-done.18.refs_2_, ...), custom_call_target="tpu_custom_call" | custom-call | bytes 1048576 | tf_op jit(solution)/shard_map/pallas_call | solution.py:358
  (21 shorter events, 0.2 us)
Async XLA Ops:
  0.0 7.0 %copy-start.2 = (bf16[80,2560]{1,0:T(8,128)(2,1)S(1)}, bf16[80,2560]{1,0:T(8,128)(2,1)}, u32[]{:S(2)}) copy-start(bf16[80,2560]{1,0:T(8,128)(2,1)} %refs_2_.3) | copy-start | bytes 1228804
  0.0 7.0 %copy-start.1 = (bf16[80,2560]{1,0:T(8,128)(2,1)S(1)}, bf16[80,2560]{1,0:T(8,128)(2,1)}, u32[]{:S(2)}) copy-start(bf16[80,2560]{1,0:T(8,128)(2,1)} %refs_1_.3) | copy-start | bytes 1228804
  0.0 7.0 %copy-start = (bf16[80,2560]{1,0:T(8,128)(2,1)S(1)}, bf16[80,2560]{1,0:T(8,128)(2,1)}, u32[]{:S(2)}) copy-start(bf16[80,2560]{1,0:T(8,128)(2,1)} %refs_0_.3) | copy-start | bytes 1228804
  1.8 12.3 %collective-permute-start.1 = (bf16[120,256]{1,0:T(8,128)(2,1)}, bf16[120,256]{1,0:T(8,128)(2,1)S(1)}, u32[]{:S(2)}, u32[]{:S(2)}) collective-permute-start(bf16[120,256]{1,0:T(8,128)(2,1)} %get-tuple-element.30), channel_id=1, source_target_pairs={{0,32},{32,64},{64,96},{96,0},{1,33},{33,65},{65,97},{97,1},{2,34}... | collective-permute-start | bytes 184328 | tf_op jit(solution)/shard_map/ppermute | solution.py:38
  3.5 10.7 %collective-permute-start.2 = (bf16[120,256]{1,0:T(8,128)(2,1)}, bf16[120,256]{1,0:T(8,128)(2,1)S(1)}, u32[]{:S(2)}, u32[]{:S(2)}) collective-permute-start(bf16[120,256]{1,0:T(8,128)(2,1)} %get-tuple-element.31), channel_id=1, source_target_pairs={{0,96},{32,0},{64,32},{96,64},{1,97},{33,1},{65,33},{97,65},{2,98}... | collective-permute-start | bytes 184328 | tf_op jit(solution)/shard_map/ppermute | solution.py:38
  5.1 9.1 %collective-permute-start.3 = (bf16[120,256]{1,0:T(8,128)(2,1)}, bf16[120,256]{1,0:T(8,128)(2,1)S(1)}, u32[]{:S(2)}, u32[]{:S(2)}) collective-permute-start(bf16[120,256]{1,0:T(8,128)(2,1)} %get-tuple-element.32), channel_id=1, source_target_pairs={{0,64},{32,96},{64,0},{96,32},{1,65},{33,97},{65,1},{97,33},{2,66}... | collective-permute-start | bytes 184328 | tf_op jit(solution)/shard_map/ppermute | solution.py:38
  8.3 5.9 %copy-start.3 = (bf16[120,256]{1,0:T(8,128)(2,1)S(1)}, bf16[120,256]{1,0:T(8,128)(2,1)}, u32[]{:S(2)}) copy-start(bf16[120,256]{1,0:T(8,128)(2,1)} %get-tuple-element.29.refs_0_) | copy-start | bytes 184324
  8.3 21.5 %all-to-all-start = ((bf16[16,120,256]{2,1,0:T(8,128)(2,1)}), bf16[16,120,256]{2,1,0:T(8,128)(2,1)S(1)}, u32[]{:S(2)}, u32[]{:S(2)}) async-start(bf16[16,120,256]{2,1,0:T(8,128)(2,1)} %shard_map.37), calls=%async_computation | async-start | bytes 1966080 | tf_op jit(solution)/shard_map/all_to_all | solution.py:379
  14.2 10.6 %collective-permute-start.9 = (bf16[320,256]{1,0:T(8,128)(2,1)S(1)}, bf16[320,256]{1,0:T(8,128)(2,1)S(1)}, u32[]{:S(2)}, u32[]{:S(2)}) collective-permute-start(bf16[320,256]{1,0:T(8,128)(2,1)S(1)} %get-tuple-element.34.refs_1_), channel_id=1, source_target_pairs={{0,2},{2,0},{16,18},{18,16},{1,3},{3,1},{17,19},{19,17},{4,6},{6,4... | collective-permute-start | bytes 491528 | tf_op jit(solution)/shard_map/ppermute | solution.py:34
  18.2 11.6 %collective-permute-start.8 = (bf16[320,256]{1,0:T(8,128)(2,1)S(1)}, bf16[320,256]{1,0:T(8,128)(2,1)S(1)}, u32[]{:S(2)}, u32[]{:S(2)}) collective-permute-start(bf16[320,256]{1,0:T(8,128)(2,1)S(1)} %get-tuple-element.34.refs_1_), channel_id=1, source_target_pairs={{0,18},{2,16},{16,0},{18,2},{1,19},{3,17},{17,1},{19,3},{4,22},{6,... | collective-permute-start | bytes 491528 | tf_op jit(solution)/shard_map/ppermute | solution.py:34
  18.9 12.9 %collective-permute-start.7 = (bf16[320,256]{1,0:T(8,128)(2,1)S(1)}, bf16[320,256]{1,0:T(8,128)(2,1)S(1)}, u32[]{:S(2)}, u32[]{:S(2)}) collective-permute-start(bf16[320,256]{1,0:T(8,128)(2,1)S(1)} %get-tuple-element.34.refs_1_), channel_id=1, source_target_pairs={{0,16},{2,18},{16,2},{18,0},{1,17},{3,19},{17,3},{19,1},{4,20},{6,... | collective-permute-start | bytes 491528 | tf_op jit(solution)/shard_map/ppermute | solution.py:34
  20.2 11.8 %collective-permute-start.6 = (bf16[160,256]{1,0:T(8,128)(2,1)S(1)}, bf16[160,256]{1,0:T(8,128)(2,1)S(1)}, u32[]{:S(2)}, u32[]{:S(2)}) collective-permute-start(bf16[160,256]{1,0:T(8,128)(2,1)S(1)} %get-tuple-element.33.refs_0_), channel_id=1, source_target_pairs={{0,8},{4,12},{8,0},{12,4},{1,9},{5,13},{9,1},{13,5},{2,10},{6,14},... | collective-permute-start | bytes 245768 | tf_op jit(solution)/shard_map/ppermute | solution.py:38
  23.7 8.4 %collective-permute-start.5 = (bf16[160,256]{1,0:T(8,128)(2,1)S(1)}, bf16[160,256]{1,0:T(8,128)(2,1)S(1)}, u32[]{:S(2)}, u32[]{:S(2)}) collective-permute-start(bf16[160,256]{1,0:T(8,128)(2,1)S(1)} %get-tuple-element.33.refs_0_), channel_id=1, source_target_pairs={{0,12},{4,0},{8,4},{12,8},{1,13},{5,1},{9,5},{13,9},{2,14},{6,2},{... | collective-permute-start | bytes 245768 | tf_op jit(solution)/shard_map/ppermute | solution.py:38
  24.8 7.4 %collective-permute-start.4 = (bf16[160,256]{1,0:T(8,128)(2,1)S(1)}, bf16[160,256]{1,0:T(8,128)(2,1)S(1)}, u32[]{:S(2)}, u32[]{:S(2)}) collective-permute-start(bf16[160,256]{1,0:T(8,128)(2,1)S(1)} %get-tuple-element.33.refs_0_), channel_id=1, source_target_pairs={{0,4},{4,8},{8,12},{12,0},{1,5},{5,9},{9,13},{13,1},{2,6},{6,10},{... | collective-permute-start | bytes 245768 | tf_op jit(solution)/shard_map/ppermute | solution.py:38
  29.8 14.7 %collective-permute-start = (bf16[1280,256]{1,0:T(8,128)(2,1)S(1)}, bf16[1280,256]{1,0:T(8,128)(2,1)S(1)}, u32[]{:S(2)}, u32[]{:S(2)}) collective-permute-start(bf16[1280,256]{1,0:T(8,128)(2,1)S(1)} %get-tuple-element.28.refs_0_.refs_1_), channel_id=1, source_target_pairs={{0,16},{16,0},{1,17},{17,1},{2,18},{18,2},{3,19},{19,3},{4,20},{20... | collective-permute-start | bytes 1966088 | tf_op jit(solution)/shard_map/ppermute | solution.py:42
  31.9 4.2 %collective-permute-start.10 = (bf16[2560,256]{1,0:T(8,128)(2,1)S(1)}, bf16[2560,256]{1,0:T(8,128)(2,1)S(1)}, u32[]{:S(2)}, u32[]{:S(2)}) collective-permute-start(bf16[2560,256]{1,0:T(8,128)(2,1)S(1)} %shard_map.42), channel_id=1, source_target_pairs={{0,1},{1,0},{2,3},{3,2},{4,5},{5,4},{6,7},{7,6},{8,9},{9,8},{10,11... | collective-permute-start | bytes 3932168 | tf_op jit(solution)/shard_map/ppermute | solution.py:50
  32.3 12.3 %collective-permute-start.11 = (bf16[640,256]{1,0:T(8,128)(2,1)S(1)}, bf16[640,256]{1,0:T(8,128)(2,1)S(1)}, u32[]{:S(2)}, u32[]{:S(2)}) collective-permute-start(bf16[640,256]{1,0:T(8,128)(2,1)S(1)} %get-tuple-element.27.refs_0_), channel_id=1, source_target_pairs={{0,18},{18,0},{2,16},{16,2},{1,19},{19,1},{3,17},{17,3},{4,22},{22... | collective-permute-start | bytes 983048 | tf_op jit(solution)/shard_map/ppermute | solution.py:46
  44.6 4.4 %collective-permute-start.12 = (bf16[1280,256]{1,0:T(8,128)(2,1)S(1)}, bf16[1280,256]{1,0:T(8,128)(2,1)S(1)}, u32[]{:S(2)}, u32[]{:S(2)}) collective-permute-start(bf16[1280,256]{1,0:T(8,128)(2,1)S(1)} %shard_map.45.refs_3_.refs_1_), channel_id=1, source_target_pairs={{0,1},{1,0},{2,3},{3,2},{4,5},{5,4},{6,7},{7,6},{8,9},{9,8},{10,11... | collective-permute-start | bytes 1966088 | tf_op jit(solution)/shard_map/ppermute | solution.py:50
  53.3 12.2 %collective-permute-start.13 = (bf16[656,256]{1,0:T(8,128)(2,1)S(1)}, bf16[656,256]{1,0:T(8,128)(2,1)S(1)}, u32[]{:S(2)}, u32[]{:S(2)}) collective-permute-start(bf16[656,256]{1,0:T(8,128)(2,1)S(1)} %shard_map.47.refs_5_), channel_id=1, source_target_pairs={{0,18},{18,0},{2,16},{16,2},{1,19},{19,1},{3,17},{17,3},{4,22},{22... | collective-permute-start | bytes 1007624 | tf_op jit(solution)/shard_map/ppermute | solution.py:46
  57.0 7.2 %collective-permute-start.14 = (bf16[176,256]{1,0:T(8,128)(2,1)S(1)}, bf16[176,256]{1,0:T(8,128)(2,1)S(1)}, u32[]{:S(2)}, u32[]{:S(2)}) collective-permute-start(bf16[176,256]{1,0:T(8,128)(2,1)S(1)} %get-tuple-element.42), channel_id=1, source_target_pairs={{0,12},{4,0},{8,4},{12,8},{1,13},{5,1},{9,5},{13,9},{2,14},{6,2},{... | collective-permute-start | bytes 270344 | tf_op jit(solution)/shard_map/ppermute | solution.py:38
  57.8 7.7 %collective-permute-start.15 = (bf16[176,256]{1,0:T(8,128)(2,1)S(1)}, bf16[176,256]{1,0:T(8,128)(2,1)S(1)}, u32[]{:S(2)}, u32[]{:S(2)}) collective-permute-start(bf16[176,256]{1,0:T(8,128)(2,1)S(1)} %get-tuple-element.43), channel_id=1, source_target_pairs={{0,4},{4,8},{8,12},{12,0},{1,5},{5,9},{9,13},{13,1},{2,6},{6,10},{... | collective-permute-start | bytes 270344 | tf_op jit(solution)/shard_map/ppermute | solution.py:38
  59.0 6.5 %collective-permute-start.16 = (bf16[176,256]{1,0:T(8,128)(2,1)S(1)}, bf16[176,256]{1,0:T(8,128)(2,1)S(1)}, u32[]{:S(2)}, u32[]{:S(2)}) collective-permute-start(bf16[176,256]{1,0:T(8,128)(2,1)S(1)} %get-tuple-element.44), channel_id=1, source_target_pairs={{0,8},{4,12},{8,0},{12,4},{1,9},{5,13},{9,1},{13,5},{2,10},{6,14},... | collective-permute-start | bytes 270344 | tf_op jit(solution)/shard_map/ppermute | solution.py:38
  66.7 13.8 %all-to-all-start.1 = ((bf16[16,40,256]{2,1,0:T(8,128)(2,1)}), bf16[16,40,256]{2,1,0:T(8,128)(2,1)S(1)}, u32[]{:S(2)}, u32[]{:S(2)}) async-start(bf16[16,40,256]{2,1,0:T(8,128)(2,1)} %bitcast), calls=%async_computation.1 | async-start | bytes 655360 | tf_op jit(solution)/shard_map/all_to_all | solution.py:399
  71.9 5.5 %collective-permute-start.17 = (bf16[40,256]{1,0:T(8,128)(2,1)S(1)}, bf16[40,256]{1,0:T(8,128)(2,1)S(1)}, u32[]{:S(2)}, u32[]{:S(2)}) collective-permute-start(bf16[40,256]{1,0:T(8,128)(2,1)S(1)} %get-tuple-element.46), channel_id=1, source_target_pairs={{0,96},{32,0},{64,32},{96,64},{1,97},{33,1},{65,33},{97,65},{2,98}... | collective-permute-start | bytes 61448 | tf_op jit(solution)/shard_map/ppermute | solution.py:38
  75.1 5.0 %collective-permute-start.18 = (bf16[40,256]{1,0:T(8,128)(2,1)S(1)}, bf16[40,256]{1,0:T(8,128)(2,1)S(1)}, u32[]{:S(2)}, u32[]{:S(2)}) collective-permute-start(bf16[40,256]{1,0:T(8,128)(2,1)S(1)} %get-tuple-element.47), channel_id=1, source_target_pairs={{0,32},{32,64},{64,96},{96,0},{1,33},{33,65},{65,97},{97,1},{2,34}... | collective-permute-start | bytes 61448 | tf_op jit(solution)/shard_map/ppermute | solution.py:38
  75.1 5.3 %collective-permute-start.19 = (bf16[40,256]{1,0:T(8,128)(2,1)S(1)}, bf16[40,256]{1,0:T(8,128)(2,1)S(1)}, u32[]{:S(2)}, u32[]{:S(2)}) collective-permute-start(bf16[40,256]{1,0:T(8,128)(2,1)S(1)} %get-tuple-element.48), channel_id=1, source_target_pairs={{0,64},{32,96},{64,0},{96,32},{1,65},{33,97},{65,1},{97,33},{2,66}... | collective-permute-start | bytes 61448 | tf_op jit(solution)/shard_map/ppermute | solution.py:38
